TPU v7x, 128 devices: a whole 4x4x4 slice. The times are simulated.
128 devices in a mesh: row: 8 (over x, z_hi), col: 8 (over y, z_lo), dp: 2 (over core).
Axes of the slice: x: 4, y: 4, z: 4 (z_hi: 2, z_lo: 2; z = z_hi * 2 + z_lo), core: 2. Of those that a mesh axis runs over, the one named last changes fastest.
Arguments:
- hid_query: bfloat16 [16384, 4096], P(('row', 'col', 'dp')), may hold values from -6 to 6
- hid_key: bfloat16 [16384, 4096], P(('row', 'col', 'dp')), may hold values from -6 to 6
- projection: bfloat16 [4096, 1024], replicated, may hold values from -0.09375 to 0.09375
- tile_rows: int32 [8, 8, 48], P('row', 'col'), may hold values from 0 to 7, as said below
- tile_cols: int32 [8, 8, 48], P('row', 'col'), may hold values from 0 to 7, as said below
- tile_count: int32 [8, 8], P('row', 'col'), may hold values from 1 to 48, as said below
- positive: int32 [16384], P(('row', 'col', 'dp')), may hold values from 0 to 16383, as said below
Outputs:
- grad_projection: float32 [4096, 1024], P(('row', 'col', 'dp'))
Inputs may be any that keep to these rules, and one draw needn't show every extreme that they name: Entry s of cell (r, c) names tile (tile_rows, tile_cols); the 48 entries of one cell name distinct tiles. `tile_cols`: see tile_rows. `tile_count`: some cell of every draw uses all 48 entries. `positive`: maps each device's 128 documents one to one onto the same device's documents.
All inputs are finite; a program needn't handle non-finite values.
Results may differ from a plain program's by a relative error of at most 0.0095.
Values may be sent and summed in bfloat16 or wider, within the bound.
No kernel may reach another device: no remote copies, remote signals or barrier semaphores. Data moves between devices by JAX's collectives and lax.ppermute only.
A program may use at most 128 MiB of HBM per device.

v0:
```python
import jax
import jax.numpy as jnp
from jax import lax
from jax.experimental import pallas as pl
from jax.experimental.pallas import tpu as pltpu
from jax.sharding import PartitionSpec as P

TAU_INV = 20.0
EPS = 1e-06
LOG2E = 1.4426950408889634
DOCS = 128
EMB = 1024
HID = 4096
BF = jnp.bfloat16
F32 = jnp.float32
VM = 56 * 1024 * 1024


def ring_pair(step, flip):
    return [(i, ((i // 2 + step) % 4) * 2 + ((i % 2) ^ flip)) for i in range(8)]


def move_query(value, step, flip):
    return lax.ppermute(value, "col", ring_pair(step, flip))


def move_key(value, step, flip):
    return lax.ppermute(value, "row", ring_pair(step, flip))


def chip(x, y, z):
    return (x * 2 + z // 2) * 8 + y * 2 + z % 2


PLANES = [
    [chip(x, y, z_hi * 2 + z_lo) for x in range(4) for z_hi in range(2) for y in range(4)]
    for z_lo in range(2)
]


def swap(value):
    return lax.ppermute(value, "dp", [(0, 1), (1, 0)])


def params():
    return pltpu.CompilerParams(vmem_limit_bytes=VM)


def sds(shape, dtype):
    return jax.ShapeDtypeStruct(shape, dtype)


ANY = pl.BlockSpec(memory_space=pl.ANY)
SMEM = pl.BlockSpec(memory_space=pltpu.SMEM)
VMEM = pl.BlockSpec(memory_space=pltpu.VMEM)


def dot(a, b):
    return lax.dot_general(a, b, (((1,), (0,)), ((), ())), preferred_element_type=F32)


def dot_t(a, b):
    return lax.dot_general(a, b, (((1,), (1,)), ((), ())), preferred_element_type=F32)


def t_dot(a, b):
    return lax.dot_general(a, b, (((0,), (0,)), ((), ())), preferred_element_type=F32)


def unit_of(raw):
    values = raw.astype(F32)
    scale = lax.rsqrt(jnp.sum(values * values, axis=1, keepdims=True) + EPS)
    return values * scale, scale


def project_body(hq, hk, proj, q_unit, k_unit, q_raw, k_raw, hid, acc):
    step = pl.program_id(0)
    hid[:DOCS, :] = hq[...]
    hid[DOCS:, :] = hk[...]
    part = dot(hid[...], proj[...])

    @pl.when(step == 0)
    def _():
        acc[...] = part

    @pl.when(step > 0)
    def _():
        acc[...] += part

    @pl.when(step == pl.num_programs(0) - 1)
    def _():
        for raw_ref, unit_ref, start in ((q_raw, q_unit, 0), (k_raw, k_unit, DOCS)):
            raw = acc[start : start + DOCS, :].astype(BF)
            raw_ref[...] = raw
            unit_ref[...] = unit_of(raw)[0].astype(BF)


def project(hid_query, hid_key, projection):
    depth = 1024
    whole = pl.BlockSpec((DOCS, EMB), lambda i: (0, 0))
    return pl.pallas_call(
        project_body,
        grid=(HID // depth,),
        in_specs=[
            pl.BlockSpec((DOCS, depth), lambda i: (0, i)),
            pl.BlockSpec((DOCS, depth), lambda i: (0, i)),
            pl.BlockSpec((depth, EMB), lambda i: (i, 0)),
        ],
        out_specs=[whole] * 4,
        out_shape=[sds((DOCS, EMB), BF)] * 4,
        scratch_shapes=[pltpu.VMEM((2 * DOCS, depth), BF), pltpu.VMEM((2 * DOCS, EMB), F32)],
        compiler_params=params(),
    )(hid_query, hid_key, projection)


def one_hot(pos):
    lane = lax.broadcasted_iota(jnp.int32, (DOCS, DOCS), 1)
    return (lane == pos).astype(F32)


def eye():
    lane = lax.broadcasted_iota(jnp.int32, (DOCS, DOCS), 1)
    row = lax.broadcasted_iota(jnp.int32, (DOCS, DOCS), 0)
    return (lane == row).astype(F32)


def pairs_body(q_unit, k_unit, pos, paired, q_perm, pos_rows):
    hot = one_hot(pos[...])
    hot_bf = hot.astype(BF)
    pair = dot(hot_bf, k_unit[...])
    paired[...] = pair.astype(BF)
    q_perm[...] = t_dot(hot_bf, q_unit[...]).astype(BF)
    score = jnp.sum(q_unit[...].astype(F32) * pair, axis=1, keepdims=True) * TAU_INV
    expo = jnp.exp(score)
    pos_rows[0:1, :] = jnp.sum(eye() * expo, axis=0, keepdims=True)
    pos_rows[1:2, :] = jnp.sum(hot * expo, axis=0, keepdims=True)
    pos_rows[2:8, :] = jnp.zeros((6, DOCS), F32)


def pair_up(q_unit, k_unit, pos):
    return pl.pallas_call(
        pairs_body,
        in_specs=[VMEM] * 3,
        out_specs=[VMEM] * 3,
        out_shape=[sds((DOCS, EMB), BF), sds((DOCS, EMB), BF), sds((8, DOCS), F32)],
        compiler_params=params(),
    )(q_unit, k_unit, pos)


PARTS = ((0, 256), (256, 256), (512, 128), (640, 128), (768, 256))


def block_copies(ins, scratch, sems, first, row):
    copies = []
    for i, (start, rows) in enumerate(PARTS):
        target = scratch.at[pl.ds(row + start, rows)]
        copies.append(pltpu.make_async_copy(ins[i], target, sems.at[first + i]))
    return copies


def scores_body(*refs):
    q_in, k_near, k_far = refs[0:5], refs[5:10], refs[10:15]
    mask, pos_rows = refs[15:17]
    e_own, mix, sums = refs[17:20]
    q_s, k_s, e_s, acc, in_sems, out_sems = refs[20:26]
    q_loads = block_copies(q_in, q_s, in_sems, 0, 0)
    k_loads = block_copies(k_near, k_s, in_sems, 5, 0) + block_copies(k_far, k_s, in_sems, 10, 1024)
    for load in k_loads[:1] + q_loads:
        load.start()
    waits = ((0,), (1,), (2, 3), (4,), (5,), (6,), (7, 8), (9,))
    stores = []
    for b in range(8):
        for i in waits[b]:
            k_loads[i].wait()
        total = [None, None]
        for m in range(4):
            if b == 0:
                for i in waits[m]:
                    q_loads[i].wait()
                if m == 3:
                    for load in k_loads[1:]:
                        load.start()
            chunk = slice(m * 256, (m + 1) * 256)
            score = dot_t(q_s[chunk, :], k_s[b * 256 : (b + 1) * 256, :])
            for n in range(2):
                a = m * 2 + n
                rows = slice(a * DOCS, (a + 1) * DOCS)
                expo = jnp.exp2(score[n * DOCS : (n + 1) * DOCS, :] * (TAU_INV * LOG2E))
                both = None
                for half in range(2):
                    slot = (b % 4) * 2 + half
                    one = expo[:, half * DOCS : (half + 1) * DOCS] * mask[a, slot]
                    e_s[b, rows, half * DOCS : (half + 1) * DOCS] = one.astype(BF)
                    both = one if half == 0 else both + one
                    part = one.reshape(16, 8, DOCS).sum(axis=0)
                    total[half] = part if a == 0 else total[half] + part
                if b == 0:
                    acc[rows, :] = both
                else:
                    acc[rows, :] += both
        out = (e_own if b < 4 else mix).at[pl.ds(0, 1024), pl.ds((b % 4) * 256, 256)]
        stores.append(pltpu.make_async_copy(e_s.at[b], out, out_sems.at[b]))
        stores[-1].start()
        if b == 0:
            stores.append(pltpu.make_async_copy(q_s, mix.at[pl.ds(1024, 1024)], out_sems.at[8]))
            stores[-1].start()
        for half in range(2):
            col = jnp.sum(total[half], axis=0, keepdims=True)
            if b == 0 and half == 0:
                col = col + pos_rows[1:2, :]
            sums[8 + 2 * b + half : 9 + 2 * b + half, :] = col
    for a in range(8):
        part = jnp.sum(acc[a * DOCS : (a + 1) * DOCS, :].T, axis=0, keepdims=True)
        if a == 0:
            part = part + pos_rows[0:1, :]
        sums[a : a + 1, :] = part
    for store in stores:
        store.wait()


def scores(q_in, k_near, k_far, mask, pos_rows):
    return pl.pallas_call(
        scores_body,
        in_specs=[ANY] * 15 + [SMEM, VMEM],
        out_specs=[ANY, ANY, VMEM],
        out_shape=[
            sds((8 * DOCS, 8 * DOCS), BF),
            sds((16 * DOCS, 8 * DOCS), BF),
            sds((24, DOCS), F32),
        ],
        scratch_shapes=[
            pltpu.VMEM((8 * DOCS, EMB), BF),
            pltpu.VMEM((16 * DOCS, EMB), BF),
            pltpu.VMEM((8, 8 * DOCS, 256), BF),
            pltpu.VMEM((8 * DOCS, DOCS), F32),
            pltpu.SemaphoreType.DMA((15,)),
            pltpu.SemaphoreType.DMA((9,)),
        ],
        compiler_params=params(),
    )(*q_in, *k_near, *k_far, mask, pos_rows)


def grads_body(*refs):
    k_near, k_far = refs[0:5], refs[5:10]
    e_own, mix, mix_far, row_in, col_in = refs[10], refs[11], refs[12], refs[13:17], refs[17:21]
    q_out, k_out, inv_out = refs[21:25], refs[25:29], refs[29]
    q_s, k_s, e_s, wq, wk, out_s, inv, sems, out_sems = refs[30:39]
    e_loads = []
    for m in range(4):
        rows = pl.ds(m * 256, 256)
        for i, ref in enumerate((e_own, mix, mix_far)):
            one = (ref.at[rows], e_s.at[i, rows], sems.at[3 * m + i])
            e_loads.append(pltpu.make_async_copy(*one))
    k_loads = block_copies(k_near, k_s, sems, 12, 0) + block_copies(k_far, k_s, sems, 17, 1024)
    q_loads = []
    for i, ref in enumerate((mix, mix_far)):
        one = (ref.at[pl.ds(1024, 1024)], q_s.at[pl.ds(i * 1024, 1024)], sems.at[22 + i])
        q_loads.append(pltpu.make_async_copy(*one))
    for load in e_loads[:3] + k_loads:
        load.start()
    for at, ins in ((0, row_in), (16, col_in)):
        for rel in range(2):
            for slot in range(8):
                total = ins[0][rel * 8 + slot : rel * 8 + slot + 1, :]
                for step in (1, 2, 3):
                    src = rel * 8 + (slot - 2 * step) % 8
                    total = total + ins[step][src : src + 1, :]
                dst = at + rel * 8 + slot
                inv[dst : dst + 1, :] = 1.0 / total
    inv_out[0:1, :] = inv[0:1, :]
    inv_out[1:2, :] = inv[16:17, :]
    inv_out[2:8, :] = jnp.zeros((6, DOCS), F32)
    stores = []

    def put(i, ref, grad):
        out_s[i] = grad.astype(BF)
        stores.append(pltpu.make_async_copy(out_s.at[i], ref, out_sems.at[i]))
        stores[-1].start()

    for m in range(4):
        for load in e_loads[3 * m : 3 * m + 3]:
            load.wait()
        for a in (2 * m, 2 * m + 1):
            rows = slice(a * DOCS, (a + 1) * DOCS)
            far = slice((8 + a) * DOCS, (9 + a) * DOCS)
            col_own = jnp.broadcast_to(inv[a : a + 1, :], (DOCS, DOCS)).T
            col_oth = jnp.broadcast_to(inv[8 + a : 9 + a, :], (DOCS, DOCS)).T
            for b in range(8):
                near_key = inv[16 + b : 17 + b, :]
                far_key = inv[24 + b : 25 + b, :]
                keys = slice(b * DOCS, (b + 1) * DOCS)
                keys_far = slice((8 + b) * DOCS, (9 + b) * DOCS)
                w1 = (e_s[0, rows, keys].astype(F32) * (col_own + near_key)).astype(BF)
                w2 = (e_s[1, rows, keys].astype(F32) * (col_own + far_key)).astype(BF)
                w3 = (e_s[2, rows, keys].astype(F32) * (col_oth + near_key)).astype(BF)
                wq[rows, keys] = w1
                wq[rows, keys_far] = w2
                wk[rows, keys] = w1
                wk[far, keys] = w3
        if m == 0:
            for load in k_loads:
                load.wait()
            for load in e_loads[3:] + q_loads:
                load.start()
        put(m, q_out[m], dot(wq[m * 256 : (m + 1) * 256, :], k_s[...]) * TAU_INV)
    for load in q_loads:
        load.wait()
    for m in range(4):
        put(4 + m, k_out[m], t_dot(wk[:, m * 256 : (m + 1) * 256], q_s[...]) * TAU_INV)
    for store in stores:
        store.wait()


def grads(k_near, k_far, e_own, mix, mix_far, row_in, col_in):
    return pl.pallas_call(
        grads_body,
        in_specs=[ANY] * 13 + [VMEM] * 8,
        out_specs=[ANY] * 8 + [VMEM],
        out_shape=[sds((256, EMB), BF)] * 8 + [sds((8, DOCS), F32)],
        scratch_shapes=[
            pltpu.VMEM((16 * DOCS, EMB), BF),
            pltpu.VMEM((16 * DOCS, EMB), BF),
            pltpu.VMEM((3, 8 * DOCS, 8 * DOCS), BF),
            pltpu.VMEM((8 * DOCS, 16 * DOCS), BF),
            pltpu.VMEM((16 * DOCS, 8 * DOCS), BF),
            pltpu.VMEM((8, 256, EMB), BF),
            pltpu.VMEM((32, DOCS), F32),
            pltpu.SemaphoreType.DMA((24,)),
            pltpu.SemaphoreType.DMA((8,)),
        ],
        compiler_params=params(),
    )(*k_near, *k_far, e_own, mix, mix_far, *row_in, *col_in)


def half_block(which):
    return pl.BlockSpec((DOCS, EMB), lambda i: (which, 0))


def pass_body(*refs):
    for ins, out in ((refs[0:4], refs[8]), (refs[4:8], refs[9])):
        out[...] = sum(ref[...].astype(F32) for ref in ins).astype(BF)


def pass_on(query_in, key_in):
    return pl.pallas_call(
        pass_body,
        grid=(1,),
        in_specs=[half_block(1)] * 8,
        out_specs=[half_block(0)] * 2,
        out_shape=[sds((DOCS, EMB), BF)] * 2,
        compiler_params=params(),
    )(*query_in, *key_in)


def keep_body(*refs):
    q_parts, k_parts = refs[0:4], refs[4:8]
    q_unit, paired, q_perm, pos, inv, q_out, k_out = refs[8:15]
    hot = one_hot(pos[...])
    same = eye()
    pair = paired[...].astype(F32)
    score = jnp.sum(q_unit[...].astype(F32) * pair, axis=1, keepdims=True) * TAU_INV
    expo = jnp.exp(score)
    inv_r = jnp.sum(same * inv[0:1, :], axis=1, keepdims=True)
    inv_c = jnp.sum(hot * inv[1:2, :], axis=1, keepdims=True)
    weight = expo * inv_r + expo * inv_c - 2.0
    weight_k = jnp.sum(same * jnp.sum(hot * weight, axis=0, keepdims=True), axis=1, keepdims=True)
    for parts, w, pair_rows, out in (
        (q_parts, weight, pair, q_out),
        (k_parts, weight_k, q_perm[...].astype(F32), k_out),
    ):
        out[...] = sum(ref[...].astype(F32) for ref in parts) + (w * TAU_INV) * pair_rows


def keep(query_in, key_in, q_unit, paired, q_perm, pos, inv):
    return pl.pallas_call(
        keep_body,
        grid=(1,),
        in_specs=[half_block(0)] * 11 + [VMEM] * 2,
        out_specs=[half_block(0)] * 2,
        out_shape=[sds((DOCS, EMB), F32)] * 2,
        compiler_params=params(),
    )(*query_in, *key_in, q_unit, paired, q_perm, pos, inv)


def back_body(q_keep, q_got, k_keep, k_got, q_raw, k_raw, out):
    for kept, got, raw, start in ((q_keep, q_got, q_raw, 0), (k_keep, k_got, k_raw, DOCS)):
        grad = kept[...] + got[...].astype(F32)
        exact, scale = unit_of(raw[...])
        inner = jnp.sum(exact * grad, axis=1, keepdims=True)
        out[start : start + DOCS, :] = (scale * (grad - exact * inner)).astype(BF)


def back(*args):
    return pl.pallas_call(
        back_body,
        in_specs=[VMEM] * 6,
        out_specs=VMEM,
        out_shape=sds((2 * DOCS, EMB), BF),
        compiler_params=params(),
    )(*args)


def contract_body(*refs):
    b_in, h_all, h_in, where, out = refs[0:4], refs[4], refs[5:8], refs[8], refs[9]
    h_s, b_s, o_s, sems, out_sems = refs[10:15]
    sources = (h_all.at[where[0]],) + tuple(h_in)
    loads = []
    for i in range(4):
        loads.append((b_in[i], b_s.at[pl.ds(i * 256, 256)]))
        loads.append((sources[i], h_s.at[:, pl.ds(i * 256, 256)]))
    loads = [pltpu.make_async_copy(s, d, sems.at[i]) for i, (s, d) in enumerate(loads)]
    for load in loads:
        load.start()
    for load in loads:
        load.wait()
    stores = []
    for m in range(4):
        rows = pl.ds(m * 256, 256)
        o_s[rows, :] = dot(h_s[rows, :], b_s[...]).astype(BF)
        stores.append(pltpu.make_async_copy(o_s.at[rows], out.at[rows], out_sems.at[m]))
        stores[-1].start()
    for store in stores:
        store.wait()


def contract(b_in, h_all, h_in, where):
    return pl.pallas_call(
        contract_body,
        in_specs=[ANY] * 8 + [SMEM],
        out_specs=ANY,
        out_shape=sds((1024, EMB), BF),
        scratch_shapes=[
            pltpu.VMEM((1024, 1024), BF),
            pltpu.VMEM((1024, EMB), BF),
            pltpu.VMEM((1024, EMB), BF),
            pltpu.SemaphoreType.DMA((8,)),
            pltpu.SemaphoreType.DMA((4,)),
        ],
        compiler_params=params(),
    )(*b_in, h_all, *h_in, where)


def flip_slots(value):
    return value[:, ::-1]


def to_owners(parts, move):
    return [parts[0]] + [move(parts[(4 - step) % 4], step, 0) for step in (1, 2, 3)]


def local(hid_query, hid_key, projection, tile_rows, tile_cols, tile_count, positive):
    row_index = lax.axis_index("row")
    col_index = lax.axis_index("col")
    core_index = lax.axis_index("dp")
    x, z_hi = row_index // 2, row_index % 2
    y, z_lo = col_index // 2, col_index % 2
    quarter = z_lo * 2 + core_index

    q_unit, k_unit, q_raw, k_raw = project(hid_query, hid_key, projection)
    k_flip = move_key(k_unit, 0, 1)
    q_flip = move_query(q_unit, 0, 1)

    pos = (positive - ((row_index * 8 + col_index) * 2 + core_index) * DOCS).reshape(DOCS, 1)
    paired, q_perm, pos_rows = pair_up(q_unit, k_unit, pos)
    turned = jnp.concatenate([hid_query, hid_key], axis=0).T.reshape(4, 2, 4, 2, 2, 32, 256)
    turned = turned.transpose(3, 4, 0, 1, 2, 5, 6).reshape(4, 1024, 256)
    h_flip = lax.dynamic_index_in_dim(turned, quarter ^ 2, 0, keepdims=False)
    h_both = lax.dynamic_index_in_dim(turned, quarter ^ 3, 0, keepdims=False)
    h_core = lax.dynamic_index_in_dim(turned, quarter ^ 1, 0, keepdims=False)
    entry_rows = tile_rows[0, 0]
    entry_cols = tile_cols[0, 0]
    used = jnp.arange(entry_rows.shape[0], dtype=jnp.int32) < tile_count[0, 0]
    slot_rows = ((y - entry_rows // 2) % 4) * 2 + (z_lo ^ (entry_rows % 2))
    slot_cols = ((x - entry_cols // 2) % 4) * 2 + (z_hi ^ (entry_cols % 2))
    eight = jnp.arange(8, dtype=jnp.int32)
    hit = (
        (slot_rows[:, None, None] == eight[None, :, None])
        & (slot_cols[:, None, None] == eight[None, None, :])
        & used[:, None, None]
    )
    mask = jnp.any(hit, axis=0).astype(F32)

    k_flip, q_flip, pos, paired, q_perm, pos_rows, turned, h_flip, h_both, h_core, mask = (
        lax.optimization_barrier(
            (k_flip, q_flip, pos, paired, q_perm, pos_rows, turned, h_flip, h_both, h_core, mask)
        )
    )
    k_pair = jnp.concatenate([k_unit, k_flip], axis=0)
    q_pair = jnp.concatenate([q_unit, q_flip], axis=0)
    k1 = move_key(k_pair, 1, 0)
    q1 = move_query(q_pair, 1, 0)
    k3 = move_key(k_pair, 3, 0)
    q3 = move_query(q_pair, 3, 0)
    k_far = swap(k_pair)
    k1, q1, k3, q3, k_far = lax.optimization_barrier((k1, q1, k3, q3, k_far))
    k_own = [
        k_pair,
        k1,
        move_key(k1[:DOCS], 1, 0),
        move_key(k3[DOCS:], 3, 0),
        k3,
    ]
    q_own = [
        q_pair,
        q1,
        move_query(q1[:DOCS], 1, 0),
        move_query(q3[DOCS:], 3, 0),
        q3,
    ]
    k1_far = swap(k1)
    k1_far, k3_late = lax.optimization_barrier((k1_far, k3))
    k3_far = swap(k3_late)
    k_oth = [k_far, k1_far, swap(k_own[2]), swap(k_own[3]), k3_far]

    h_flip, *blocks = lax.optimization_barrier((h_flip, *q_own, *k_oth))
    q_own, k_oth = blocks[:5], blocks[5:]
    h_flip = move_query(h_flip, 0, 1)
    e_own, mix, sums = scores(q_own, k_own, k_oth, mask, pos_rows)
    sums, mix, h_flip = lax.optimization_barrier((sums, mix, h_flip))
    far = swap(sums)
    far, mix = lax.optimization_barrier((far, mix))
    mix_far = swap(mix)
    row_part = jnp.concatenate([sums[:8], far[:8]], axis=0).reshape(8, 2, DOCS)
    col_part = sums[8:] + jnp.concatenate([far[16:], far[8:16]], axis=0)
    col_part = col_part.reshape(8, 2, DOCS)
    row_part = row_part + flip_slots(move_query(row_part, 0, 1))
    col_part = col_part + flip_slots(move_key(col_part, 0, 1))
    row_part = row_part.reshape(16, DOCS)
    col_part = col_part.reshape(16, DOCS)
    row_got = [row_part] + [move_query(row_part, step, 0) for step in (1, 2, 3)]
    col_got = [col_part] + [move_key(col_part, step, 0) for step in (1, 2, 3)]

    h_both, h_core, *got = lax.optimization_barrier((h_both, h_core, *row_got, *col_got))
    h_both = move_query(h_both, 0, 1)
    parts = grads(k_own, k_oth, e_own, mix, mix_far, got[:4], got[4:])
    h_both, *parts = lax.optimization_barrier((h_both, *parts))
    inv = parts[8]
    query_in = to_owners(parts[:4], move_query)
    key_in = to_owners(parts[4:8], move_key)
    q_send, k_send = pass_on(query_in, key_in)
    q_got = move_query(q_send, 0, 1)
    k_got = move_key(k_send, 0, 1)
    q_keep, k_keep = keep(query_in, key_in, q_unit, paired, q_perm, pos, inv)
    b_own = back(q_keep, q_got, k_keep, k_got, q_raw, k_raw)
    b_flip = move_query(b_own, 0, 1)
    out = contract(
        [b_own, swap(b_own), b_flip, swap(b_flip)],
        turned,
        [swap(h_core), h_flip, swap(h_both)],
        quarter.reshape(1).astype(jnp.int32),
    )
    out = lax.all_to_all(out, ("row", "col"), 0, 0, tiled=True, axis_index_groups=PLANES)
    return jnp.sum(out.reshape(32, 32, EMB).astype(F32), axis=0)


def solution(mesh):
    return jax.shard_map(
        local,
        mesh=mesh,
        in_specs=(
            P(("row", "col", "dp"), None),
            P(("row", "col", "dp"), None),
            P(),
            P("row", "col", None),
            P("row", "col", None),
            P("row", "col"),
            P(("row", "col", "dp")),
        ),
        out_specs=P(("row", "col", "dp"), None),
        check_vma=False,
    )
```

profile of v0, /device:TPU:0, one launch (start us, length us, event | category | flops | bytes accessed | tf_op | source)
XLA Modules:
  0.0 216.0 jit_solution(5222316955324455283)
XLA Ops:
  0.0 7.4 %shard_map.73 = (bf16[128,1024]{1,0:T(8,128)(2,1)}, bf16[128,1024]{1,0:T(8,128)(2,1)}, bf16[128,1024]{1,0:T(8,128)(2,1)}, bf16[128,1024]{1,0:T(8,128)(2,1)}) custom-call(bf16[128,4096]{1,0:T(8,128)(2,1)} %hq.1, bf16[128,4096]{1,0:T(8,128)(2,1)} %hk.1, bf16[4096,1024]{1,0:T(8,128)(2,1)} %proj.1), custom_call_target="tpu_custom_call" | custom-call | tf_op jit(solution)/shard_map/pallas_call | solution.py:101
  7.4 2.0 collective-permute-start.1
  9.4 3.6 %collective-permute-start = (bf16[128,1024]{1,0:T(8,128)(2,1)}, bf16[128,1024]{1,0:T(8,128)(2,1)}, u32[]{:S(2)}, u32[]{:S(2)}) collective-permute-start(bf16[128,1024]{1,0:T(8,128)(2,1)} %get-tuple-element.82.k_unit), channel_id=1, source_target_pairs={{0,16},{16,0},{32,48},{48,32},{64,80},{80,64},{96,112},{112,96},{1... | collective-permute-start | bytes 786440 | tf_op jit(solution)/shard_map/ppermute | solution.py:28
  18.3 2.2 %shard_map.74 = (bf16[128,1024]{1,0:T(8,128)(2,1)}, bf16[128,1024]{1,0:T(8,128)(2,1)}, f32[8,128]{1,0:T(8,128)}) custom-call(bf16[128,1024]{1,0:T(8,128)(2,1)} %get-tuple-element.83.q_unit.refs_8_, bf16[128,1024]{1,0:T(8,128)(2,1)} %get-tuple-element.82.k_unit, s32[128,1]{1,0:T(8,128)} %copy.16.pos), custom_call_target="tpu_custom_call" | custom-call | tf_op jit(solution)/shard_map/pallas_call | solution.py:141
  21.4 3.5 %collective-permute-done = bf16[128,1024]{1,0:T(8,128)(2,1)} collective-permute-done((bf16[128,1024]{1,0:T(8,128)(2,1)}, bf16[128,1024]{1,0:T(8,128)(2,1)}, u32[]{:S(2)}, u32[]{:S(2)}) %collective-permute-start) | collective-permute-done | bytes 262176 | tf_op jit(solution)/shard_map/ppermute | solution.py:28
  27.5 1.7 collective-permute-start.4
  31.9 1.7 collective-permute-start.5
  33.5 6.5 %collective-permute-done.2.refs_6_.refs_1_ = bf16[256,1024]{1,0:T(8,128)(2,1)S(1)} collective-permute-done((bf16[256,1024]{1,0:T(8,128)(2,1)S(1)}, bf16[256,1024]{1,0:T(8,128)(2,1)S(1)}, u32[]{:S(2)}, u32[]{:S(2)}) %collective-permute-start.2) | collective-permute-done | bytes 524320 | tf_op jit(solution)/shard_map/ppermute | solution.py:28
  40.0 5.9 %collective-permute-done.3.refs_1_ = bf16[256,1024]{1,0:T(8,128)(2,1)S(1)} collective-permute-done((bf16[256,1024]{1,0:T(8,128)(2,1)S(1)}, bf16[256,1024]{1,0:T(8,128)(2,1)S(1)}, u32[]{:S(2)}, u32[]{:S(2)}) %collective-permute-start.3) | collective-permute-done | bytes 524320 | tf_op jit(solution)/shard_map/ppermute | solution.py:24
  46.4 3.0 %collective-permute-start.12 = (bf16[128,1024]{1,0:T(8,128)(2,1)S(1)}, bf16[128,1024]{1,0:T(8,128)(2,1)S(1)}, u32[]{:S(2)}, u32[]{:S(2)}) collective-permute-start(bf16[128,1024]{1,0:T(8,128)(2,1)S(1)} %slice.30), channel_id=1, source_target_pairs={{0,96},{16,112},{32,0},{48,16},{64,32},{80,48},{96,64},{112,80},{1... | collective-permute-start | bytes 786440 | tf_op jit(solution)/shard_map/ppermute | solution.py:28
  51.1 1.8 collective-permute-start.8
  52.9 3.2 %collective-permute-done.10.refs_7_.refs_2_ = bf16[128,1024]{1,0:T(8,128)(2,1)S(1)} collective-permute-done((bf16[128,1024]{1,0:T(8,128)(2,1)S(1)}, bf16[128,1024]{1,0:T(8,128)(2,1)S(1)}, u32[]{:S(2)}, u32[]{:S(2)}) %collective-permute-start.10) | collective-permute-done | bytes 262176 | tf_op jit(solution)/shard_map/ppermute | solution.py:28
  56.5 2.9 %collective-permute-done.7.refs_2_ = bf16[128,1024]{1,0:T(8,128)(2,1)S(1)} collective-permute-done((bf16[128,1024]{1,0:T(8,128)(2,1)S(1)}, bf16[128,1024]{1,0:T(8,128)(2,1)S(1)}, u32[]{:S(2)}, u32[]{:S(2)}) %collective-permute-start.7) | collective-permute-done | bytes 262176 | tf_op jit(solution)/shard_map/ppermute | solution.py:24
  60.6 12.0 %shard_map.75 = (bf16[1024,1024]{1,0:T(8,128)(2,1)}, bf16[2048,1024]{1,0:T(8,128)(2,1)}, f32[24,128]{1,0:T(8,128)}) custom-call(bf16[256,1024]{1,0:T(8,128)(2,1)} %copy-done.19, bf16[256,1024]{1,0:T(8,128)(2,1)} %copy-done.17, bf16[128,1024]{1,0:T(8,128)(2,1)} %copy-done.31, bf16[128,1024]{1,0:T(8,128)(2,1)} %copy-done.32, bf16[256,1024]{1,0:T(8,128)(2,1)} %copy-done.18, ...), custom_call_target="tpu_custom_call" | custom-call | tf_op jit(solution)/shard_map/pallas_call | solution.py:222
  77.1 4.4 %collective-permute-done.21 = f32[8,2,128]{2,1,0:T(2,128)S(1)} collective-permute-done((f32[8,2,128]{2,1,0:T(2,128)S(1)}, f32[8,2,128]{2,1,0:T(2,128)S(1)}, u32[]{:S(2)}, u32[]{:S(2)}) %collective-permute-start.21) | collective-permute-done | bytes 8224 | tf_op jit(solution)/shard_map/ppermute | solution.py:28
  81.7 3.0 %collective-permute-start.23 = (f32[16,128]{1,0:T(8,128)S(1)}, f32[16,128]{1,0:T(8,128)S(1)}, u32[]{:S(2)}, u32[]{:S(2)}) collective-permute-start(f32[16,128]{1,0:T(8,128)S(1)} %bitcast.53), channel_id=1, source_target_pairs={{0,64},{16,80},{32,96},{48,112},{64,0},{80,16},{96,32},{112,48},{1... | collective-permute-start | bytes 24584 | tf_op jit(solution)/shard_map/ppermute | solution.py:28
  86.5 2.7 %collective-permute-start.19 = (f32[16,128]{1,0:T(8,128)S(1)}, f32[16,128]{1,0:T(8,128)S(1)}, u32[]{:S(2)}, u32[]{:S(2)}) collective-permute-start(f32[16,128]{1,0:T(8,128)S(1)} %bitcast.57), channel_id=1, source_target_pairs={{0,8},{2,10},{4,12},{6,14},{8,0},{10,2},{12,4},{14,6},{1,9},{3,11}... | collective-permute-start | bytes 24584 | tf_op jit(solution)/shard_map/ppermute | solution.py:24
  93.8 15.5 %shard_map.76 = (bf16[256,1024]{1,0:T(8,128)(2,1)}, bf16[256,1024]{1,0:T(8,128)(2,1)}, bf16[256,1024]{1,0:T(8,128)(2,1)}, bf16[256,1024]{1,0:T(8,128)(2,1)}, bf1...) custom-call(bf16[256,1024]{1,0:T(8,128)(2,1)} %copy-done.6, ...), custom_call_target="tpu_custom_call" | custom-call | tf_op jit(solution)/shard_map/pallas_call | solution.py:315
  111.0 2.9 %collective-permute-start.28 = (bf16[256,1024]{1,0:T(8,128)(2,1)}, bf16[256,1024]{1,0:T(8,128)(2,1)S(1)}, u32[]{:S(2)}, u32[]{:S(2)}) collective-permute-start(bf16[256,1024]{1,0:T(8,128)(2,1)} %get-tuple-element.139), channel_id=1, source_target_pairs={{0,8},{2,10},{4,12},{6,14},{8,0},{10,2},{12,4},{14,6},{1,9},{3,11}... | collective-permute-start | bytes 1572872 | tf_op jit(solution)/shard_map/ppermute | solution.py:24
  115.8 2.0 collective-permute-start.31
  117.8 8.2 %collective-permute-done.27.refs_1_ = bf16[256,1024]{1,0:T(8,128)(2,1)S(1)} collective-permute-done((bf16[256,1024]{1,0:T(8,128)(2,1)}, bf16[256,1024]{1,0:T(8,128)(2,1)S(1)}, u32[]{:S(2)}, u32[]{:S(2)}) %collective-permute-start.27) | collective-permute-done | bytes 524320 | tf_op jit(solution)/shard_map/ppermute | solution.py:24
  127.0 6.8 %collective-permute-done.28.refs_2_ = bf16[256,1024]{1,0:T(8,128)(2,1)S(1)} collective-permute-done((bf16[256,1024]{1,0:T(8,128)(2,1)}, bf16[256,1024]{1,0:T(8,128)(2,1)S(1)}, u32[]{:S(2)}, u32[]{:S(2)}) %collective-permute-start.28) | collective-permute-done | bytes 524320 | tf_op jit(solution)/shard_map/ppermute | solution.py:24
  133.9 3.2 %collective-permute-done.30.refs_5_ = bf16[256,1024]{1,0:T(8,128)(2,1)S(1)} collective-permute-done((bf16[256,1024]{1,0:T(8,128)(2,1)}, bf16[256,1024]{1,0:T(8,128)(2,1)S(1)}, u32[]{:S(2)}, u32[]{:S(2)}) %collective-permute-start.30) | collective-permute-done | bytes 524320 | tf_op jit(solution)/shard_map/ppermute | solution.py:28
  138.9 2.5 %shard_map.78 = (bf16[128,1024]{1,0:T(8,128)(2,1)}, bf16[128,1024]{1,0:T(8,128)(2,1)}) custom-call(bf16[256,1024]{1,0:T(8,128)(2,1)} %get-tuple-element.137.refs_0_, bf16[256,1024]{1,0:T(8,128)(2,1)} %copy-done.11, bf16[256,1024]{1,0:T(8,128)(2,1)} %copy-done.12, bf16[256,1024]{1,0:T(8,128)(2,1)} %copy-done.13, ...), custom_call_target="tpu_custom_call" | custom-call | tf_op jit(solution)/shard_map/pallas_call | solution.py:345
  143.5 3.1 %shard_map.77 = (f32[128,1024]{1,0:T(8,128)}, f32[128,1024]{1,0:T(8,128)}) custom-call(bf16[256,1024]{1,0:T(8,128)(2,1)} %get-tuple-element.137.refs_0_, bf16[256,1024]{1,0:T(8,128)(2,1)} %copy-done.11, bf16[256,1024]{1,0:T(8,128)(2,1)} %copy-done.12, bf16[256,1024]{1,0:T(8,128)(2,1)} %copy-done.13, bf16[256,1024]{1,0:T(8,128)(2,1)} %get-tuple-element.141.refs_4_, ...), custom_call_target="tpu_custom_call" | custom-call | tf_op jit(solution)/shard_map/pallas_call | solution.py:375
  146.6 2.1 collective-permute-done.33.q_got
  148.7 2.5 %collective-permute-done.34.k_got = bf16[128,1024]{1,0:T(8,128)(2,1)S(1)} collective-permute-done((bf16[128,1024]{1,0:T(8,128)(2,1)}, bf16[128,1024]{1,0:T(8,128)(2,1)S(1)}, u32[]{:S(2)}, u32[]{:S(2)}) %collective-permute-start.34) | collective-permute-done | bytes 262176 | tf_op jit(solution)/shard_map/ppermute | solution.py:28
  151.8 2.7 %shard_map.79.refs_0_ = bf16[256,1024]{1,0:T(8,128)(2,1)} custom-call(f32[128,1024]{1,0:T(8,128)} %get-tuple-element.149.q_keep, bf16[128,1024]{1,0:T(8,128)(2,1)} %copy-done.33, f32[128,1024]{1,0:T(8,128)} %get-tuple-element.151.k_keep, bf16[128,1024]{1,0:T(8,128)(2,1)} %copy-done.34, bf16[128,1024]{1,0:T(8,128)(2,1)} %get-tuple-element.153.q_raw, ...), custom_call_target="tpu_custom_call" | custom-call | tf_op jit(solution)/shard_map/pallas_call | solution.py:394
  155.9 8.0 %collective-permute-done.36.refs_2_ = bf16[256,1024]{1,0:T(8,128)(2,1)S(1)} collective-permute-done((bf16[256,1024]{1,0:T(8,128)(2,1)}, bf16[256,1024]{1,0:T(8,128)(2,1)S(1)}, u32[]{:S(2)}, u32[]{:S(2)}) %collective-permute-start.36) | collective-permute-done | bytes 524320 | tf_op jit(solution)/shard_map/ppermute | solution.py:24
  164.0 1.9 collective-permute-done.37.refs_3_
  166.7 5.4 %shard_map.80 = bf16[1024,1024]{1,0:T(8,128)(2,1)} custom-call(bf16[256,1024]{1,0:T(8,128)(2,1)} %shard_map.79.refs_0_, bf16[256,1024]{1,0:T(8,128)(2,1)} %copy-done.29, bf16[256,1024]{1,0:T(8,128)(2,1)} %copy-done.26, bf16[256,1024]{1,0:T(8,128)(2,1)} %copy-done.30, bf16[4,1024,256]{2,1,0:T(8,128)(2,1)} %bitcast.49, bf16[1024,256]{1,0:T(8,128)(2,1)} %copy-done.27, ...), custom_call_target="tpu_custom_call" | custom-call | tf_op jit(solution)/shard_map/pallas_call | solution.py:427
  172.0 42.9 %all_to_all.9 = bf16[32,32,1024]{2,1,0:T(8,128)(2,1)S(1)} all-to-all(bf16[32,32,1024]{2,1,0:T(8,128)(2,1)} %bitcast.51), channel_id=1, replica_groups={{0,4,8,12,16,20,24,28,32,36,40,44,48,52,56,60,64,68,72,76,80,84,88,92,9..., dimensions={0} | all-to-all | bytes 4194304 | tf_op jit(solution)/shard_map/all_to_all | solution.py:552
  (184 shorter events, 37.9 us)
Async XLA Ops:
  7.4 14.0 %collective-permute-start.1 = (bf16[128,1024]{1,0:T(8,128)(2,1)}, bf16[128,1024]{1,0:T(8,128)(2,1)}, u32[]{:S(2)}, u32[]{:S(2)}) collective-permute-start(bf16[128,1024]{1,0:T(8,128)(2,1)} %get-tuple-element.83.q_unit.refs_8_), channel_id=1, source_target_pairs={{0,2},{2,0},{4,6},{6,4},{8,10},{10,8},{12,14},{14,12},{1,3},{3,1},... | collective-permute-start | bytes 786440 | tf_op jit(solution)/shard_map/ppermute | solution.py:24
  9.4 15.5 %collective-permute-start = (bf16[128,1024]{1,0:T(8,128)(2,1)}, bf16[128,1024]{1,0:T(8,128)(2,1)}, u32[]{:S(2)}, u32[]{:S(2)}) collective-permute-start(bf16[128,1024]{1,0:T(8,128)(2,1)} %get-tuple-element.82.k_unit), channel_id=1, source_target_pairs={{0,16},{16,0},{32,48},{48,32},{64,80},{80,64},{96,112},{112,96},{1... | collective-permute-start | bytes 786440 | tf_op jit(solution)/shard_map/ppermute | solution.py:28
  25.9 14.1 %collective-permute-start.2 = (bf16[256,1024]{1,0:T(8,128)(2,1)S(1)}, bf16[256,1024]{1,0:T(8,128)(2,1)S(1)}, u32[]{:S(2)}, u32[]{:S(2)}) collective-permute-start(bf16[256,1024]{1,0:T(8,128)(2,1)S(1)} %constant_dynamic-update-slice_fusion.2.refs_5_.refs_0_), channel_id=1, source_target_pairs={{0,32},{16,48},{32,64},{48,80},{64,96},{80,112},{96,0},{112,16},{1... | collective-permute-start | bytes 1572872 | tf_op jit(solution)/shard_map/ppermute | solution.py:28
  27.5 12.5 %collective-permute-start.4 = (bf16[256,1024]{1,0:T(8,128)(2,1)S(1)}, bf16[256,1024]{1,0:T(8,128)(2,1)S(1)}, u32[]{:S(2)}, u32[]{:S(2)}) collective-permute-start(bf16[256,1024]{1,0:T(8,128)(2,1)S(1)} %constant_dynamic-update-slice_fusion.2.refs_5_.refs_0_), channel_id=1, source_target_pairs={{0,96},{16,112},{32,0},{48,16},{64,32},{80,48},{96,64},{112,80},{1... | collective-permute-start | bytes 1572872 | tf_op jit(solution)/shard_map/ppermute | solution.py:28
  29.2 10.8 %collective-permute-start.6 = (bf16[256,1024]{1,0:T(8,128)(2,1)S(1)}, bf16[256,1024]{1,0:T(8,128)(2,1)S(1)}, u32[]{:S(2)}, u32[]{:S(2)}) collective-permute-start(bf16[256,1024]{1,0:T(8,128)(2,1)S(1)} %constant_dynamic-update-slice_fusion.2.refs_5_.refs_0_), channel_id=1, source_target_pairs={{0,1},{1,0},{2,3},{3,2},{4,5},{5,4},{6,7},{7,6},{8,9},{9,8},{10,11... | collective-permute-start | bytes 1572872 | tf_op jit(solution)/shard_map/ppermute | solution.py:42
  30.2 15.7 %collective-permute-start.3 = (bf16[256,1024]{1,0:T(8,128)(2,1)S(1)}, bf16[256,1024]{1,0:T(8,128)(2,1)S(1)}, u32[]{:S(2)}, u32[]{:S(2)}) collective-permute-start(bf16[256,1024]{1,0:T(8,128)(2,1)S(1)} %constant_dynamic-update-slice_fusion.refs_0_), channel_id=1, source_target_pairs={{0,4},{2,6},{4,8},{6,10},{8,12},{10,14},{12,0},{14,2},{1,5},{3,7},... | collective-permute-start | bytes 1572872 | tf_op jit(solution)/shard_map/ppermute | solution.py:24
  31.9 14.1 %collective-permute-start.5 = (bf16[256,1024]{1,0:T(8,128)(2,1)S(1)}, bf16[256,1024]{1,0:T(8,128)(2,1)S(1)}, u32[]{:S(2)}, u32[]{:S(2)}) collective-permute-start(bf16[256,1024]{1,0:T(8,128)(2,1)S(1)} %constant_dynamic-update-slice_fusion.refs_0_), channel_id=1, source_target_pairs={{0,12},{2,14},{4,0},{6,2},{8,4},{10,6},{12,8},{14,10},{1,13},{3,15... | collective-permute-start | bytes 1572872 | tf_op jit(solution)/shard_map/ppermute | solution.py:24
  46.0 10.0 %collective-permute-start.10 = (bf16[128,1024]{1,0:T(8,128)(2,1)S(1)}, bf16[128,1024]{1,0:T(8,128)(2,1)S(1)}, u32[]{:S(2)}, u32[]{:S(2)}) collective-permute-start(bf16[128,1024]{1,0:T(8,128)(2,1)S(1)} %slice.29), channel_id=1, source_target_pairs={{0,32},{16,48},{32,64},{48,80},{64,96},{80,112},{96,0},{112,16},{1... | collective-permute-start | bytes 786440 | tf_op jit(solution)/shard_map/ppermute | solution.py:28
  46.4 9.6 %collective-permute-start.12 = (bf16[128,1024]{1,0:T(8,128)(2,1)S(1)}, bf16[128,1024]{1,0:T(8,128)(2,1)S(1)}, u32[]{:S(2)}, u32[]{:S(2)}) collective-permute-start(bf16[128,1024]{1,0:T(8,128)(2,1)S(1)} %slice.30), channel_id=1, source_target_pairs={{0,96},{16,112},{32,0},{48,16},{64,32},{80,48},{96,64},{112,80},{1... | collective-permute-start | bytes 786440 | tf_op jit(solution)/shard_map/ppermute | solution.py:28
  49.4 10.2 %collective-permute-start.14 = (bf16[256,1024]{1,0:T(8,128)(2,1)S(1)}, bf16[256,1024]{1,0:T(8,128)(2,1)S(1)}, u32[]{:S(2)}, u32[]{:S(2)}) collective-permute-start(bf16[256,1024]{1,0:T(8,128)(2,1)S(1)} %collective-permute-done.4.refs_9_.refs_4_), channel_id=1, source_target_pairs={{0,1},{1,0},{2,3},{3,2},{4,5},{5,4},{6,7},{7,6},{8,9},{9,8},{10,11... | collective-permute-start | bytes 1572872 | tf_op jit(solution)/shard_map/ppermute | solution.py:42
  49.5 10.0 %collective-permute-start.7 = (bf16[128,1024]{1,0:T(8,128)(2,1)S(1)}, bf16[128,1024]{1,0:T(8,128)(2,1)S(1)}, u32[]{:S(2)}, u32[]{:S(2)}) collective-permute-start(bf16[128,1024]{1,0:T(8,128)(2,1)S(1)} %slice.27), channel_id=1, source_target_pairs={{0,4},{2,6},{4,8},{6,10},{8,12},{10,14},{12,0},{14,2},{1,5},{3,7},... | collective-permute-start | bytes 786440 | tf_op jit(solution)/shard_map/ppermute | solution.py:24
  51.1 8.5 %collective-permute-start.8 = (bf16[128,1024]{1,0:T(8,128)(2,1)S(1)}, bf16[128,1024]{1,0:T(8,128)(2,1)S(1)}, u32[]{:S(2)}, u32[]{:S(2)}) collective-permute-start(bf16[128,1024]{1,0:T(8,128)(2,1)S(1)} %slice.28), channel_id=1, source_target_pairs={{0,12},{2,14},{4,0},{6,2},{8,4},{10,6},{12,8},{14,10},{1,13},{3,15... | collective-permute-start | bytes 786440 | tf_op jit(solution)/shard_map/ppermute | solution.py:24
  59.6 13.8 %collective-permute-start.15 = (bf16[1024,256]{1,0:T(8,128)(2,1)S(1)}, bf16[1024,256]{1,0:T(8,128)(2,1)}, u32[]{:S(2)}, u32[]{:S(2)}) collective-permute-start(bf16[1024,256]{1,0:T(8,128)(2,1)S(1)} %get-tuple-element.113), channel_id=1, source_target_pairs={{0,2},{2,0},{4,6},{6,4},{8,10},{10,8},{12,14},{14,12},{1,3},{3,1},... | collective-permute-start | bytes 1572872 | tf_op jit(solution)/shard_map/ppermute | solution.py:24
  74.8 18.9 %collective-permute-start.26 = (bf16[2048,1024]{1,0:T(8,128)(2,1)}, bf16[2048,1024]{1,0:T(8,128)(2,1)}, u32[]{:S(2)}, u32[]{:S(2)}) collective-permute-start(bf16[2048,1024]{1,0:T(8,128)(2,1)} %get-tuple-element.119.refs_11_), channel_id=1, source_target_pairs={{0,1},{1,0},{2,3},{3,2},{4,5},{5,4},{6,7},{7,6},{8,9},{9,8},{10,11... | collective-permute-start | bytes 12582920 | tf_op jit(solution)/shard_map/ppermute | solution.py:42
  76.4 8.5 %collective-permute-start.17 = (f32[8,2,128]{2,1,0:T(2,128)S(1)}, f32[8,2,128]{2,1,0:T(2,128)S(1)}, u32[]{:S(2)}, u32[]{:S(2)}) collective-permute-start(f32[8,2,128]{2,1,0:T(2,128)S(1)} %bitcast.62), channel_id=1, source_target_pairs={{0,2},{2,0},{4,6},{6,4},{8,10},{10,8},{12,14},{14,12},{1,3},{3,1},... | collective-permute-start | bytes 24584 | tf_op jit(solution)/shard_map/ppermute | solution.py:24
  81.7 7.5 %collective-permute-start.23 = (f32[16,128]{1,0:T(8,128)S(1)}, f32[16,128]{1,0:T(8,128)S(1)}, u32[]{:S(2)}, u32[]{:S(2)}) collective-permute-start(f32[16,128]{1,0:T(8,128)S(1)} %bitcast.53), channel_id=1, source_target_pairs={{0,64},{16,80},{32,96},{48,112},{64,0},{80,16},{96,32},{112,48},{1... | collective-permute-start | bytes 24584 | tf_op jit(solution)/shard_map/ppermute | solution.py:28
  84.6 5.7 %collective-permute-start.24 = (f32[16,128]{1,0:T(8,128)S(1)}, f32[16,128]{1,0:T(8,128)S(1)}, u32[]{:S(2)}, u32[]{:S(2)}) collective-permute-start(f32[16,128]{1,0:T(8,128)S(1)} %bitcast.54), channel_id=1, source_target_pairs={{0,96},{16,112},{32,0},{48,16},{64,32},{80,48},{96,64},{112,80},{1... | collective-permute-start | bytes 24584 | tf_op jit(solution)/shard_map/ppermute | solution.py:28
  85.0 5.4 %collective-permute-start.18 = (f32[16,128]{1,0:T(8,128)S(1)}, f32[16,128]{1,0:T(8,128)S(1)}, u32[]{:S(2)}, u32[]{:S(2)}) collective-permute-start(f32[16,128]{1,0:T(8,128)S(1)} %bitcast.56), channel_id=1, source_target_pairs={{0,4},{2,6},{4,8},{6,10},{8,12},{10,14},{12,0},{14,2},{1,5},{3,7},... | collective-permute-start | bytes 24584 | tf_op jit(solution)/shard_map/ppermute | solution.py:24
  86.5 5.2 %collective-permute-start.19 = (f32[16,128]{1,0:T(8,128)S(1)}, f32[16,128]{1,0:T(8,128)S(1)}, u32[]{:S(2)}, u32[]{:S(2)}) collective-permute-start(f32[16,128]{1,0:T(8,128)S(1)} %bitcast.57), channel_id=1, source_target_pairs={{0,8},{2,10},{4,12},{6,14},{8,0},{10,2},{12,4},{14,6},{1,9},{3,11}... | collective-permute-start | bytes 24584 | tf_op jit(solution)/shard_map/ppermute | solution.py:24
  92.9 16.4 %collective-permute-start.25 = (bf16[1024,256]{1,0:T(8,128)(2,1)S(1)}, bf16[1024,256]{1,0:T(8,128)(2,1)S(1)}, u32[]{:S(2)}, u32[]{:S(2)}) collective-permute-start(bf16[1024,256]{1,0:T(8,128)(2,1)S(1)} %get-tuple-element.117), channel_id=1, source_target_pairs={{0,2},{2,0},{4,6},{6,4},{8,10},{10,8},{12,14},{14,12},{1,3},{3,1},... | collective-permute-start | bytes 1572872 | tf_op jit(solution)/shard_map/ppermute | solution.py:24
  110.1 15.9 %collective-permute-start.27 = (bf16[256,1024]{1,0:T(8,128)(2,1)}, bf16[256,1024]{1,0:T(8,128)(2,1)S(1)}, u32[]{:S(2)}, u32[]{:S(2)}) collective-permute-start(bf16[256,1024]{1,0:T(8,128)(2,1)} %get-tuple-element.138), channel_id=1, source_target_pairs={{0,4},{2,6},{4,8},{6,10},{8,12},{10,14},{12,0},{14,2},{1,5},{3,7},... | collective-permute-start | bytes 1572872 | tf_op jit(solution)/shard_map/ppermute | solution.py:24
  111.0 22.8 %collective-permute-start.28 = (bf16[256,1024]{1,0:T(8,128)(2,1)}, bf16[256,1024]{1,0:T(8,128)(2,1)S(1)}, u32[]{:S(2)}, u32[]{:S(2)}) collective-permute-start(bf16[256,1024]{1,0:T(8,128)(2,1)} %get-tuple-element.139), channel_id=1, source_target_pairs={{0,8},{2,10},{4,12},{6,14},{8,0},{10,2},{12,4},{14,6},{1,9},{3,11}... | collective-permute-start | bytes 1572872 | tf_op jit(solution)/shard_map/ppermute | solution.py:24
  113.9 20.0 %collective-permute-start.29 = (bf16[256,1024]{1,0:T(8,128)(2,1)}, bf16[256,1024]{1,0:T(8,128)(2,1)S(1)}, u32[]{:S(2)}, u32[]{:S(2)}) collective-permute-start(bf16[256,1024]{1,0:T(8,128)(2,1)} %get-tuple-element.140), channel_id=1, source_target_pairs={{0,12},{2,14},{4,0},{6,2},{8,4},{10,6},{12,8},{14,10},{1,13},{3,15... | collective-permute-start | bytes 1572872 | tf_op jit(solution)/shard_map/ppermute | solution.py:24
  114.5 22.6 %collective-permute-start.30 = (bf16[256,1024]{1,0:T(8,128)(2,1)}, bf16[256,1024]{1,0:T(8,128)(2,1)S(1)}, u32[]{:S(2)}, u32[]{:S(2)}) collective-permute-start(bf16[256,1024]{1,0:T(8,128)(2,1)} %get-tuple-element.142), channel_id=1, source_target_pairs={{0,32},{16,48},{32,64},{48,80},{64,96},{80,112},{96,0},{112,16},{1... | collective-permute-start | bytes 1572872 | tf_op jit(solution)/shard_map/ppermute | solution.py:28
  115.8 21.3 %collective-permute-start.31 = (bf16[256,1024]{1,0:T(8,128)(2,1)}, bf16[256,1024]{1,0:T(8,128)(2,1)S(1)}, u32[]{:S(2)}, u32[]{:S(2)}) collective-permute-start(bf16[256,1024]{1,0:T(8,128)(2,1)} %get-tuple-element.143), channel_id=1, source_target_pairs={{0,64},{16,80},{32,96},{48,112},{64,0},{80,16},{96,32},{112,48},{1... | collective-permute-start | bytes 1572872 | tf_op jit(solution)/shard_map/ppermute | solution.py:28
  126.0 11.7 %collective-permute-start.32 = (bf16[256,1024]{1,0:T(8,128)(2,1)}, bf16[256,1024]{1,0:T(8,128)(2,1)S(1)}, u32[]{:S(2)}, u32[]{:S(2)}) collective-permute-start(bf16[256,1024]{1,0:T(8,128)(2,1)} %get-tuple-element.144), channel_id=1, source_target_pairs={{0,96},{16,112},{32,0},{48,16},{64,32},{80,48},{96,64},{112,80},{1... | collective-permute-start | bytes 1572872 | tf_op jit(solution)/shard_map/ppermute | solution.py:28
  141.4 7.3 %collective-permute-start.33 = (bf16[128,1024]{1,0:T(8,128)(2,1)}, bf16[128,1024]{1,0:T(8,128)(2,1)S(1)}, u32[]{:S(2)}, u32[]{:S(2)}) collective-permute-start(bf16[128,1024]{1,0:T(8,128)(2,1)} %get-tuple-element.150), channel_id=1, source_target_pairs={{0,2},{2,0},{4,6},{6,4},{8,10},{10,8},{12,14},{14,12},{1,3},{3,1},... | collective-permute-start | bytes 786440 | tf_op jit(solution)/shard_map/ppermute | solution.py:24
  142.5 8.6 %collective-permute-start.34 = (bf16[128,1024]{1,0:T(8,128)(2,1)}, bf16[128,1024]{1,0:T(8,128)(2,1)S(1)}, u32[]{:S(2)}, u32[]{:S(2)}) collective-permute-start(bf16[128,1024]{1,0:T(8,128)(2,1)} %get-tuple-element.152), channel_id=1, source_target_pairs={{0,16},{16,0},{32,48},{48,32},{64,80},{80,64},{96,112},{112,96},{1... | collective-permute-start | bytes 786440 | tf_op jit(solution)/shard_map/ppermute | solution.py:28
  154.6 9.4 %collective-permute-start.36 = (bf16[256,1024]{1,0:T(8,128)(2,1)}, bf16[256,1024]{1,0:T(8,128)(2,1)S(1)}, u32[]{:S(2)}, u32[]{:S(2)}) collective-permute-start(bf16[256,1024]{1,0:T(8,128)(2,1)} %shard_map.79.refs_0_), channel_id=1, source_target_pairs={{0,2},{2,0},{4,6},{6,4},{8,10},{10,8},{12,14},{14,12},{1,3},{3,1},... | collective-permute-start | bytes 1572872 | tf_op jit(solution)/shard_map/ppermute | solution.py:24
  155.3 8.6 %collective-permute-start.38 = (bf16[1024,256]{1,0:T(8,128)(2,1)S(1)}, bf16[1024,256]{1,0:T(8,128)(2,1)S(1)}, u32[]{:S(2)}, u32[]{:S(2)}) collective-permute-start(bf16[1024,256]{1,0:T(8,128)(2,1)S(1)} %copy-done.25), channel_id=1, source_target_pairs={{0,1},{1,0},{2,3},{3,2},{4,5},{5,4},{6,7},{7,6},{8,9},{9,8},{10,11... | collective-permute-start | bytes 1572872 | tf_op jit(solution)/shard_map/ppermute | solution.py:42
  155.3 8.6 %collective-permute-start.39 = (bf16[1024,256]{1,0:T(8,128)(2,1)S(1)}, bf16[1024,256]{1,0:T(8,128)(2,1)S(1)}, u32[]{:S(2)}, u32[]{:S(2)}) collective-permute-start(bf16[1024,256]{1,0:T(8,128)(2,1)S(1)} %copy-done.46), channel_id=1, source_target_pairs={{0,1},{1,0},{2,3},{3,2},{4,5},{5,4},{6,7},{7,6},{8,9},{9,8},{10,11... | collective-permute-start | bytes 1572872 | tf_op jit(solution)/shard_map/ppermute | solution.py:42
  155.8 8.2 %collective-permute-start.35 = (bf16[256,1024]{1,0:T(8,128)(2,1)}, bf16[256,1024]{1,0:T(8,128)(2,1)S(1)}, u32[]{:S(2)}, u32[]{:S(2)}) collective-permute-start(bf16[256,1024]{1,0:T(8,128)(2,1)} %shard_map.79.refs_0_), channel_id=1, source_target_pairs={{0,1},{1,0},{2,3},{3,2},{4,5},{5,4},{6,7},{7,6},{8,9},{9,8},{10,11... | collective-permute-start | bytes 1572872 | tf_op jit(solution)/shard_map/ppermute | solution.py:42
  (56 other events, 338.0 us)
where the time goes:
time: 217 us; the launch traced here: 216 us
  waiting for transfers between devices  64.7 us (30%)
  Pallas kernels  50.6 us (23%)
  blocking collectives  42.9 us (20%)
  starting transfers between devices  41.5 us (19%)
  local copies, waits for them, and re-layouts  12.1 us (6%)
  other arithmetic  2.84 us (1%)
    all_to_all x1, blocking collectives, local(): lax.all_to_all(out, ('row', 'col'), 0, 0, tiled=True, axis_index_groups=P...  42.9 us
    ppermute x16, waiting for transfers between devices, move_query(): return lax.ppermute(value, 'col', ring_pair(step, flip))  37.4 us
    ppermute x13, waiting for transfers between devices, move_key(): return lax.ppermute(value, 'row', ring_pair(step, flip))  24 us
    ppermute x16, starting transfers between devices, move_query(): return lax.ppermute(value, 'col', ring_pair(step, flip))  22.1 us
    ppermute x13, starting transfers between devices, move_key(): return lax.ppermute(value, 'row', ring_pair(step, flip))  18.1 us
    pallas_call x1, Pallas kernels, grads(): pl.pallas_call(grads_body, in_specs=[ANY] * 13 + [VMEM] * 8, out_specs=[A...  15.5 us
    pallas_call x1, Pallas kernels, scores(): pl.pallas_call(scores_body, in_specs=[ANY] * 15 + [SMEM, VMEM], out_specs...  12 us
    pallas_call x1, Pallas kernels, project(): pl.pallas_call(project_body, grid=(HID // depth,), in_specs=[pl.BlockSpec...  7.4 us
  transfers between devices with their start and end apart: 40, of which 21 were waited for; matrix products, arithmetic and copies ran while one was open for 4% of the time, Pallas kernels for 15%

commit v1 on v0

--- a/solution.py
+++ b/solution.py
@@ -165,23 +165,27 @@
     q_s, k_s, e_s, acc, in_sems, out_sems = refs[20:26]
     q_loads = block_copies(q_in, q_s, in_sems, 0, 0)
     k_loads = block_copies(k_near, k_s, in_sems, 5, 0) + block_copies(k_far, k_s, in_sems, 10, 1024)
-    for load in k_loads[:1] + q_loads:
+    for load in k_loads[:1] + q_loads + k_loads[1:]:
         load.start()
     waits = ((0,), (1,), (2, 3), (4,), (5,), (6,), (7, 8), (9,))
+
+    def score_of(b, m):
+        if m == 0:
+            for i in waits[b]:
+                k_loads[i].wait()
+        if b == 0:
+            for i in waits[m]:
+                q_loads[i].wait()
+        return dot_t(q_s[m * 256 : (m + 1) * 256, :], k_s[b * 256 : (b + 1) * 256, :])
+
     stores = []
+    following = score_of(0, 0)
     for b in range(8):
-        for i in waits[b]:
-            k_loads[i].wait()
         total = [None, None]
         for m in range(4):
-            if b == 0:
-                for i in waits[m]:
-                    q_loads[i].wait()
-                if m == 3:
-                    for load in k_loads[1:]:
-                        load.start()
-            chunk = slice(m * 256, (m + 1) * 256)
-            score = dot_t(q_s[chunk, :], k_s[b * 256 : (b + 1) * 256, :])
+            score = following
+            if m < 3 or b < 7:
+                following = score_of(b + (m + 1) // 4, (m + 1) % 4)
             for n in range(2):
                 a = m * 2 + n
                 rows = slice(a * DOCS, (a + 1) * DOCS)
@@ -487,6 +491,7 @@
     )
     k_pair = jnp.concatenate([k_unit, k_flip], axis=0)
     q_pair = jnp.concatenate([q_unit, q_flip], axis=0)
+    k_pair, q_pair = lax.optimization_barrier((k_pair, q_pair))
     k1 = move_key(k_pair, 1, 0)
     q1 = move_query(q_pair, 1, 0)
     k3 = move_key(k_pair, 3, 0)

time: 217 us -> 214 us (0.986)
  local copies, waits for them, and re-layouts: 12.1 us -> 9.66 us
    unnamed x100 -> x98, local copies, waits for them, and re-layouts: 6.74 us -> 6.1 us
  transfers between devices with their start and end apart: 40 -> 40, of which waited for: 21 -> 22; matrix products, arithmetic and copies ran while one was open for 4% -> 3% of each run, Pallas kernels for 15% -> 15%
where the time goes in v1:
time: 214 us; the launch traced here: 213 us
  waiting for transfers between devices  65.1 us (30%)
  Pallas kernels  49.8 us (23%)
  blocking collectives  42.7 us (20%)
  starting transfers between devices  40.5 us (19%)
  local copies, waits for them, and re-layouts  9.66 us (5%)
  other arithmetic  3.88 us (2%)
    all_to_all x1, blocking collectives, local(): lax.all_to_all(out, ('row', 'col'), 0, 0, tiled=True, axis_index_groups=P...  42.7 us
    ppermute x16, waiting for transfers between devices, move_query(): return lax.ppermute(value, 'col', ring_pair(step, flip))  36.3 us
    ppermute x13, waiting for transfers between devices, move_key(): return lax.ppermute(value, 'row', ring_pair(step, flip))  25.5 us
    ppermute x16, starting transfers between devices, move_query(): return lax.ppermute(value, 'col', ring_pair(step, flip))  21.3 us
    ppermute x13, starting transfers between devices, move_key(): return lax.ppermute(value, 'row', ring_pair(step, flip))  17.8 us
    pallas_call x1, Pallas kernels, grads(): pl.pallas_call(grads_body, in_specs=[ANY] * 13 + [VMEM] * 8, out_specs=[A...  15.4 us
    pallas_call x1, Pallas kernels, scores(): pl.pallas_call(scores_body, in_specs=[ANY] * 15 + [SMEM, VMEM], out_specs...  11.2 us
    pallas_call x1, Pallas kernels, project(): pl.pallas_call(project_body, grid=(HID // depth,), in_specs=[pl.BlockSpec...  7.4 us
  transfers between devices with their start and end apart: 40, of which 22 were waited for; matrix products, arithmetic and copies ran while one was open for 3% of the time, Pallas kernels for 15%

profile of v1, /device:TPU:0, one launch (start us, length us, event | category | flops | bytes accessed | tf_op | source)
XLA Modules:
  0.0 213.0 jit_solution(1829977015823056354)
XLA Ops:
  0.0 7.4 %shard_map.73 = (bf16[128,1024]{1,0:T(8,128)(2,1)}, bf16[128,1024]{1,0:T(8,128)(2,1)}, bf16[128,1024]{1,0:T(8,128)(2,1)}, bf16[128,1024]{1,0:T(8,128)(2,1)}) custom-call(bf16[128,4096]{1,0:T(8,128)(2,1)} %hq.1, bf16[128,4096]{1,0:T(8,128)(2,1)} %hk.1, bf16[4096,1024]{1,0:T(8,128)(2,1)} %proj.1), custom_call_target="tpu_custom_call" | custom-call | tf_op jit(solution)/shard_map/pallas_call | solution.py:101
  7.4 2.0 collective-permute-start.1
  9.4 3.6 %collective-permute-start = (bf16[128,1024]{1,0:T(8,128)(2,1)}, bf16[128,1024]{1,0:T(8,128)(2,1)}, u32[]{:S(2)}, u32[]{:S(2)}) collective-permute-start(bf16[128,1024]{1,0:T(8,128)(2,1)} %get-tuple-element.84.k_unit), channel_id=1, source_target_pairs={{0,16},{16,0},{32,48},{48,32},{64,80},{80,64},{96,112},{112,96},{1... | collective-permute-start | bytes 786440 | tf_op jit(solution)/shard_map/ppermute | solution.py:28
  17.7 2.1 shard_map.74
  20.9 4.1 %collective-permute-done = bf16[128,1024]{1,0:T(8,128)(2,1)} collective-permute-done((bf16[128,1024]{1,0:T(8,128)(2,1)}, bf16[128,1024]{1,0:T(8,128)(2,1)}, u32[]{:S(2)}, u32[]{:S(2)}) %collective-permute-start) | collective-permute-done | bytes 262176 | tf_op jit(solution)/shard_map/ppermute | solution.py:28
  29.1 1.7 collective-permute-start.4
  30.9 1.7 collective-permute-start.5
  32.6 7.5 %collective-permute-done.2.refs_6_.refs_1_ = bf16[256,1024]{1,0:T(8,128)(2,1)S(1)} collective-permute-done((bf16[256,1024]{1,0:T(8,128)(2,1)S(1)}, bf16[256,1024]{1,0:T(8,128)(2,1)S(1)}, u32[]{:S(2)}, u32[]{:S(2)}) %collective-permute-start.2) | collective-permute-done | bytes 524320 | tf_op jit(solution)/shard_map/ppermute | solution.py:28
  43.3 3.0 %collective-permute-start.12 = (bf16[128,1024]{1,0:T(8,128)(2,1)S(1)}, bf16[128,1024]{1,0:T(8,128)(2,1)S(1)}, u32[]{:S(2)}, u32[]{:S(2)}) collective-permute-start(bf16[128,1024]{1,0:T(8,128)(2,1)S(1)} %slice.30), channel_id=1, source_target_pairs={{0,96},{16,112},{32,0},{48,16},{64,32},{80,48},{96,64},{112,80},{1... | collective-permute-start | bytes 786440 | tf_op jit(solution)/shard_map/ppermute | solution.py:28
  48.1 1.7 collective-permute-start.8
  49.8 3.2 %collective-permute-done.10.refs_7_.refs_2_ = bf16[128,1024]{1,0:T(8,128)(2,1)S(1)} collective-permute-done((bf16[128,1024]{1,0:T(8,128)(2,1)S(1)}, bf16[128,1024]{1,0:T(8,128)(2,1)S(1)}, u32[]{:S(2)}, u32[]{:S(2)}) %collective-permute-start.10) | collective-permute-done | bytes 262176 | tf_op jit(solution)/shard_map/ppermute | solution.py:28
  53.5 2.9 %collective-permute-done.7.refs_2_ = bf16[128,1024]{1,0:T(8,128)(2,1)S(1)} collective-permute-done((bf16[128,1024]{1,0:T(8,128)(2,1)S(1)}, bf16[128,1024]{1,0:T(8,128)(2,1)S(1)}, u32[]{:S(2)}, u32[]{:S(2)}) %collective-permute-start.7) | collective-permute-done | bytes 262176 | tf_op jit(solution)/shard_map/ppermute | solution.py:24
  57.6 11.2 %shard_map.75 = (bf16[1024,1024]{1,0:T(8,128)(2,1)}, bf16[2048,1024]{1,0:T(8,128)(2,1)}, f32[24,128]{1,0:T(8,128)}) custom-call(bf16[256,1024]{1,0:T(8,128)(2,1)} %copy-done.10, bf16[256,1024]{1,0:T(8,128)(2,1)} %copy-done.17, bf16[128,1024]{1,0:T(8,128)(2,1)} %copy-done.31, bf16[128,1024]{1,0:T(8,128)(2,1)} %copy-done.32, bf16[256,1024]{1,0:T(8,128)(2,1)} %copy-done.18, ...), custom_call_target="tpu_custom_call" | custom-call | tf_op jit(solution)/shard_map/pallas_call | solution.py:226
  73.9 4.7 %collective-permute-done.21 = f32[8,2,128]{2,1,0:T(2,128)S(1)} collective-permute-done((f32[8,2,128]{2,1,0:T(2,128)S(1)}, f32[8,2,128]{2,1,0:T(2,128)S(1)}, u32[]{:S(2)}, u32[]{:S(2)}) %collective-permute-start.21) | collective-permute-done | bytes 8224 | tf_op jit(solution)/shard_map/ppermute | solution.py:28
  78.8 2.9 %collective-permute-start.23 = (f32[16,128]{1,0:T(8,128)S(1)}, f32[16,128]{1,0:T(8,128)S(1)}, u32[]{:S(2)}, u32[]{:S(2)}) collective-permute-start(f32[16,128]{1,0:T(8,128)S(1)} %bitcast.53), channel_id=1, source_target_pairs={{0,64},{16,80},{32,96},{48,112},{64,0},{80,16},{96,32},{112,48},{1... | collective-permute-start | bytes 24584 | tf_op jit(solution)/shard_map/ppermute | solution.py:28
  83.6 2.7 %collective-permute-start.19 = (f32[16,128]{1,0:T(8,128)S(1)}, f32[16,128]{1,0:T(8,128)S(1)}, u32[]{:S(2)}, u32[]{:S(2)}) collective-permute-start(f32[16,128]{1,0:T(8,128)S(1)} %bitcast.57), channel_id=1, source_target_pairs={{0,8},{2,10},{4,12},{6,14},{8,0},{10,2},{12,4},{14,6},{1,9},{3,11}... | collective-permute-start | bytes 24584 | tf_op jit(solution)/shard_map/ppermute | solution.py:24
  90.6 15.4 %shard_map.76 = (bf16[256,1024]{1,0:T(8,128)(2,1)}, bf16[256,1024]{1,0:T(8,128)(2,1)}, bf16[256,1024]{1,0:T(8,128)(2,1)}, bf16[256,1024]{1,0:T(8,128)(2,1)}, bf1...) custom-call(bf16[256,1024]{1,0:T(8,128)(2,1)} %copy-done.1, ...), custom_call_target="tpu_custom_call" | custom-call | tf_op jit(solution)/shard_map/pallas_call | solution.py:319
  107.7 2.9 %collective-permute-start.28 = (bf16[256,1024]{1,0:T(8,128)(2,1)}, bf16[256,1024]{1,0:T(8,128)(2,1)S(1)}, u32[]{:S(2)}, u32[]{:S(2)}) collective-permute-start(bf16[256,1024]{1,0:T(8,128)(2,1)} %get-tuple-element.143), channel_id=1, source_target_pairs={{0,8},{2,10},{4,12},{6,14},{8,0},{10,2},{12,4},{14,6},{1,9},{3,11}... | collective-permute-start | bytes 1572872 | tf_op jit(solution)/shard_map/ppermute | solution.py:24
  111.0 1.9 collective-permute-start.30
  114.5 8.6 %collective-permute-done.27.refs_1_ = bf16[256,1024]{1,0:T(8,128)(2,1)S(1)} collective-permute-done((bf16[256,1024]{1,0:T(8,128)(2,1)}, bf16[256,1024]{1,0:T(8,128)(2,1)S(1)}, u32[]{:S(2)}, u32[]{:S(2)}) %collective-permute-start.27) | collective-permute-done | bytes 524320 | tf_op jit(solution)/shard_map/ppermute | solution.py:24
  123.7 7.0 %collective-permute-done.28.refs_2_ = bf16[256,1024]{1,0:T(8,128)(2,1)S(1)} collective-permute-done((bf16[256,1024]{1,0:T(8,128)(2,1)}, bf16[256,1024]{1,0:T(8,128)(2,1)S(1)}, u32[]{:S(2)}, u32[]{:S(2)}) %collective-permute-start.28) | collective-permute-done | bytes 524320 | tf_op jit(solution)/shard_map/ppermute | solution.py:24
  131.1 2.7 %collective-permute-done.31.refs_6_ = bf16[256,1024]{1,0:T(8,128)(2,1)S(1)} collective-permute-done((bf16[256,1024]{1,0:T(8,128)(2,1)}, bf16[256,1024]{1,0:T(8,128)(2,1)S(1)}, u32[]{:S(2)}, u32[]{:S(2)}) %collective-permute-start.31) | collective-permute-done | bytes 524320 | tf_op jit(solution)/shard_map/ppermute | solution.py:28
  135.4 2.5 %shard_map.78 = (bf16[128,1024]{1,0:T(8,128)(2,1)}, bf16[128,1024]{1,0:T(8,128)(2,1)}) custom-call(bf16[256,1024]{1,0:T(8,128)(2,1)} %get-tuple-element.141.refs_0_, bf16[256,1024]{1,0:T(8,128)(2,1)} %copy-done.11, bf16[256,1024]{1,0:T(8,128)(2,1)} %copy-done.12, bf16[256,1024]{1,0:T(8,128)(2,1)} %copy-done.13, ...), custom_call_target="tpu_custom_call" | custom-call | tf_op jit(solution)/shard_map/pallas_call | solution.py:349
  137.8 1.7 collective-permute-start.33
  140.4 3.1 %shard_map.77 = (f32[128,1024]{1,0:T(8,128)}, f32[128,1024]{1,0:T(8,128)}) custom-call(bf16[256,1024]{1,0:T(8,128)(2,1)} %get-tuple-element.141.refs_0_, bf16[256,1024]{1,0:T(8,128)(2,1)} %copy-done.11, bf16[256,1024]{1,0:T(8,128)(2,1)} %copy-done.12, bf16[256,1024]{1,0:T(8,128)(2,1)} %copy-done.13, bf16[256,1024]{1,0:T(8,128)(2,1)} %get-tuple-element.145.refs_4_, ...), custom_call_target="tpu_custom_call" | custom-call | tf_op jit(solution)/shard_map/pallas_call | solution.py:379
  143.5 2.3 %collective-permute-done.33.q_got = bf16[128,1024]{1,0:T(8,128)(2,1)S(1)} collective-permute-done((bf16[128,1024]{1,0:T(8,128)(2,1)}, bf16[128,1024]{1,0:T(8,128)(2,1)S(1)}, u32[]{:S(2)}, u32[]{:S(2)}) %collective-permute-start.33) | collective-permute-done | bytes 262176 | tf_op jit(solution)/shard_map/ppermute | solution.py:24
  145.8 2.5 %collective-permute-done.34.k_got = bf16[128,1024]{1,0:T(8,128)(2,1)S(1)} collective-permute-done((bf16[128,1024]{1,0:T(8,128)(2,1)}, bf16[128,1024]{1,0:T(8,128)(2,1)S(1)}, u32[]{:S(2)}, u32[]{:S(2)}) %collective-permute-start.34) | collective-permute-done | bytes 262176 | tf_op jit(solution)/shard_map/ppermute | solution.py:28
  149.0 2.7 %shard_map.79.refs_0_ = bf16[256,1024]{1,0:T(8,128)(2,1)} custom-call(f32[128,1024]{1,0:T(8,128)} %get-tuple-element.153.q_keep, bf16[128,1024]{1,0:T(8,128)(2,1)} %copy-done.33, f32[128,1024]{1,0:T(8,128)} %get-tuple-element.155.k_keep, bf16[128,1024]{1,0:T(8,128)(2,1)} %copy-done.34, bf16[128,1024]{1,0:T(8,128)(2,1)} %get-tuple-element.157.q_raw, ...), custom_call_target="tpu_custom_call" | custom-call | tf_op jit(solution)/shard_map/pallas_call | solution.py:398
  153.1 8.1 %collective-permute-done.36.refs_2_ = bf16[256,1024]{1,0:T(8,128)(2,1)S(1)} collective-permute-done((bf16[256,1024]{1,0:T(8,128)(2,1)}, bf16[256,1024]{1,0:T(8,128)(2,1)S(1)}, u32[]{:S(2)}, u32[]{:S(2)}) %collective-permute-start.36) | collective-permute-done | bytes 524320 | tf_op jit(solution)/shard_map/ppermute | solution.py:24
  161.2 1.9 collective-permute-done.37.refs_3_
  163.9 5.4 %shard_map.80 = bf16[1024,1024]{1,0:T(8,128)(2,1)} custom-call(bf16[256,1024]{1,0:T(8,128)(2,1)} %shard_map.79.refs_0_, bf16[256,1024]{1,0:T(8,128)(2,1)} %copy-done.29, bf16[256,1024]{1,0:T(8,128)(2,1)} %copy-done.26, bf16[256,1024]{1,0:T(8,128)(2,1)} %copy-done.30, bf16[4,1024,256]{2,1,0:T(8,128)(2,1)} %bitcast.49, bf16[1024,256]{1,0:T(8,128)(2,1)} %copy-done.27, ...), custom_call_target="tpu_custom_call" | custom-call | tf_op jit(solution)/shard_map/pallas_call | solution.py:431
  169.2 42.7 %all_to_all.9 = bf16[32,32,1024]{2,1,0:T(8,128)(2,1)S(1)} all-to-all(bf16[32,32,1024]{2,1,0:T(8,128)(2,1)} %bitcast.51), channel_id=1, replica_groups={{0,4,8,12,16,20,24,28,32,36,40,44,48,52,56,60,64,68,72,76,80,84,88,92,9..., dimensions={0} | all-to-all | bytes 4194304 | tf_op jit(solution)/shard_map/all_to_all | solution.py:557
  (182 shorter events, 37.8 us)
Async XLA Ops:
  7.4 13.5 %collective-permute-start.1 = (bf16[128,1024]{1,0:T(8,128)(2,1)}, bf16[128,1024]{1,0:T(8,128)(2,1)S(1)}, u32[]{:S(2)}, u32[]{:S(2)}) collective-permute-start(bf16[128,1024]{1,0:T(8,128)(2,1)} %get-tuple-element.85.q_unit.refs_8_), channel_id=1, source_target_pairs={{0,2},{2,0},{4,6},{6,4},{8,10},{10,8},{12,14},{14,12},{1,3},{3,1},... | collective-permute-start | bytes 786440 | tf_op jit(solution)/shard_map/ppermute | solution.py:24
  9.4 15.5 %collective-permute-start = (bf16[128,1024]{1,0:T(8,128)(2,1)}, bf16[128,1024]{1,0:T(8,128)(2,1)}, u32[]{:S(2)}, u32[]{:S(2)}) collective-permute-start(bf16[128,1024]{1,0:T(8,128)(2,1)} %get-tuple-element.84.k_unit), channel_id=1, source_target_pairs={{0,16},{16,0},{32,48},{48,32},{64,80},{80,64},{96,112},{112,96},{1... | collective-permute-start | bytes 786440 | tf_op jit(solution)/shard_map/ppermute | solution.py:28
  26.0 14.1 %collective-permute-start.2 = (bf16[256,1024]{1,0:T(8,128)(2,1)S(1)}, bf16[256,1024]{1,0:T(8,128)(2,1)S(1)}, u32[]{:S(2)}, u32[]{:S(2)}) collective-permute-start(bf16[256,1024]{1,0:T(8,128)(2,1)S(1)} %get-tuple-element.95.refs_5_.refs_0_), channel_id=1, source_target_pairs={{0,32},{16,48},{32,64},{48,80},{64,96},{80,112},{96,0},{112,16},{1... | collective-permute-start | bytes 1572872 | tf_op jit(solution)/shard_map/ppermute | solution.py:28
  27.6 13.8 %collective-permute-start.3 = (bf16[256,1024]{1,0:T(8,128)(2,1)S(1)}, bf16[256,1024]{1,0:T(8,128)(2,1)S(1)}, u32[]{:S(2)}, u32[]{:S(2)}) collective-permute-start(bf16[256,1024]{1,0:T(8,128)(2,1)S(1)} %get-tuple-element.103.refs_0_), channel_id=1, source_target_pairs={{0,4},{2,6},{4,8},{6,10},{8,12},{10,14},{12,0},{14,2},{1,5},{3,7},... | collective-permute-start | bytes 1572872 | tf_op jit(solution)/shard_map/ppermute | solution.py:24
  29.1 12.2 %collective-permute-start.4 = (bf16[256,1024]{1,0:T(8,128)(2,1)S(1)}, bf16[256,1024]{1,0:T(8,128)(2,1)S(1)}, u32[]{:S(2)}, u32[]{:S(2)}) collective-permute-start(bf16[256,1024]{1,0:T(8,128)(2,1)S(1)} %get-tuple-element.95.refs_5_.refs_0_), channel_id=1, source_target_pairs={{0,96},{16,112},{32,0},{48,16},{64,32},{80,48},{96,64},{112,80},{1... | collective-permute-start | bytes 1572872 | tf_op jit(solution)/shard_map/ppermute | solution.py:28
  30.9 12.0 %collective-permute-start.5 = (bf16[256,1024]{1,0:T(8,128)(2,1)S(1)}, bf16[256,1024]{1,0:T(8,128)(2,1)S(1)}, u32[]{:S(2)}, u32[]{:S(2)}) collective-permute-start(bf16[256,1024]{1,0:T(8,128)(2,1)S(1)} %get-tuple-element.103.refs_0_), channel_id=1, source_target_pairs={{0,12},{2,14},{4,0},{6,2},{8,4},{10,6},{12,8},{14,10},{1,13},{3,15... | collective-permute-start | bytes 1572872 | tf_op jit(solution)/shard_map/ppermute | solution.py:24
  32.6 10.3 %collective-permute-start.6 = (bf16[256,1024]{1,0:T(8,128)(2,1)S(1)}, bf16[256,1024]{1,0:T(8,128)(2,1)S(1)}, u32[]{:S(2)}, u32[]{:S(2)}) collective-permute-start(bf16[256,1024]{1,0:T(8,128)(2,1)S(1)} %get-tuple-element.95.refs_5_.refs_0_), channel_id=1, source_target_pairs={{0,1},{1,0},{2,3},{3,2},{4,5},{5,4},{6,7},{7,6},{8,9},{9,8},{10,11... | collective-permute-start | bytes 1572872 | tf_op jit(solution)/shard_map/ppermute | solution.py:42
  43.0 10.0 %collective-permute-start.10 = (bf16[128,1024]{1,0:T(8,128)(2,1)S(1)}, bf16[128,1024]{1,0:T(8,128)(2,1)S(1)}, u32[]{:S(2)}, u32[]{:S(2)}) collective-permute-start(bf16[128,1024]{1,0:T(8,128)(2,1)S(1)} %slice.29), channel_id=1, source_target_pairs={{0,32},{16,48},{32,64},{48,80},{64,96},{80,112},{96,0},{112,16},{1... | collective-permute-start | bytes 786440 | tf_op jit(solution)/shard_map/ppermute | solution.py:28
  43.3 9.6 %collective-permute-start.12 = (bf16[128,1024]{1,0:T(8,128)(2,1)S(1)}, bf16[128,1024]{1,0:T(8,128)(2,1)S(1)}, u32[]{:S(2)}, u32[]{:S(2)}) collective-permute-start(bf16[128,1024]{1,0:T(8,128)(2,1)S(1)} %slice.30), channel_id=1, source_target_pairs={{0,96},{16,112},{32,0},{48,16},{64,32},{80,48},{96,64},{112,80},{1... | collective-permute-start | bytes 786440 | tf_op jit(solution)/shard_map/ppermute | solution.py:28
  46.4 10.2 %collective-permute-start.14 = (bf16[256,1024]{1,0:T(8,128)(2,1)S(1)}, bf16[256,1024]{1,0:T(8,128)(2,1)S(1)}, u32[]{:S(2)}, u32[]{:S(2)}) collective-permute-start(bf16[256,1024]{1,0:T(8,128)(2,1)S(1)} %collective-permute-done.4.refs_9_.refs_4_), channel_id=1, source_target_pairs={{0,1},{1,0},{2,3},{3,2},{4,5},{5,4},{6,7},{7,6},{8,9},{9,8},{10,11... | collective-permute-start | bytes 1572872 | tf_op jit(solution)/shard_map/ppermute | solution.py:42
  46.4 10.0 %collective-permute-start.7 = (bf16[128,1024]{1,0:T(8,128)(2,1)S(1)}, bf16[128,1024]{1,0:T(8,128)(2,1)S(1)}, u32[]{:S(2)}, u32[]{:S(2)}) collective-permute-start(bf16[128,1024]{1,0:T(8,128)(2,1)S(1)} %slice.27), channel_id=1, source_target_pairs={{0,4},{2,6},{4,8},{6,10},{8,12},{10,14},{12,0},{14,2},{1,5},{3,7},... | collective-permute-start | bytes 786440 | tf_op jit(solution)/shard_map/ppermute | solution.py:24
  48.1 8.5 %collective-permute-start.8 = (bf16[128,1024]{1,0:T(8,128)(2,1)S(1)}, bf16[128,1024]{1,0:T(8,128)(2,1)S(1)}, u32[]{:S(2)}, u32[]{:S(2)}) collective-permute-start(bf16[128,1024]{1,0:T(8,128)(2,1)S(1)} %slice.28), channel_id=1, source_target_pairs={{0,12},{2,14},{4,0},{6,2},{8,4},{10,6},{12,8},{14,10},{1,13},{3,15... | collective-permute-start | bytes 786440 | tf_op jit(solution)/shard_map/ppermute | solution.py:24
  56.6 13.9 %collective-permute-start.15 = (bf16[1024,256]{1,0:T(8,128)(2,1)}, bf16[1024,256]{1,0:T(8,128)(2,1)S(1)}, u32[]{:S(2)}, u32[]{:S(2)}) collective-permute-start(bf16[1024,256]{1,0:T(8,128)(2,1)} %get-tuple-element.117), channel_id=1, source_target_pairs={{0,2},{2,0},{4,6},{6,4},{8,10},{10,8},{12,14},{14,12},{1,3},{3,1},... | collective-permute-start | bytes 1572872 | tf_op jit(solution)/shard_map/ppermute | solution.py:24
  71.9 18.3 %collective-permute-start.26 = (bf16[2048,1024]{1,0:T(8,128)(2,1)}, bf16[2048,1024]{1,0:T(8,128)(2,1)}, u32[]{:S(2)}, u32[]{:S(2)}) collective-permute-start(bf16[2048,1024]{1,0:T(8,128)(2,1)} %get-tuple-element.123.refs_11_), channel_id=1, source_target_pairs={{0,1},{1,0},{2,3},{3,2},{4,5},{5,4},{6,7},{7,6},{8,9},{9,8},{10,11... | collective-permute-start | bytes 12582920 | tf_op jit(solution)/shard_map/ppermute | solution.py:42
  73.4 5.2 %collective-permute-start.21 = (f32[8,2,128]{2,1,0:T(2,128)S(1)}, f32[8,2,128]{2,1,0:T(2,128)S(1)}, u32[]{:S(2)}, u32[]{:S(2)}) collective-permute-start(f32[8,2,128]{2,1,0:T(2,128)S(1)} %bitcast.60), channel_id=1, source_target_pairs={{0,16},{16,0},{32,48},{48,32},{64,80},{80,64},{96,112},{112,96},{1... | collective-permute-start | bytes 24584 | tf_op jit(solution)/shard_map/ppermute | solution.py:28
  73.4 8.6 %collective-permute-start.17 = (f32[8,2,128]{2,1,0:T(2,128)S(1)}, f32[8,2,128]{2,1,0:T(2,128)S(1)}, u32[]{:S(2)}, u32[]{:S(2)}) collective-permute-start(f32[8,2,128]{2,1,0:T(2,128)S(1)} %bitcast.62), channel_id=1, source_target_pairs={{0,2},{2,0},{4,6},{6,4},{8,10},{10,8},{12,14},{14,12},{1,3},{3,1},... | collective-permute-start | bytes 24584 | tf_op jit(solution)/shard_map/ppermute | solution.py:24
  78.8 7.5 %collective-permute-start.23 = (f32[16,128]{1,0:T(8,128)S(1)}, f32[16,128]{1,0:T(8,128)S(1)}, u32[]{:S(2)}, u32[]{:S(2)}) collective-permute-start(f32[16,128]{1,0:T(8,128)S(1)} %bitcast.53), channel_id=1, source_target_pairs={{0,64},{16,80},{32,96},{48,112},{64,0},{80,16},{96,32},{112,48},{1... | collective-permute-start | bytes 24584 | tf_op jit(solution)/shard_map/ppermute | solution.py:28
  81.7 5.8 %collective-permute-start.24 = (f32[16,128]{1,0:T(8,128)S(1)}, f32[16,128]{1,0:T(8,128)S(1)}, u32[]{:S(2)}, u32[]{:S(2)}) collective-permute-start(f32[16,128]{1,0:T(8,128)S(1)} %bitcast.54), channel_id=1, source_target_pairs={{0,96},{16,112},{32,0},{48,16},{64,32},{80,48},{96,64},{112,80},{1... | collective-permute-start | bytes 24584 | tf_op jit(solution)/shard_map/ppermute | solution.py:28
  82.1 5.4 %collective-permute-start.18 = (f32[16,128]{1,0:T(8,128)S(1)}, f32[16,128]{1,0:T(8,128)S(1)}, u32[]{:S(2)}, u32[]{:S(2)}) collective-permute-start(f32[16,128]{1,0:T(8,128)S(1)} %bitcast.56), channel_id=1, source_target_pairs={{0,4},{2,6},{4,8},{6,10},{8,12},{10,14},{12,0},{14,2},{1,5},{3,7},... | collective-permute-start | bytes 24584 | tf_op jit(solution)/shard_map/ppermute | solution.py:24
  90.0 16.0 %collective-permute-start.25 = (bf16[1024,256]{1,0:T(8,128)(2,1)S(1)}, bf16[1024,256]{1,0:T(8,128)(2,1)S(1)}, u32[]{:S(2)}, u32[]{:S(2)}) collective-permute-start(bf16[1024,256]{1,0:T(8,128)(2,1)S(1)} %get-tuple-element.121), channel_id=1, source_target_pairs={{0,2},{2,0},{4,6},{6,4},{8,10},{10,8},{12,14},{14,12},{1,3},{3,1},... | collective-permute-start | bytes 1572872 | tf_op jit(solution)/shard_map/ppermute | solution.py:24
  106.8 16.3 %collective-permute-start.27 = (bf16[256,1024]{1,0:T(8,128)(2,1)}, bf16[256,1024]{1,0:T(8,128)(2,1)S(1)}, u32[]{:S(2)}, u32[]{:S(2)}) collective-permute-start(bf16[256,1024]{1,0:T(8,128)(2,1)} %get-tuple-element.142), channel_id=1, source_target_pairs={{0,4},{2,6},{4,8},{6,10},{8,12},{10,14},{12,0},{14,2},{1,5},{3,7},... | collective-permute-start | bytes 1572872 | tf_op jit(solution)/shard_map/ppermute | solution.py:24
  107.7 23.0 %collective-permute-start.28 = (bf16[256,1024]{1,0:T(8,128)(2,1)}, bf16[256,1024]{1,0:T(8,128)(2,1)S(1)}, u32[]{:S(2)}, u32[]{:S(2)}) collective-permute-start(bf16[256,1024]{1,0:T(8,128)(2,1)} %get-tuple-element.143), channel_id=1, source_target_pairs={{0,8},{2,10},{4,12},{6,14},{8,0},{10,2},{12,4},{14,6},{1,9},{3,11}... | collective-permute-start | bytes 1572872 | tf_op jit(solution)/shard_map/ppermute | solution.py:24
  110.6 20.5 %collective-permute-start.29 = (bf16[256,1024]{1,0:T(8,128)(2,1)}, bf16[256,1024]{1,0:T(8,128)(2,1)S(1)}, u32[]{:S(2)}, u32[]{:S(2)}) collective-permute-start(bf16[256,1024]{1,0:T(8,128)(2,1)} %get-tuple-element.144), channel_id=1, source_target_pairs={{0,12},{2,14},{4,0},{6,2},{8,4},{10,6},{12,8},{14,10},{1,13},{3,15... | collective-permute-start | bytes 1572872 | tf_op jit(solution)/shard_map/ppermute | solution.py:24
  111.0 20.1 %collective-permute-start.30 = (bf16[256,1024]{1,0:T(8,128)(2,1)}, bf16[256,1024]{1,0:T(8,128)(2,1)S(1)}, u32[]{:S(2)}, u32[]{:S(2)}) collective-permute-start(bf16[256,1024]{1,0:T(8,128)(2,1)} %get-tuple-element.146), channel_id=1, source_target_pairs={{0,32},{16,48},{32,64},{48,80},{64,96},{80,112},{96,0},{112,16},{1... | collective-permute-start | bytes 1572872 | tf_op jit(solution)/shard_map/ppermute | solution.py:28
  112.9 20.9 %collective-permute-start.31 = (bf16[256,1024]{1,0:T(8,128)(2,1)}, bf16[256,1024]{1,0:T(8,128)(2,1)S(1)}, u32[]{:S(2)}, u32[]{:S(2)}) collective-permute-start(bf16[256,1024]{1,0:T(8,128)(2,1)} %get-tuple-element.147), channel_id=1, source_target_pairs={{0,64},{16,80},{32,96},{48,112},{64,0},{80,16},{96,32},{112,48},{1... | collective-permute-start | bytes 1572872 | tf_op jit(solution)/shard_map/ppermute | solution.py:28
  123.1 11.2 %collective-permute-start.32 = (bf16[256,1024]{1,0:T(8,128)(2,1)}, bf16[256,1024]{1,0:T(8,128)(2,1)S(1)}, u32[]{:S(2)}, u32[]{:S(2)}) collective-permute-start(bf16[256,1024]{1,0:T(8,128)(2,1)} %get-tuple-element.148), channel_id=1, source_target_pairs={{0,96},{16,112},{32,0},{48,16},{64,32},{80,48},{96,64},{112,80},{1... | collective-permute-start | bytes 1572872 | tf_op jit(solution)/shard_map/ppermute | solution.py:28
  137.8 8.0 %collective-permute-start.33 = (bf16[128,1024]{1,0:T(8,128)(2,1)}, bf16[128,1024]{1,0:T(8,128)(2,1)S(1)}, u32[]{:S(2)}, u32[]{:S(2)}) collective-permute-start(bf16[128,1024]{1,0:T(8,128)(2,1)} %get-tuple-element.154), channel_id=1, source_target_pairs={{0,2},{2,0},{4,6},{6,4},{8,10},{10,8},{12,14},{14,12},{1,3},{3,1},... | collective-permute-start | bytes 786440 | tf_op jit(solution)/shard_map/ppermute | solution.py:24
  139.6 8.7 %collective-permute-start.34 = (bf16[128,1024]{1,0:T(8,128)(2,1)}, bf16[128,1024]{1,0:T(8,128)(2,1)S(1)}, u32[]{:S(2)}, u32[]{:S(2)}) collective-permute-start(bf16[128,1024]{1,0:T(8,128)(2,1)} %get-tuple-element.156), channel_id=1, source_target_pairs={{0,16},{16,0},{32,48},{48,32},{64,80},{80,64},{96,112},{112,96},{1... | collective-permute-start | bytes 786440 | tf_op jit(solution)/shard_map/ppermute | solution.py:28
  151.7 9.4 %collective-permute-start.36 = (bf16[256,1024]{1,0:T(8,128)(2,1)}, bf16[256,1024]{1,0:T(8,128)(2,1)S(1)}, u32[]{:S(2)}, u32[]{:S(2)}) collective-permute-start(bf16[256,1024]{1,0:T(8,128)(2,1)} %shard_map.79.refs_0_), channel_id=1, source_target_pairs={{0,2},{2,0},{4,6},{6,4},{8,10},{10,8},{12,14},{14,12},{1,3},{3,1},... | collective-permute-start | bytes 1572872 | tf_op jit(solution)/shard_map/ppermute | solution.py:24
  152.5 8.7 %collective-permute-start.38 = (bf16[1024,256]{1,0:T(8,128)(2,1)S(1)}, bf16[1024,256]{1,0:T(8,128)(2,1)S(1)}, u32[]{:S(2)}, u32[]{:S(2)}) collective-permute-start(bf16[1024,256]{1,0:T(8,128)(2,1)S(1)} %copy-done.24), channel_id=1, source_target_pairs={{0,1},{1,0},{2,3},{3,2},{4,5},{5,4},{6,7},{7,6},{8,9},{9,8},{10,11... | collective-permute-start | bytes 1572872 | tf_op jit(solution)/shard_map/ppermute | solution.py:42
  152.5 8.7 %collective-permute-start.39 = (bf16[1024,256]{1,0:T(8,128)(2,1)S(1)}, bf16[1024,256]{1,0:T(8,128)(2,1)S(1)}, u32[]{:S(2)}, u32[]{:S(2)}) collective-permute-start(bf16[1024,256]{1,0:T(8,128)(2,1)S(1)} %copy-done.46), channel_id=1, source_target_pairs={{0,1},{1,0},{2,3},{3,2},{4,5},{5,4},{6,7},{7,6},{8,9},{9,8},{10,11... | collective-permute-start | bytes 1572872 | tf_op jit(solution)/shard_map/ppermute | solution.py:42
  153.0 8.2 %collective-permute-start.35 = (bf16[256,1024]{1,0:T(8,128)(2,1)}, bf16[256,1024]{1,0:T(8,128)(2,1)S(1)}, u32[]{:S(2)}, u32[]{:S(2)}) collective-permute-start(bf16[256,1024]{1,0:T(8,128)(2,1)} %shard_map.79.refs_0_), channel_id=1, source_target_pairs={{0,1},{1,0},{2,3},{3,2},{4,5},{5,4},{6,7},{7,6},{8,9},{9,8},{10,11... | collective-permute-start | bytes 1572872 | tf_op jit(solution)/shard_map/ppermute | solution.py:42
  (56 other events, 368.4 us)

commit v2 on v1

--- a/solution.py
+++ b/solution.py
@@ -73,42 +73,45 @@
     return values * scale, scale
 
 
-def project_body(hq, hk, proj, q_unit, k_unit, q_raw, k_raw, hid, acc):
-    step = pl.program_id(0)
-    hid[:DOCS, :] = hq[...]
-    hid[DOCS:, :] = hk[...]
-    part = dot(hid[...], proj[...])
-
-    @pl.when(step == 0)
-    def _():
-        acc[...] = part
-
-    @pl.when(step > 0)
-    def _():
-        acc[...] += part
-
-    @pl.when(step == pl.num_programs(0) - 1)
-    def _():
-        for raw_ref, unit_ref, start in ((q_raw, q_unit, 0), (k_raw, k_unit, DOCS)):
-            raw = acc[start : start + DOCS, :].astype(BF)
-            raw_ref[...] = raw
-            unit_ref[...] = unit_of(raw)[0].astype(BF)
+def project_body(hq, hk, proj, q_unit, k_unit, q_raw, k_raw, hid, proj_s, acc, sems):
+    depth = 512
+    loads = [
+        pltpu.make_async_copy(hq, hid.at[pl.ds(0, DOCS)], sems.at[0]),
+        pltpu.make_async_copy(hk, hid.at[pl.ds(DOCS, DOCS)], sems.at[1]),
+    ]
+    for c in range(HID // depth):
+        rows = pl.ds(c * depth, depth)
+        loads.append(pltpu.make_async_copy(proj.at[rows], proj_s.at[rows], sems.at[2 + c]))
+    for load in loads:
+        load.start()
+    loads[0].wait()
+    loads[1].wait()
+    for c in range(HID // depth):
+        loads[2 + c].wait()
+        chunk = slice(c * depth, (c + 1) * depth)
+        part = dot(hid[:, chunk], proj_s[chunk, :])
+        if c == 0:
+            acc[...] = part
+        else:
+            acc[...] += part
+    for raw_ref, unit_ref, start in ((k_raw, k_unit, DOCS), (q_raw, q_unit, 0)):
+        raw = acc[start : start + DOCS, :].astype(BF)
+        raw_ref[...] = raw
+        unit_ref[...] = unit_of(raw)[0].astype(BF)
 
 
 def project(hid_query, hid_key, projection):
-    depth = 1024
-    whole = pl.BlockSpec((DOCS, EMB), lambda i: (0, 0))
     return pl.pallas_call(
         project_body,
-        grid=(HID // depth,),
-        in_specs=[
-            pl.BlockSpec((DOCS, depth), lambda i: (0, i)),
-            pl.BlockSpec((DOCS, depth), lambda i: (0, i)),
-            pl.BlockSpec((depth, EMB), lambda i: (i, 0)),
+        in_specs=[ANY] * 3,
+        out_specs=[VMEM] * 4,
+        out_shape=[sds((DOCS, EMB), BF)] * 4,
+        scratch_shapes=[
+            pltpu.VMEM((2 * DOCS, HID), BF),
+            pltpu.VMEM((HID, EMB), BF),
+            pltpu.VMEM((2 * DOCS, EMB), F32),
+            pltpu.SemaphoreType.DMA((2 + HID // 512,)),
         ],
-        out_specs=[whole] * 4,
-        out_shape=[sds((DOCS, EMB), BF)] * 4,
-        scratch_shapes=[pltpu.VMEM((2 * DOCS, depth), BF), pltpu.VMEM((2 * DOCS, EMB), F32)],
         compiler_params=params(),
     )(hid_query, hid_key, projection)
 
@@ -521,9 +524,8 @@
     q_own, k_oth = blocks[:5], blocks[5:]
     h_flip = move_query(h_flip, 0, 1)
     e_own, mix, sums = scores(q_own, k_own, k_oth, mask, pos_rows)
-    sums, mix, h_flip = lax.optimization_barrier((sums, mix, h_flip))
     far = swap(sums)
-    far, mix = lax.optimization_barrier((far, mix))
+    far, mix, h_flip = lax.optimization_barrier((far, mix, h_flip))
     mix_far = swap(mix)
     row_part = jnp.concatenate([sums[:8], far[:8]], axis=0).reshape(8, 2, DOCS)
     col_part = sums[8:] + jnp.concatenate([far[16:], far[8:16]], axis=0)

time: 214 us -> 211 us (0.986)
  waiting for transfers between devices: 65.1 us -> 61.8 us
  starting transfers between devices: 40.5 us -> 42.9 us
    ppermute x16, waiting for transfers between devices: 36.3 us -> 33.6 us  [move_query(): return lax.ppermute(value, 'col', ring_pair(step, flip))]
where the time goes in v2:
time: 211 us; the launch traced here: 210 us
  waiting for transfers between devices  61.8 us (29%)
  Pallas kernels  48.2 us (23%)
  starting transfers between devices  42.9 us (20%)
  blocking collectives  42.5 us (20%)
  local copies, waits for them, and re-layouts  9.57 us (5%)
  other arithmetic  3.88 us (2%)
    all_to_all x1, blocking collectives, local(): lax.all_to_all(out, ('row', 'col'), 0, 0, tiled=True, axis_index_groups=P...  42.5 us
    ppermute x16, waiting for transfers between devices, move_query(): return lax.ppermute(value, 'col', ring_pair(step, flip))  33.6 us
    ppermute x13, waiting for transfers between devices, move_key(): return lax.ppermute(value, 'row', ring_pair(step, flip))  25 us
    ppermute x16, starting transfers between devices, move_query(): return lax.ppermute(value, 'col', ring_pair(step, flip))  22.3 us
    ppermute x13, starting transfers between devices, move_key(): return lax.ppermute(value, 'row', ring_pair(step, flip))  19.4 us
    pallas_call x1, Pallas kernels, grads(): pl.pallas_call(grads_body, in_specs=[ANY] * 13 + [VMEM] * 8, out_specs=[A...  15.5 us
    pallas_call x1, Pallas kernels, scores(): pl.pallas_call(scores_body, in_specs=[ANY] * 15 + [SMEM, VMEM], out_specs...  11.3 us
    unnamed x98, local copies, waits for them, and re-layouts  5.98 us
  transfers between devices with their start and end apart: 40, of which 22 were waited for; matrix products, arithmetic and copies ran while one was open for 3% of the time, Pallas kernels for 15%

profile of v2, /device:TPU:0, one launch (start us, length us, event | category | flops | bytes accessed | tf_op | source)
XLA Modules:
  0.0 210.4 jit_solution(7525357509370257776)
XLA Ops:
  0.0 5.8 %shard_map.73 = (bf16[128,1024]{1,0:T(8,128)(2,1)}, bf16[128,1024]{1,0:T(8,128)(2,1)}, bf16[128,1024]{1,0:T(8,128)(2,1)}, bf16[128,1024]{1,0:T(8,128)(2,1)}) custom-call(bf16[128,4096]{1,0:T(8,128)(2,1)} %hq.1, bf16[128,4096]{1,0:T(8,128)(2,1)} %hk.1, bf16[4096,1024]{1,0:T(8,128)(2,1)} %proj.1), custom_call_target="tpu_custom_call" | custom-call | tf_op jit(solution)/shard_map/pallas_call | solution.py:104
  5.8 2.1 collective-permute-start.1
  7.9 3.6 %collective-permute-start = (bf16[128,1024]{1,0:T(8,128)(2,1)}, bf16[128,1024]{1,0:T(8,128)(2,1)}, u32[]{:S(2)}, u32[]{:S(2)}) collective-permute-start(bf16[128,1024]{1,0:T(8,128)(2,1)} %get-tuple-element.82.k_unit), channel_id=1, source_target_pairs={{0,16},{16,0},{32,48},{48,32},{64,80},{80,64},{96,112},{112,96},{1... | collective-permute-start | bytes 786440 | tf_op jit(solution)/shard_map/ppermute | solution.py:28
  16.1 2.1 %shard_map.74 = (bf16[128,1024]{1,0:T(8,128)(2,1)}, bf16[128,1024]{1,0:T(8,128)(2,1)}, f32[8,128]{1,0:T(8,128)}) custom-call(bf16[128,1024]{1,0:T(8,128)(2,1)} %get-tuple-element.83.q_unit.refs_8_, bf16[128,1024]{1,0:T(8,128)(2,1)} %get-tuple-element.82.k_unit, s32[128,1]{1,0:T(8,128)} %copy.16.pos), custom_call_target="tpu_custom_call" | custom-call | tf_op jit(solution)/shard_map/pallas_call | solution.py:144
  19.3 4.1 %collective-permute-done = bf16[128,1024]{1,0:T(8,128)(2,1)} collective-permute-done((bf16[128,1024]{1,0:T(8,128)(2,1)}, bf16[128,1024]{1,0:T(8,128)(2,1)}, u32[]{:S(2)}, u32[]{:S(2)}) %collective-permute-start) | collective-permute-done | bytes 262176 | tf_op jit(solution)/shard_map/ppermute | solution.py:28
  27.6 1.7 collective-permute-start.4
  29.4 1.7 collective-permute-start.5
  31.0 7.5 %collective-permute-done.2.refs_6_.refs_1_ = bf16[256,1024]{1,0:T(8,128)(2,1)S(1)} collective-permute-done((bf16[256,1024]{1,0:T(8,128)(2,1)S(1)}, bf16[256,1024]{1,0:T(8,128)(2,1)S(1)}, u32[]{:S(2)}, u32[]{:S(2)}) %collective-permute-start.2) | collective-permute-done | bytes 524320 | tf_op jit(solution)/shard_map/ppermute | solution.py:28
  41.8 3.0 %collective-permute-start.12 = (bf16[128,1024]{1,0:T(8,128)(2,1)S(1)}, bf16[128,1024]{1,0:T(8,128)(2,1)S(1)}, u32[]{:S(2)}, u32[]{:S(2)}) collective-permute-start(bf16[128,1024]{1,0:T(8,128)(2,1)S(1)} %slice.30), channel_id=1, source_target_pairs={{0,96},{16,112},{32,0},{48,16},{64,32},{80,48},{96,64},{112,80},{1... | collective-permute-start | bytes 786440 | tf_op jit(solution)/shard_map/ppermute | solution.py:28
  44.9 1.7 collective-permute-start.7
  46.5 1.7 collective-permute-start.8
  48.3 3.2 %collective-permute-done.10.refs_7_.refs_2_ = bf16[128,1024]{1,0:T(8,128)(2,1)S(1)} collective-permute-done((bf16[128,1024]{1,0:T(8,128)(2,1)S(1)}, bf16[128,1024]{1,0:T(8,128)(2,1)S(1)}, u32[]{:S(2)}, u32[]{:S(2)}) %collective-permute-start.10) | collective-permute-done | bytes 262176 | tf_op jit(solution)/shard_map/ppermute | solution.py:28
  51.9 2.9 %collective-permute-done.7.refs_2_ = bf16[128,1024]{1,0:T(8,128)(2,1)S(1)} collective-permute-done((bf16[128,1024]{1,0:T(8,128)(2,1)S(1)}, bf16[128,1024]{1,0:T(8,128)(2,1)S(1)}, u32[]{:S(2)}, u32[]{:S(2)}) %collective-permute-start.7) | collective-permute-done | bytes 262176 | tf_op jit(solution)/shard_map/ppermute | solution.py:24
  56.1 11.3 %shard_map.75 = (bf16[1024,1024]{1,0:T(8,128)(2,1)}, bf16[2048,1024]{1,0:T(8,128)(2,1)}, f32[24,128]{1,0:T(8,128)}) custom-call(bf16[256,1024]{1,0:T(8,128)(2,1)} %copy-done.10, bf16[256,1024]{1,0:T(8,128)(2,1)} %copy-done.17, bf16[128,1024]{1,0:T(8,128)(2,1)} %copy-done.31, bf16[128,1024]{1,0:T(8,128)(2,1)} %copy-done.32, bf16[256,1024]{1,0:T(8,128)(2,1)} %copy-done.18, ...), custom_call_target="tpu_custom_call" | custom-call | tf_op jit(solution)/shard_map/pallas_call | solution.py:229
  71.9 3.7 %collective-permute-done.21 = f32[8,2,128]{2,1,0:T(2,128)S(1)} collective-permute-done((f32[8,2,128]{2,1,0:T(2,128)S(1)}, f32[8,2,128]{2,1,0:T(2,128)S(1)}, u32[]{:S(2)}, u32[]{:S(2)}) %collective-permute-start.21) | collective-permute-done | bytes 8224 | tf_op jit(solution)/shard_map/ppermute | solution.py:28
  75.7 2.8 %collective-permute-start.23 = (f32[16,128]{1,0:T(8,128)S(1)}, f32[16,128]{1,0:T(8,128)S(1)}, u32[]{:S(2)}, u32[]{:S(2)}) collective-permute-start(f32[16,128]{1,0:T(8,128)S(1)} %bitcast.53), channel_id=1, source_target_pairs={{0,64},{16,80},{32,96},{48,112},{64,0},{80,16},{96,32},{112,48},{1... | collective-permute-start | bytes 24584 | tf_op jit(solution)/shard_map/ppermute | solution.py:28
  80.6 2.8 %collective-permute-start.19 = (f32[16,128]{1,0:T(8,128)S(1)}, f32[16,128]{1,0:T(8,128)S(1)}, u32[]{:S(2)}, u32[]{:S(2)}) collective-permute-start(f32[16,128]{1,0:T(8,128)S(1)} %bitcast.57), channel_id=1, source_target_pairs={{0,8},{2,10},{4,12},{6,14},{8,0},{10,2},{12,4},{14,6},{1,9},{3,11}... | collective-permute-start | bytes 24584 | tf_op jit(solution)/shard_map/ppermute | solution.py:24
  88.5 15.5 %shard_map.76 = (bf16[256,1024]{1,0:T(8,128)(2,1)}, bf16[256,1024]{1,0:T(8,128)(2,1)}, bf16[256,1024]{1,0:T(8,128)(2,1)}, bf16[256,1024]{1,0:T(8,128)(2,1)}, bf1...) custom-call(bf16[256,1024]{1,0:T(8,128)(2,1)} %copy-done.1, ...), custom_call_target="tpu_custom_call" | custom-call | tf_op jit(solution)/shard_map/pallas_call | solution.py:322
  105.7 2.9 %collective-permute-start.28 = (bf16[256,1024]{1,0:T(8,128)(2,1)}, bf16[256,1024]{1,0:T(8,128)(2,1)S(1)}, u32[]{:S(2)}, u32[]{:S(2)}) collective-permute-start(bf16[256,1024]{1,0:T(8,128)(2,1)} %get-tuple-element.139), channel_id=1, source_target_pairs={{0,8},{2,10},{4,12},{6,14},{8,0},{10,2},{12,4},{14,6},{1,9},{3,11}... | collective-permute-start | bytes 1572872 | tf_op jit(solution)/shard_map/ppermute | solution.py:24
  110.5 2.0 collective-permute-start.31
  112.5 8.2 %collective-permute-done.27.refs_1_ = bf16[256,1024]{1,0:T(8,128)(2,1)S(1)} collective-permute-done((bf16[256,1024]{1,0:T(8,128)(2,1)}, bf16[256,1024]{1,0:T(8,128)(2,1)S(1)}, u32[]{:S(2)}, u32[]{:S(2)}) %collective-permute-start.27) | collective-permute-done | bytes 524320 | tf_op jit(solution)/shard_map/ppermute | solution.py:24
  121.7 6.8 %collective-permute-done.28.refs_2_ = bf16[256,1024]{1,0:T(8,128)(2,1)S(1)} collective-permute-done((bf16[256,1024]{1,0:T(8,128)(2,1)}, bf16[256,1024]{1,0:T(8,128)(2,1)S(1)}, u32[]{:S(2)}, u32[]{:S(2)}) %collective-permute-start.28) | collective-permute-done | bytes 524320 | tf_op jit(solution)/shard_map/ppermute | solution.py:24
  128.6 3.1 %collective-permute-done.30.refs_5_ = bf16[256,1024]{1,0:T(8,128)(2,1)S(1)} collective-permute-done((bf16[256,1024]{1,0:T(8,128)(2,1)}, bf16[256,1024]{1,0:T(8,128)(2,1)S(1)}, u32[]{:S(2)}, u32[]{:S(2)}) %collective-permute-start.30) | collective-permute-done | bytes 524320 | tf_op jit(solution)/shard_map/ppermute | solution.py:28
  133.6 2.5 %shard_map.78 = (bf16[128,1024]{1,0:T(8,128)(2,1)}, bf16[128,1024]{1,0:T(8,128)(2,1)}) custom-call(bf16[256,1024]{1,0:T(8,128)(2,1)} %get-tuple-element.137.refs_0_, bf16[256,1024]{1,0:T(8,128)(2,1)} %copy-done.11, bf16[256,1024]{1,0:T(8,128)(2,1)} %copy-done.12, bf16[256,1024]{1,0:T(8,128)(2,1)} %copy-done.13, ...), custom_call_target="tpu_custom_call" | custom-call | tf_op jit(solution)/shard_map/pallas_call | solution.py:352
  138.4 3.1 %shard_map.77 = (f32[128,1024]{1,0:T(8,128)}, f32[128,1024]{1,0:T(8,128)}) custom-call(bf16[256,1024]{1,0:T(8,128)(2,1)} %get-tuple-element.137.refs_0_, bf16[256,1024]{1,0:T(8,128)(2,1)} %copy-done.11, bf16[256,1024]{1,0:T(8,128)(2,1)} %copy-done.12, bf16[256,1024]{1,0:T(8,128)(2,1)} %copy-done.13, bf16[256,1024]{1,0:T(8,128)(2,1)} %get-tuple-element.141.refs_4_, ...), custom_call_target="tpu_custom_call" | custom-call | tf_op jit(solution)/shard_map/pallas_call | solution.py:382
  141.5 1.9 collective-permute-done.33.q_got
  143.3 2.6 %collective-permute-done.34.k_got = bf16[128,1024]{1,0:T(8,128)(2,1)S(1)} collective-permute-done((bf16[128,1024]{1,0:T(8,128)(2,1)}, bf16[128,1024]{1,0:T(8,128)(2,1)S(1)}, u32[]{:S(2)}, u32[]{:S(2)}) %collective-permute-start.34) | collective-permute-done | bytes 262176 | tf_op jit(solution)/shard_map/ppermute | solution.py:28
  146.6 2.7 %shard_map.79.refs_0_ = bf16[256,1024]{1,0:T(8,128)(2,1)} custom-call(f32[128,1024]{1,0:T(8,128)} %get-tuple-element.149.q_keep, bf16[128,1024]{1,0:T(8,128)(2,1)} %copy-done.33, f32[128,1024]{1,0:T(8,128)} %get-tuple-element.151.k_keep, bf16[128,1024]{1,0:T(8,128)(2,1)} %copy-done.34, bf16[128,1024]{1,0:T(8,128)(2,1)} %get-tuple-element.153.q_raw, ...), custom_call_target="tpu_custom_call" | custom-call | tf_op jit(solution)/shard_map/pallas_call | solution.py:401
  150.6 8.1 %collective-permute-done.36.refs_2_ = bf16[256,1024]{1,0:T(8,128)(2,1)S(1)} collective-permute-done((bf16[256,1024]{1,0:T(8,128)(2,1)}, bf16[256,1024]{1,0:T(8,128)(2,1)S(1)}, u32[]{:S(2)}, u32[]{:S(2)}) %collective-permute-start.36) | collective-permute-done | bytes 524320 | tf_op jit(solution)/shard_map/ppermute | solution.py:24
  158.8 1.9 collective-permute-done.37.refs_3_
  161.4 5.4 %shard_map.80 = bf16[1024,1024]{1,0:T(8,128)(2,1)} custom-call(bf16[256,1024]{1,0:T(8,128)(2,1)} %shard_map.79.refs_0_, bf16[256,1024]{1,0:T(8,128)(2,1)} %copy-done.29, bf16[256,1024]{1,0:T(8,128)(2,1)} %copy-done.26, bf16[256,1024]{1,0:T(8,128)(2,1)} %copy-done.30, bf16[4,1024,256]{2,1,0:T(8,128)(2,1)} %bitcast.49, bf16[1024,256]{1,0:T(8,128)(2,1)} %copy-done.27, ...), custom_call_target="tpu_custom_call" | custom-call | tf_op jit(solution)/shard_map/pallas_call | solution.py:434
  166.8 42.5 %all_to_all.9 = bf16[32,32,1024]{2,1,0:T(8,128)(2,1)S(1)} all-to-all(bf16[32,32,1024]{2,1,0:T(8,128)(2,1)} %bitcast.51), channel_id=1, replica_groups={{0,4,8,12,16,20,24,28,32,36,40,44,48,52,56,60,64,68,72,76,80,84,88,92,9..., dimensions={0} | all-to-all | bytes 4194304 | tf_op jit(solution)/shard_map/all_to_all | solution.py:559
  (182 shorter events, 38.3 us)
Async XLA Ops:
  5.8 13.5 %collective-permute-start.1 = (bf16[128,1024]{1,0:T(8,128)(2,1)}, bf16[128,1024]{1,0:T(8,128)(2,1)S(1)}, u32[]{:S(2)}, u32[]{:S(2)}) collective-permute-start(bf16[128,1024]{1,0:T(8,128)(2,1)} %get-tuple-element.83.q_unit.refs_8_), channel_id=1, source_target_pairs={{0,2},{2,0},{4,6},{6,4},{8,10},{10,8},{12,14},{14,12},{1,3},{3,1},... | collective-permute-start | bytes 786440 | tf_op jit(solution)/shard_map/ppermute | solution.py:24
  7.9 15.5 %collective-permute-start = (bf16[128,1024]{1,0:T(8,128)(2,1)}, bf16[128,1024]{1,0:T(8,128)(2,1)}, u32[]{:S(2)}, u32[]{:S(2)}) collective-permute-start(bf16[128,1024]{1,0:T(8,128)(2,1)} %get-tuple-element.82.k_unit), channel_id=1, source_target_pairs={{0,16},{16,0},{32,48},{48,32},{64,80},{80,64},{96,112},{112,96},{1... | collective-permute-start | bytes 786440 | tf_op jit(solution)/shard_map/ppermute | solution.py:28
  24.5 14.1 %collective-permute-start.2 = (bf16[256,1024]{1,0:T(8,128)(2,1)S(1)}, bf16[256,1024]{1,0:T(8,128)(2,1)S(1)}, u32[]{:S(2)}, u32[]{:S(2)}) collective-permute-start(bf16[256,1024]{1,0:T(8,128)(2,1)S(1)} %get-tuple-element.93.refs_5_.refs_0_), channel_id=1, source_target_pairs={{0,32},{16,48},{32,64},{48,80},{64,96},{80,112},{96,0},{112,16},{1... | collective-permute-start | bytes 1572872 | tf_op jit(solution)/shard_map/ppermute | solution.py:28
  26.0 13.8 %collective-permute-start.3 = (bf16[256,1024]{1,0:T(8,128)(2,1)S(1)}, bf16[256,1024]{1,0:T(8,128)(2,1)S(1)}, u32[]{:S(2)}, u32[]{:S(2)}) collective-permute-start(bf16[256,1024]{1,0:T(8,128)(2,1)S(1)} %get-tuple-element.101.refs_0_), channel_id=1, source_target_pairs={{0,4},{2,6},{4,8},{6,10},{8,12},{10,14},{12,0},{14,2},{1,5},{3,7},... | collective-permute-start | bytes 1572872 | tf_op jit(solution)/shard_map/ppermute | solution.py:24
  27.6 12.2 %collective-permute-start.4 = (bf16[256,1024]{1,0:T(8,128)(2,1)S(1)}, bf16[256,1024]{1,0:T(8,128)(2,1)S(1)}, u32[]{:S(2)}, u32[]{:S(2)}) collective-permute-start(bf16[256,1024]{1,0:T(8,128)(2,1)S(1)} %get-tuple-element.93.refs_5_.refs_0_), channel_id=1, source_target_pairs={{0,96},{16,112},{32,0},{48,16},{64,32},{80,48},{96,64},{112,80},{1... | collective-permute-start | bytes 1572872 | tf_op jit(solution)/shard_map/ppermute | solution.py:28
  29.4 11.9 %collective-permute-start.5 = (bf16[256,1024]{1,0:T(8,128)(2,1)S(1)}, bf16[256,1024]{1,0:T(8,128)(2,1)S(1)}, u32[]{:S(2)}, u32[]{:S(2)}) collective-permute-start(bf16[256,1024]{1,0:T(8,128)(2,1)S(1)} %get-tuple-element.101.refs_0_), channel_id=1, source_target_pairs={{0,12},{2,14},{4,0},{6,2},{8,4},{10,6},{12,8},{14,10},{1,13},{3,15... | collective-permute-start | bytes 1572872 | tf_op jit(solution)/shard_map/ppermute | solution.py:24
  31.0 10.3 %collective-permute-start.6 = (bf16[256,1024]{1,0:T(8,128)(2,1)S(1)}, bf16[256,1024]{1,0:T(8,128)(2,1)S(1)}, u32[]{:S(2)}, u32[]{:S(2)}) collective-permute-start(bf16[256,1024]{1,0:T(8,128)(2,1)S(1)} %get-tuple-element.93.refs_5_.refs_0_), channel_id=1, source_target_pairs={{0,1},{1,0},{2,3},{3,2},{4,5},{5,4},{6,7},{7,6},{8,9},{9,8},{10,11... | collective-permute-start | bytes 1572872 | tf_op jit(solution)/shard_map/ppermute | solution.py:42
  41.4 10.0 %collective-permute-start.10 = (bf16[128,1024]{1,0:T(8,128)(2,1)S(1)}, bf16[128,1024]{1,0:T(8,128)(2,1)S(1)}, u32[]{:S(2)}, u32[]{:S(2)}) collective-permute-start(bf16[128,1024]{1,0:T(8,128)(2,1)S(1)} %slice.29), channel_id=1, source_target_pairs={{0,32},{16,48},{32,64},{48,80},{64,96},{80,112},{96,0},{112,16},{1... | collective-permute-start | bytes 786440 | tf_op jit(solution)/shard_map/ppermute | solution.py:28
  41.8 9.6 %collective-permute-start.12 = (bf16[128,1024]{1,0:T(8,128)(2,1)S(1)}, bf16[128,1024]{1,0:T(8,128)(2,1)S(1)}, u32[]{:S(2)}, u32[]{:S(2)}) collective-permute-start(bf16[128,1024]{1,0:T(8,128)(2,1)S(1)} %slice.30), channel_id=1, source_target_pairs={{0,96},{16,112},{32,0},{48,16},{64,32},{80,48},{96,64},{112,80},{1... | collective-permute-start | bytes 786440 | tf_op jit(solution)/shard_map/ppermute | solution.py:28
  44.8 10.2 %collective-permute-start.14 = (bf16[256,1024]{1,0:T(8,128)(2,1)S(1)}, bf16[256,1024]{1,0:T(8,128)(2,1)S(1)}, u32[]{:S(2)}, u32[]{:S(2)}) collective-permute-start(bf16[256,1024]{1,0:T(8,128)(2,1)S(1)} %collective-permute-done.4.refs_9_.refs_4_), channel_id=1, source_target_pairs={{0,1},{1,0},{2,3},{3,2},{4,5},{5,4},{6,7},{7,6},{8,9},{9,8},{10,11... | collective-permute-start | bytes 1572872 | tf_op jit(solution)/shard_map/ppermute | solution.py:42
  44.9 10.0 %collective-permute-start.7 = (bf16[128,1024]{1,0:T(8,128)(2,1)S(1)}, bf16[128,1024]{1,0:T(8,128)(2,1)S(1)}, u32[]{:S(2)}, u32[]{:S(2)}) collective-permute-start(bf16[128,1024]{1,0:T(8,128)(2,1)S(1)} %slice.27), channel_id=1, source_target_pairs={{0,4},{2,6},{4,8},{6,10},{8,12},{10,14},{12,0},{14,2},{1,5},{3,7},... | collective-permute-start | bytes 786440 | tf_op jit(solution)/shard_map/ppermute | solution.py:24
  46.5 8.5 %collective-permute-start.8 = (bf16[128,1024]{1,0:T(8,128)(2,1)S(1)}, bf16[128,1024]{1,0:T(8,128)(2,1)S(1)}, u32[]{:S(2)}, u32[]{:S(2)}) collective-permute-start(bf16[128,1024]{1,0:T(8,128)(2,1)S(1)} %slice.28), channel_id=1, source_target_pairs={{0,12},{2,14},{4,0},{6,2},{8,4},{10,6},{12,8},{14,10},{1,13},{3,15... | collective-permute-start | bytes 786440 | tf_op jit(solution)/shard_map/ppermute | solution.py:24
  55.1 13.9 %collective-permute-start.16 = (bf16[1024,256]{1,0:T(8,128)(2,1)}, bf16[1024,256]{1,0:T(8,128)(2,1)S(1)}, u32[]{:S(2)}, u32[]{:S(2)}) collective-permute-start(bf16[1024,256]{1,0:T(8,128)(2,1)} %get-tuple-element.115), channel_id=1, source_target_pairs={{0,2},{2,0},{4,6},{6,4},{8,10},{10,8},{12,14},{14,12},{1,3},{3,1},... | collective-permute-start | bytes 1572872 | tf_op jit(solution)/shard_map/ppermute | solution.py:24
  68.9 19.5 %collective-permute-start.26 = (bf16[2048,1024]{1,0:T(8,128)(2,1)}, bf16[2048,1024]{1,0:T(8,128)(2,1)}, u32[]{:S(2)}, u32[]{:S(2)}) collective-permute-start(bf16[2048,1024]{1,0:T(8,128)(2,1)} %get-tuple-element.119.refs_11_), channel_id=1, source_target_pairs={{0,1},{1,0},{2,3},{3,2},{4,5},{5,4},{6,7},{7,6},{8,9},{9,8},{10,11... | collective-permute-start | bytes 12582920 | tf_op jit(solution)/shard_map/ppermute | solution.py:42
  70.4 5.2 %collective-permute-start.21 = (f32[8,2,128]{2,1,0:T(2,128)S(1)}, f32[8,2,128]{2,1,0:T(2,128)S(1)}, u32[]{:S(2)}, u32[]{:S(2)}) collective-permute-start(f32[8,2,128]{2,1,0:T(2,128)S(1)} %bitcast.60), channel_id=1, source_target_pairs={{0,16},{16,0},{32,48},{48,32},{64,80},{80,64},{96,112},{112,96},{1... | collective-permute-start | bytes 24584 | tf_op jit(solution)/shard_map/ppermute | solution.py:28
  70.8 8.1 %collective-permute-start.17 = (f32[8,2,128]{2,1,0:T(2,128)S(1)}, f32[8,2,128]{2,1,0:T(2,128)S(1)}, u32[]{:S(2)}, u32[]{:S(2)}) collective-permute-start(f32[8,2,128]{2,1,0:T(2,128)S(1)} %bitcast.62), channel_id=1, source_target_pairs={{0,2},{2,0},{4,6},{6,4},{8,10},{10,8},{12,14},{14,12},{1,3},{3,1},... | collective-permute-start | bytes 24584 | tf_op jit(solution)/shard_map/ppermute | solution.py:24
  75.7 7.7 %collective-permute-start.23 = (f32[16,128]{1,0:T(8,128)S(1)}, f32[16,128]{1,0:T(8,128)S(1)}, u32[]{:S(2)}, u32[]{:S(2)}) collective-permute-start(f32[16,128]{1,0:T(8,128)S(1)} %bitcast.53), channel_id=1, source_target_pairs={{0,64},{16,80},{32,96},{48,112},{64,0},{80,16},{96,32},{112,48},{1... | collective-permute-start | bytes 24584 | tf_op jit(solution)/shard_map/ppermute | solution.py:28
  78.5 6.0 %collective-permute-start.24 = (f32[16,128]{1,0:T(8,128)S(1)}, f32[16,128]{1,0:T(8,128)S(1)}, u32[]{:S(2)}, u32[]{:S(2)}) collective-permute-start(f32[16,128]{1,0:T(8,128)S(1)} %bitcast.54), channel_id=1, source_target_pairs={{0,96},{16,112},{32,0},{48,16},{64,32},{80,48},{96,64},{112,80},{1... | collective-permute-start | bytes 24584 | tf_op jit(solution)/shard_map/ppermute | solution.py:28
  79.0 5.5 %collective-permute-start.18 = (f32[16,128]{1,0:T(8,128)S(1)}, f32[16,128]{1,0:T(8,128)S(1)}, u32[]{:S(2)}, u32[]{:S(2)}) collective-permute-start(f32[16,128]{1,0:T(8,128)S(1)} %bitcast.56), channel_id=1, source_target_pairs={{0,4},{2,6},{4,8},{6,10},{8,12},{10,14},{12,0},{14,2},{1,5},{3,7},... | collective-permute-start | bytes 24584 | tf_op jit(solution)/shard_map/ppermute | solution.py:24
  87.1 16.9 %collective-permute-start.25 = (bf16[1024,256]{1,0:T(8,128)(2,1)S(1)}, bf16[1024,256]{1,0:T(8,128)(2,1)S(1)}, u32[]{:S(2)}, u32[]{:S(2)}) collective-permute-start(bf16[1024,256]{1,0:T(8,128)(2,1)S(1)} %get-tuple-element.117), channel_id=1, source_target_pairs={{0,2},{2,0},{4,6},{6,4},{8,10},{10,8},{12,14},{14,12},{1,3},{3,1},... | collective-permute-start | bytes 1572872 | tf_op jit(solution)/shard_map/ppermute | solution.py:24
  104.8 15.9 %collective-permute-start.27 = (bf16[256,1024]{1,0:T(8,128)(2,1)}, bf16[256,1024]{1,0:T(8,128)(2,1)S(1)}, u32[]{:S(2)}, u32[]{:S(2)}) collective-permute-start(bf16[256,1024]{1,0:T(8,128)(2,1)} %get-tuple-element.138), channel_id=1, source_target_pairs={{0,4},{2,6},{4,8},{6,10},{8,12},{10,14},{12,0},{14,2},{1,5},{3,7},... | collective-permute-start | bytes 1572872 | tf_op jit(solution)/shard_map/ppermute | solution.py:24
  105.7 22.8 %collective-permute-start.28 = (bf16[256,1024]{1,0:T(8,128)(2,1)}, bf16[256,1024]{1,0:T(8,128)(2,1)S(1)}, u32[]{:S(2)}, u32[]{:S(2)}) collective-permute-start(bf16[256,1024]{1,0:T(8,128)(2,1)} %get-tuple-element.139), channel_id=1, source_target_pairs={{0,8},{2,10},{4,12},{6,14},{8,0},{10,2},{12,4},{14,6},{1,9},{3,11}... | collective-permute-start | bytes 1572872 | tf_op jit(solution)/shard_map/ppermute | solution.py:24
  108.6 20.0 %collective-permute-start.29 = (bf16[256,1024]{1,0:T(8,128)(2,1)}, bf16[256,1024]{1,0:T(8,128)(2,1)S(1)}, u32[]{:S(2)}, u32[]{:S(2)}) collective-permute-start(bf16[256,1024]{1,0:T(8,128)(2,1)} %get-tuple-element.140), channel_id=1, source_target_pairs={{0,12},{2,14},{4,0},{6,2},{8,4},{10,6},{12,8},{14,10},{1,13},{3,15... | collective-permute-start | bytes 1572872 | tf_op jit(solution)/shard_map/ppermute | solution.py:24
  109.2 22.5 %collective-permute-start.30 = (bf16[256,1024]{1,0:T(8,128)(2,1)}, bf16[256,1024]{1,0:T(8,128)(2,1)S(1)}, u32[]{:S(2)}, u32[]{:S(2)}) collective-permute-start(bf16[256,1024]{1,0:T(8,128)(2,1)} %get-tuple-element.142), channel_id=1, source_target_pairs={{0,32},{16,48},{32,64},{48,80},{64,96},{80,112},{96,0},{112,16},{1... | collective-permute-start | bytes 1572872 | tf_op jit(solution)/shard_map/ppermute | solution.py:28
  110.5 21.3 %collective-permute-start.31 = (bf16[256,1024]{1,0:T(8,128)(2,1)}, bf16[256,1024]{1,0:T(8,128)(2,1)S(1)}, u32[]{:S(2)}, u32[]{:S(2)}) collective-permute-start(bf16[256,1024]{1,0:T(8,128)(2,1)} %get-tuple-element.143), channel_id=1, source_target_pairs={{0,64},{16,80},{32,96},{48,112},{64,0},{80,16},{96,32},{112,48},{1... | collective-permute-start | bytes 1572872 | tf_op jit(solution)/shard_map/ppermute | solution.py:28
  120.7 11.6 %collective-permute-start.32 = (bf16[256,1024]{1,0:T(8,128)(2,1)}, bf16[256,1024]{1,0:T(8,128)(2,1)S(1)}, u32[]{:S(2)}, u32[]{:S(2)}) collective-permute-start(bf16[256,1024]{1,0:T(8,128)(2,1)} %get-tuple-element.144), channel_id=1, source_target_pairs={{0,96},{16,112},{32,0},{48,16},{64,32},{80,48},{96,64},{112,80},{1... | collective-permute-start | bytes 1572872 | tf_op jit(solution)/shard_map/ppermute | solution.py:28
  136.0 7.3 %collective-permute-start.33 = (bf16[128,1024]{1,0:T(8,128)(2,1)}, bf16[128,1024]{1,0:T(8,128)(2,1)S(1)}, u32[]{:S(2)}, u32[]{:S(2)}) collective-permute-start(bf16[128,1024]{1,0:T(8,128)(2,1)} %get-tuple-element.150), channel_id=1, source_target_pairs={{0,2},{2,0},{4,6},{6,4},{8,10},{10,8},{12,14},{14,12},{1,3},{3,1},... | collective-permute-start | bytes 786440 | tf_op jit(solution)/shard_map/ppermute | solution.py:24
  136.5 9.4 %collective-permute-start.34 = (bf16[128,1024]{1,0:T(8,128)(2,1)}, bf16[128,1024]{1,0:T(8,128)(2,1)S(1)}, u32[]{:S(2)}, u32[]{:S(2)}) collective-permute-start(bf16[128,1024]{1,0:T(8,128)(2,1)} %get-tuple-element.152), channel_id=1, source_target_pairs={{0,16},{16,0},{32,48},{48,32},{64,80},{80,64},{96,112},{112,96},{1... | collective-permute-start | bytes 786440 | tf_op jit(solution)/shard_map/ppermute | solution.py:28
  149.3 9.4 %collective-permute-start.36 = (bf16[256,1024]{1,0:T(8,128)(2,1)}, bf16[256,1024]{1,0:T(8,128)(2,1)S(1)}, u32[]{:S(2)}, u32[]{:S(2)}) collective-permute-start(bf16[256,1024]{1,0:T(8,128)(2,1)} %shard_map.79.refs_0_), channel_id=1, source_target_pairs={{0,2},{2,0},{4,6},{6,4},{8,10},{10,8},{12,14},{14,12},{1,3},{3,1},... | collective-permute-start | bytes 1572872 | tf_op jit(solution)/shard_map/ppermute | solution.py:24
  150.0 8.7 %collective-permute-start.38 = (bf16[1024,256]{1,0:T(8,128)(2,1)S(1)}, bf16[1024,256]{1,0:T(8,128)(2,1)S(1)}, u32[]{:S(2)}, u32[]{:S(2)}) collective-permute-start(bf16[1024,256]{1,0:T(8,128)(2,1)S(1)} %copy-done.24), channel_id=1, source_target_pairs={{0,1},{1,0},{2,3},{3,2},{4,5},{5,4},{6,7},{7,6},{8,9},{9,8},{10,11... | collective-permute-start | bytes 1572872 | tf_op jit(solution)/shard_map/ppermute | solution.py:42
  150.0 8.7 %collective-permute-start.39 = (bf16[1024,256]{1,0:T(8,128)(2,1)S(1)}, bf16[1024,256]{1,0:T(8,128)(2,1)S(1)}, u32[]{:S(2)}, u32[]{:S(2)}) collective-permute-start(bf16[1024,256]{1,0:T(8,128)(2,1)S(1)} %copy-done.46), channel_id=1, source_target_pairs={{0,1},{1,0},{2,3},{3,2},{4,5},{5,4},{6,7},{7,6},{8,9},{9,8},{10,11... | collective-permute-start | bytes 1572872 | tf_op jit(solution)/shard_map/ppermute | solution.py:42
  150.5 8.3 %collective-permute-start.35 = (bf16[256,1024]{1,0:T(8,128)(2,1)}, bf16[256,1024]{1,0:T(8,128)(2,1)S(1)}, u32[]{:S(2)}, u32[]{:S(2)}) collective-permute-start(bf16[256,1024]{1,0:T(8,128)(2,1)} %shard_map.79.refs_0_), channel_id=1, source_target_pairs={{0,1},{1,0},{2,3},{3,2},{4,5},{5,4},{6,7},{7,6},{8,9},{9,8},{10,11... | collective-permute-start | bytes 1572872 | tf_op jit(solution)/shard_map/ppermute | solution.py:42
  (56 other events, 374.4 us)

commit v3 on v2

--- a/solution.py
+++ b/solution.py
@@ -410,19 +410,25 @@
 def contract_body(*refs):
     b_in, h_all, h_in, where, out = refs[0:4], refs[4], refs[5:8], refs[8], refs[9]
     h_s, b_s, o_s, sems, out_sems = refs[10:15]
-    sources = (h_all.at[where[0]],) + tuple(h_in)
-    loads = []
-    for i in range(4):
-        loads.append((b_in[i], b_s.at[pl.ds(i * 256, 256)]))
-        loads.append((sources[i], h_s.at[:, pl.ds(i * 256, 256)]))
-    loads = [pltpu.make_async_copy(s, d, sems.at[i]) for i, (s, d) in enumerate(loads)]
-    for load in loads:
+    b_loads = [
+        pltpu.make_async_copy(b_in[i], b_s.at[pl.ds(i * 256, 256)], sems.at[i]) for i in range(4)
+    ]
+    h_loads = []
+    for m in range(4):
+        rows = pl.ds(m * 256, 256)
+        sources = [h_all.at[where[0], rows]] + [ref.at[rows] for ref in h_in]
+        for i in range(4):
+            target = h_s.at[rows, pl.ds(i * 256, 256)]
+            h_loads.append(pltpu.make_async_copy(sources[i], target, sems.at[4 + m * 4 + i]))
+    for load in h_loads[:4] + b_loads + h_loads[4:]:
         load.start()
-    for load in loads:
+    for load in b_loads:
         load.wait()
     stores = []
     for m in range(4):
         rows = pl.ds(m * 256, 256)
+        for load in h_loads[m * 4 : m * 4 + 4]:
+            load.wait()
         o_s[rows, :] = dot(h_s[rows, :], b_s[...]).astype(BF)
         stores.append(pltpu.make_async_copy(o_s.at[rows], out.at[rows], out_sems.at[m]))
         stores[-1].start()
@@ -440,7 +446,7 @@
             pltpu.VMEM((1024, 1024), BF),
             pltpu.VMEM((1024, EMB), BF),
             pltpu.VMEM((1024, EMB), BF),
-            pltpu.SemaphoreType.DMA((8,)),
+            pltpu.SemaphoreType.DMA((20,)),
             pltpu.SemaphoreType.DMA((4,)),
         ],
         compiler_params=params(),
@@ -540,10 +546,10 @@
     h_both, h_core, *got = lax.optimization_barrier((h_both, h_core, *row_got, *col_got))
     h_both = move_query(h_both, 0, 1)
     parts = grads(k_own, k_oth, e_own, mix, mix_far, got[:4], got[4:])
-    h_both, *parts = lax.optimization_barrier((h_both, *parts))
     inv = parts[8]
     query_in = to_owners(parts[:4], move_query)
     key_in = to_owners(parts[4:8], move_key)
+    h_both, *query_in = lax.optimization_barrier((h_both, *query_in))
     q_send, k_send = pass_on(query_in, key_in)
     q_got = move_query(q_send, 0, 1)
     k_got = move_key(k_send, 0, 1)

time: 211 us -> 208 us (0.986)
    all_to_all x1, blocking collectives: 42.5 us -> 40.4 us  [local(): lax.all_to_all(out, ('row', 'col'), 0, 0, tiled=True, axis_index_groups=P...]
where the time goes in v3:
time: 208 us
  waiting for transfers between devices  61.7 us (30%)
  Pallas kernels  48.5 us (23%)
  starting transfers between devices  42.9 us (21%)
  blocking collectives  40.4 us (19%)
  local copies, waits for them, and re-layouts  9.13 us (4%)
  other arithmetic  3.88 us (2%)
    all_to_all x1, blocking collectives, local(): lax.all_to_all(out, ('row', 'col'), 0, 0, tiled=True, axis_index_groups=P...  40.4 us
    ppermute x16, waiting for transfers between devices, move_query(): return lax.ppermute(value, 'col', ring_pair(step, flip))  32.3 us
    ppermute x13, waiting for transfers between devices, move_key(): return lax.ppermute(value, 'row', ring_pair(step, flip))  26.1 us
    ppermute x16, starting transfers between devices, move_query(): return lax.ppermute(value, 'col', ring_pair(step, flip))  22.4 us
    ppermute x13, starting transfers between devices, move_key(): return lax.ppermute(value, 'row', ring_pair(step, flip))  19.2 us
    pallas_call x1, Pallas kernels, grads(): pl.pallas_call(grads_body, in_specs=[ANY] * 13 + [VMEM] * 8, out_specs=[A...  15.5 us
    pallas_call x1, Pallas kernels, scores(): pl.pallas_call(scores_body, in_specs=[ANY] * 15 + [SMEM, VMEM], out_specs...  11.3 us
    pallas_call x1, Pallas kernels, project(): pl.pallas_call(project_body, in_specs=[ANY] * 3, out_specs=[VMEM] * 4, ou...  5.78 us
  transfers between devices with their start and end apart: 40, of which 22 were waited for; matrix products, arithmetic and copies ran while one was open for 3% of the time, Pallas kernels for 15%

profile of v3, /device:TPU:0, one launch (start us, length us, event | category | flops | bytes accessed | tf_op | source)
XLA Modules:
  0.0 207.8 jit_solution(3863464265699342646)
XLA Ops:
  0.0 5.8 %shard_map.73 = (bf16[128,1024]{1,0:T(8,128)(2,1)}, bf16[128,1024]{1,0:T(8,128)(2,1)}, bf16[128,1024]{1,0:T(8,128)(2,1)}, bf16[128,1024]{1,0:T(8,128)(2,1)}) custom-call(bf16[128,4096]{1,0:T(8,128)(2,1)} %hq.1, bf16[128,4096]{1,0:T(8,128)(2,1)} %hk.1, bf16[4096,1024]{1,0:T(8,128)(2,1)} %proj.1), custom_call_target="tpu_custom_call" | custom-call | tf_op jit(solution)/shard_map/pallas_call | solution.py:104
  5.8 2.1 %collective-permute-start.1 = (bf16[128,1024]{1,0:T(8,128)(2,1)}, bf16[128,1024]{1,0:T(8,128)(2,1)S(1)}, u32[]{:S(2)}, u32[]{:S(2)}) collective-permute-start(bf16[128,1024]{1,0:T(8,128)(2,1)} %get-tuple-element.78.q_unit.refs_8_), channel_id=1, source_target_pairs={{0,2},{2,0},{4,6},{6,4},{8,10},{10,8},{12,14},{14,12},{1,3},{3,1},... | collective-permute-start | bytes 786440 | tf_op jit(solution)/shard_map/ppermute | solution.py:24
  7.9 3.6 %collective-permute-start = (bf16[128,1024]{1,0:T(8,128)(2,1)}, bf16[128,1024]{1,0:T(8,128)(2,1)}, u32[]{:S(2)}, u32[]{:S(2)}) collective-permute-start(bf16[128,1024]{1,0:T(8,128)(2,1)} %get-tuple-element.77.k_unit), channel_id=1, source_target_pairs={{0,16},{16,0},{32,48},{48,32},{64,80},{80,64},{96,112},{112,96},{1... | collective-permute-start | bytes 786440 | tf_op jit(solution)/shard_map/ppermute | solution.py:28
  16.1 2.1 %shard_map.74 = (bf16[128,1024]{1,0:T(8,128)(2,1)}, bf16[128,1024]{1,0:T(8,128)(2,1)}, f32[8,128]{1,0:T(8,128)}) custom-call(bf16[128,1024]{1,0:T(8,128)(2,1)} %get-tuple-element.78.q_unit.refs_8_, bf16[128,1024]{1,0:T(8,128)(2,1)} %get-tuple-element.77.k_unit, s32[128,1]{1,0:T(8,128)} %copy.16.pos), custom_call_target="tpu_custom_call" | custom-call | tf_op jit(solution)/shard_map/pallas_call | solution.py:144
  19.3 4.1 %collective-permute-done = bf16[128,1024]{1,0:T(8,128)(2,1)} collective-permute-done((bf16[128,1024]{1,0:T(8,128)(2,1)}, bf16[128,1024]{1,0:T(8,128)(2,1)}, u32[]{:S(2)}, u32[]{:S(2)}) %collective-permute-start) | collective-permute-done | bytes 262176 | tf_op jit(solution)/shard_map/ppermute | solution.py:28
  26.0 1.6 collective-permute-start.3
  27.6 1.7 collective-permute-start.4
  29.4 1.7 collective-permute-start.5
  31.0 7.5 %collective-permute-done.2.refs_6_.refs_1_ = bf16[256,1024]{1,0:T(8,128)(2,1)S(1)} collective-permute-done((bf16[256,1024]{1,0:T(8,128)(2,1)S(1)}, bf16[256,1024]{1,0:T(8,128)(2,1)S(1)}, u32[]{:S(2)}, u32[]{:S(2)}) %collective-permute-start.2) | collective-permute-done | bytes 524320 | tf_op jit(solution)/shard_map/ppermute | solution.py:28
  41.8 3.0 %collective-permute-start.12 = (bf16[128,1024]{1,0:T(8,128)(2,1)S(1)}, bf16[128,1024]{1,0:T(8,128)(2,1)S(1)}, u32[]{:S(2)}, u32[]{:S(2)}) collective-permute-start(bf16[128,1024]{1,0:T(8,128)(2,1)S(1)} %slice.30), channel_id=1, source_target_pairs={{0,96},{16,112},{32,0},{48,16},{64,32},{80,48},{96,64},{112,80},{1... | collective-permute-start | bytes 786440 | tf_op jit(solution)/shard_map/ppermute | solution.py:28
  44.9 1.7 collective-permute-start.7
  46.5 1.7 collective-permute-start.8
  48.3 3.2 %collective-permute-done.10.refs_7_.refs_2_ = bf16[128,1024]{1,0:T(8,128)(2,1)S(1)} collective-permute-done((bf16[128,1024]{1,0:T(8,128)(2,1)S(1)}, bf16[128,1024]{1,0:T(8,128)(2,1)S(1)}, u32[]{:S(2)}, u32[]{:S(2)}) %collective-permute-start.10) | collective-permute-done | bytes 262176 | tf_op jit(solution)/shard_map/ppermute | solution.py:28
  51.9 2.9 %collective-permute-done.7.refs_2_ = bf16[128,1024]{1,0:T(8,128)(2,1)S(1)} collective-permute-done((bf16[128,1024]{1,0:T(8,128)(2,1)S(1)}, bf16[128,1024]{1,0:T(8,128)(2,1)S(1)}, u32[]{:S(2)}, u32[]{:S(2)}) %collective-permute-start.7) | collective-permute-done | bytes 262176 | tf_op jit(solution)/shard_map/ppermute | solution.py:24
  56.1 11.3 %shard_map.75 = (bf16[1024,1024]{1,0:T(8,128)(2,1)}, bf16[2048,1024]{1,0:T(8,128)(2,1)}, f32[24,128]{1,0:T(8,128)}) custom-call(bf16[256,1024]{1,0:T(8,128)(2,1)} %copy-done.10, bf16[256,1024]{1,0:T(8,128)(2,1)} %copy-done.17, bf16[128,1024]{1,0:T(8,128)(2,1)} %copy-done.31, bf16[128,1024]{1,0:T(8,128)(2,1)} %copy-done.32, bf16[256,1024]{1,0:T(8,128)(2,1)} %copy-done.18, ...), custom_call_target="tpu_custom_call" | custom-call | tf_op jit(solution)/shard_map/pallas_call | solution.py:229
  71.9 3.7 %collective-permute-done.21 = f32[8,2,128]{2,1,0:T(2,128)S(1)} collective-permute-done((f32[8,2,128]{2,1,0:T(2,128)S(1)}, f32[8,2,128]{2,1,0:T(2,128)S(1)}, u32[]{:S(2)}, u32[]{:S(2)}) %collective-permute-start.21) | collective-permute-done | bytes 8224 | tf_op jit(solution)/shard_map/ppermute | solution.py:28
  75.7 2.8 %collective-permute-start.23 = (f32[16,128]{1,0:T(8,128)S(1)}, f32[16,128]{1,0:T(8,128)S(1)}, u32[]{:S(2)}, u32[]{:S(2)}) collective-permute-start(f32[16,128]{1,0:T(8,128)S(1)} %bitcast.53), channel_id=1, source_target_pairs={{0,64},{16,80},{32,96},{48,112},{64,0},{80,16},{96,32},{112,48},{1... | collective-permute-start | bytes 24584 | tf_op jit(solution)/shard_map/ppermute | solution.py:28
  80.6 2.8 %collective-permute-start.19 = (f32[16,128]{1,0:T(8,128)S(1)}, f32[16,128]{1,0:T(8,128)S(1)}, u32[]{:S(2)}, u32[]{:S(2)}) collective-permute-start(f32[16,128]{1,0:T(8,128)S(1)} %bitcast.57), channel_id=1, source_target_pairs={{0,8},{2,10},{4,12},{6,14},{8,0},{10,2},{12,4},{14,6},{1,9},{3,11}... | collective-permute-start | bytes 24584 | tf_op jit(solution)/shard_map/ppermute | solution.py:24
  88.5 15.5 %shard_map.76 = (bf16[256,1024]{1,0:T(8,128)(2,1)}, bf16[256,1024]{1,0:T(8,128)(2,1)}, bf16[256,1024]{1,0:T(8,128)(2,1)}, bf16[256,1024]{1,0:T(8,128)(2,1)}, bf1...) custom-call(bf16[256,1024]{1,0:T(8,128)(2,1)} %copy-done.1, ...), custom_call_target="tpu_custom_call" | custom-call | tf_op jit(solution)/shard_map/pallas_call | solution.py:322
  104.9 2.9 %collective-permute-start.28 = (bf16[256,1024]{1,0:T(8,128)(2,1)}, bf16[256,1024]{1,0:T(8,128)(2,1)S(1)}, u32[]{:S(2)}, u32[]{:S(2)}) collective-permute-start(bf16[256,1024]{1,0:T(8,128)(2,1)} %get-tuple-element.125), channel_id=1, source_target_pairs={{0,8},{2,10},{4,12},{6,14},{8,0},{10,2},{12,4},{14,6},{1,9},{3,11}... | collective-permute-start | bytes 1572872 | tf_op jit(solution)/shard_map/ppermute | solution.py:24
  110.5 2.0 collective-permute-start.31
  112.5 7.4 %collective-permute-done.27.refs_1_ = bf16[256,1024]{1,0:T(8,128)(2,1)S(1)} collective-permute-done((bf16[256,1024]{1,0:T(8,128)(2,1)}, bf16[256,1024]{1,0:T(8,128)(2,1)S(1)}, u32[]{:S(2)}, u32[]{:S(2)}) %collective-permute-start.27) | collective-permute-done | bytes 524320 | tf_op jit(solution)/shard_map/ppermute | solution.py:24
  121.0 6.7 %collective-permute-done.28.refs_2_ = bf16[256,1024]{1,0:T(8,128)(2,1)S(1)} collective-permute-done((bf16[256,1024]{1,0:T(8,128)(2,1)}, bf16[256,1024]{1,0:T(8,128)(2,1)S(1)}, u32[]{:S(2)}, u32[]{:S(2)}) %collective-permute-start.28) | collective-permute-done | bytes 524320 | tf_op jit(solution)/shard_map/ppermute | solution.py:24
  127.9 3.1 %collective-permute-done.30.refs_5_ = bf16[256,1024]{1,0:T(8,128)(2,1)S(1)} collective-permute-done((bf16[256,1024]{1,0:T(8,128)(2,1)}, bf16[256,1024]{1,0:T(8,128)(2,1)S(1)}, u32[]{:S(2)}, u32[]{:S(2)}) %collective-permute-start.30) | collective-permute-done | bytes 524320 | tf_op jit(solution)/shard_map/ppermute | solution.py:28
  133.2 2.5 %shard_map.78 = (bf16[128,1024]{1,0:T(8,128)(2,1)}, bf16[128,1024]{1,0:T(8,128)(2,1)}) custom-call(bf16[256,1024]{1,0:T(8,128)(2,1)} %get-tuple-element.127.refs_0_, bf16[256,1024]{1,0:T(8,128)(2,1)} %copy-done.11, bf16[256,1024]{1,0:T(8,128)(2,1)} %copy-done.12, bf16[256,1024]{1,0:T(8,128)(2,1)} %copy-done.13, ...), custom_call_target="tpu_custom_call" | custom-call | tf_op jit(solution)/shard_map/pallas_call | solution.py:352
  138.0 3.1 %shard_map.77 = (f32[128,1024]{1,0:T(8,128)}, f32[128,1024]{1,0:T(8,128)}) custom-call(bf16[256,1024]{1,0:T(8,128)(2,1)} %get-tuple-element.127.refs_0_, bf16[256,1024]{1,0:T(8,128)(2,1)} %copy-done.11, bf16[256,1024]{1,0:T(8,128)(2,1)} %copy-done.12, bf16[256,1024]{1,0:T(8,128)(2,1)} %copy-done.13, bf16[256,1024]{1,0:T(8,128)(2,1)} %get-tuple-element.131.refs_4_, ...), custom_call_target="tpu_custom_call" | custom-call | tf_op jit(solution)/shard_map/pallas_call | solution.py:382
  142.3 2.9 %collective-permute-done.34.k_got = bf16[128,1024]{1,0:T(8,128)(2,1)S(1)} collective-permute-done((bf16[128,1024]{1,0:T(8,128)(2,1)}, bf16[128,1024]{1,0:T(8,128)(2,1)S(1)}, u32[]{:S(2)}, u32[]{:S(2)}) %collective-permute-start.34) | collective-permute-done | bytes 262176 | tf_op jit(solution)/shard_map/ppermute | solution.py:28
  145.9 2.7 %shard_map.79.refs_0_ = bf16[256,1024]{1,0:T(8,128)(2,1)} custom-call(f32[128,1024]{1,0:T(8,128)} %get-tuple-element.139.q_keep, bf16[128,1024]{1,0:T(8,128)(2,1)} %copy-done.33, f32[128,1024]{1,0:T(8,128)} %get-tuple-element.141.k_keep, bf16[128,1024]{1,0:T(8,128)(2,1)} %copy-done.34, bf16[128,1024]{1,0:T(8,128)(2,1)} %get-tuple-element.143.q_raw, ...), custom_call_target="tpu_custom_call" | custom-call | tf_op jit(solution)/shard_map/pallas_call | solution.py:401
  149.8 8.3 %collective-permute-done.36.refs_2_ = bf16[256,1024]{1,0:T(8,128)(2,1)S(1)} collective-permute-done((bf16[256,1024]{1,0:T(8,128)(2,1)}, bf16[256,1024]{1,0:T(8,128)(2,1)S(1)}, u32[]{:S(2)}, u32[]{:S(2)}) %collective-permute-start.36) | collective-permute-done | bytes 524320 | tf_op jit(solution)/shard_map/ppermute | solution.py:24
  158.1 1.9 collective-permute-done.37.refs_3_
  160.7 5.6 %shard_map.80 = bf16[1024,1024]{1,0:T(8,128)(2,1)} custom-call(bf16[256,1024]{1,0:T(8,128)(2,1)} %shard_map.79.refs_0_, bf16[256,1024]{1,0:T(8,128)(2,1)} %copy-done.29, bf16[256,1024]{1,0:T(8,128)(2,1)} %copy-done.26, bf16[256,1024]{1,0:T(8,128)(2,1)} %copy-done.30, bf16[4,1024,256]{2,1,0:T(8,128)(2,1)} %bitcast.49, bf16[1024,256]{1,0:T(8,128)(2,1)} %copy-done.27, ...), custom_call_target="tpu_custom_call" | custom-call | tf_op jit(solution)/shard_map/pallas_call | solution.py:440
  166.4 40.4 %all_to_all.9 = bf16[32,32,1024]{2,1,0:T(8,128)(2,1)S(1)} all-to-all(bf16[32,32,1024]{2,1,0:T(8,128)(2,1)} %bitcast.51), channel_id=1, replica_groups={{0,4,8,12,16,20,24,28,32,36,40,44,48,52,56,60,64,68,72,76,80,84,88,92,9..., dimensions={0} | all-to-all | bytes 4194304 | tf_op jit(solution)/shard_map/all_to_all | solution.py:565
  (182 shorter events, 38.3 us)
Async XLA Ops:
  5.8 13.5 %collective-permute-start.1 = (bf16[128,1024]{1,0:T(8,128)(2,1)}, bf16[128,1024]{1,0:T(8,128)(2,1)S(1)}, u32[]{:S(2)}, u32[]{:S(2)}) collective-permute-start(bf16[128,1024]{1,0:T(8,128)(2,1)} %get-tuple-element.78.q_unit.refs_8_), channel_id=1, source_target_pairs={{0,2},{2,0},{4,6},{6,4},{8,10},{10,8},{12,14},{14,12},{1,3},{3,1},... | collective-permute-start | bytes 786440 | tf_op jit(solution)/shard_map/ppermute | solution.py:24
  7.9 15.5 %collective-permute-start = (bf16[128,1024]{1,0:T(8,128)(2,1)}, bf16[128,1024]{1,0:T(8,128)(2,1)}, u32[]{:S(2)}, u32[]{:S(2)}) collective-permute-start(bf16[128,1024]{1,0:T(8,128)(2,1)} %get-tuple-element.77.k_unit), channel_id=1, source_target_pairs={{0,16},{16,0},{32,48},{48,32},{64,80},{80,64},{96,112},{112,96},{1... | collective-permute-start | bytes 786440 | tf_op jit(solution)/shard_map/ppermute | solution.py:28
  24.5 14.1 %collective-permute-start.2 = (bf16[256,1024]{1,0:T(8,128)(2,1)S(1)}, bf16[256,1024]{1,0:T(8,128)(2,1)S(1)}, u32[]{:S(2)}, u32[]{:S(2)}) collective-permute-start(bf16[256,1024]{1,0:T(8,128)(2,1)S(1)} %get-tuple-element.88.refs_5_.refs_0_), channel_id=1, source_target_pairs={{0,32},{16,48},{32,64},{48,80},{64,96},{80,112},{96,0},{112,16},{1... | collective-permute-start | bytes 1572872 | tf_op jit(solution)/shard_map/ppermute | solution.py:28
  26.0 13.8 %collective-permute-start.3 = (bf16[256,1024]{1,0:T(8,128)(2,1)S(1)}, bf16[256,1024]{1,0:T(8,128)(2,1)S(1)}, u32[]{:S(2)}, u32[]{:S(2)}) collective-permute-start(bf16[256,1024]{1,0:T(8,128)(2,1)S(1)} %get-tuple-element.96.refs_0_), channel_id=1, source_target_pairs={{0,4},{2,6},{4,8},{6,10},{8,12},{10,14},{12,0},{14,2},{1,5},{3,7},... | collective-permute-start | bytes 1572872 | tf_op jit(solution)/shard_map/ppermute | solution.py:24
  27.6 12.2 %collective-permute-start.4 = (bf16[256,1024]{1,0:T(8,128)(2,1)S(1)}, bf16[256,1024]{1,0:T(8,128)(2,1)S(1)}, u32[]{:S(2)}, u32[]{:S(2)}) collective-permute-start(bf16[256,1024]{1,0:T(8,128)(2,1)S(1)} %get-tuple-element.88.refs_5_.refs_0_), channel_id=1, source_target_pairs={{0,96},{16,112},{32,0},{48,16},{64,32},{80,48},{96,64},{112,80},{1... | collective-permute-start | bytes 1572872 | tf_op jit(solution)/shard_map/ppermute | solution.py:28
  29.4 11.9 %collective-permute-start.5 = (bf16[256,1024]{1,0:T(8,128)(2,1)S(1)}, bf16[256,1024]{1,0:T(8,128)(2,1)S(1)}, u32[]{:S(2)}, u32[]{:S(2)}) collective-permute-start(bf16[256,1024]{1,0:T(8,128)(2,1)S(1)} %get-tuple-element.96.refs_0_), channel_id=1, source_target_pairs={{0,12},{2,14},{4,0},{6,2},{8,4},{10,6},{12,8},{14,10},{1,13},{3,15... | collective-permute-start | bytes 1572872 | tf_op jit(solution)/shard_map/ppermute | solution.py:24
  31.0 10.3 %collective-permute-start.6 = (bf16[256,1024]{1,0:T(8,128)(2,1)S(1)}, bf16[256,1024]{1,0:T(8,128)(2,1)S(1)}, u32[]{:S(2)}, u32[]{:S(2)}) collective-permute-start(bf16[256,1024]{1,0:T(8,128)(2,1)S(1)} %get-tuple-element.88.refs_5_.refs_0_), channel_id=1, source_target_pairs={{0,1},{1,0},{2,3},{3,2},{4,5},{5,4},{6,7},{7,6},{8,9},{9,8},{10,11... | collective-permute-start | bytes 1572872 | tf_op jit(solution)/shard_map/ppermute | solution.py:42
  41.4 10.0 %collective-permute-start.10 = (bf16[128,1024]{1,0:T(8,128)(2,1)S(1)}, bf16[128,1024]{1,0:T(8,128)(2,1)S(1)}, u32[]{:S(2)}, u32[]{:S(2)}) collective-permute-start(bf16[128,1024]{1,0:T(8,128)(2,1)S(1)} %slice.29), channel_id=1, source_target_pairs={{0,32},{16,48},{32,64},{48,80},{64,96},{80,112},{96,0},{112,16},{1... | collective-permute-start | bytes 786440 | tf_op jit(solution)/shard_map/ppermute | solution.py:28
  41.8 9.6 %collective-permute-start.12 = (bf16[128,1024]{1,0:T(8,128)(2,1)S(1)}, bf16[128,1024]{1,0:T(8,128)(2,1)S(1)}, u32[]{:S(2)}, u32[]{:S(2)}) collective-permute-start(bf16[128,1024]{1,0:T(8,128)(2,1)S(1)} %slice.30), channel_id=1, source_target_pairs={{0,96},{16,112},{32,0},{48,16},{64,32},{80,48},{96,64},{112,80},{1... | collective-permute-start | bytes 786440 | tf_op jit(solution)/shard_map/ppermute | solution.py:28
  44.8 10.2 %collective-permute-start.14 = (bf16[256,1024]{1,0:T(8,128)(2,1)S(1)}, bf16[256,1024]{1,0:T(8,128)(2,1)S(1)}, u32[]{:S(2)}, u32[]{:S(2)}) collective-permute-start(bf16[256,1024]{1,0:T(8,128)(2,1)S(1)} %collective-permute-done.4.refs_9_.refs_4_), channel_id=1, source_target_pairs={{0,1},{1,0},{2,3},{3,2},{4,5},{5,4},{6,7},{7,6},{8,9},{9,8},{10,11... | collective-permute-start | bytes 1572872 | tf_op jit(solution)/shard_map/ppermute | solution.py:42
  44.9 10.0 %collective-permute-start.7 = (bf16[128,1024]{1,0:T(8,128)(2,1)S(1)}, bf16[128,1024]{1,0:T(8,128)(2,1)S(1)}, u32[]{:S(2)}, u32[]{:S(2)}) collective-permute-start(bf16[128,1024]{1,0:T(8,128)(2,1)S(1)} %slice.27), channel_id=1, source_target_pairs={{0,4},{2,6},{4,8},{6,10},{8,12},{10,14},{12,0},{14,2},{1,5},{3,7},... | collective-permute-start | bytes 786440 | tf_op jit(solution)/shard_map/ppermute | solution.py:24
  46.5 8.5 %collective-permute-start.8 = (bf16[128,1024]{1,0:T(8,128)(2,1)S(1)}, bf16[128,1024]{1,0:T(8,128)(2,1)S(1)}, u32[]{:S(2)}, u32[]{:S(2)}) collective-permute-start(bf16[128,1024]{1,0:T(8,128)(2,1)S(1)} %slice.28), channel_id=1, source_target_pairs={{0,12},{2,14},{4,0},{6,2},{8,4},{10,6},{12,8},{14,10},{1,13},{3,15... | collective-permute-start | bytes 786440 | tf_op jit(solution)/shard_map/ppermute | solution.py:24
  55.1 13.9 %collective-permute-start.16 = (bf16[1024,256]{1,0:T(8,128)(2,1)}, bf16[1024,256]{1,0:T(8,128)(2,1)S(1)}, u32[]{:S(2)}, u32[]{:S(2)}) collective-permute-start(bf16[1024,256]{1,0:T(8,128)(2,1)} %get-tuple-element.110), channel_id=1, source_target_pairs={{0,2},{2,0},{4,6},{6,4},{8,10},{10,8},{12,14},{14,12},{1,3},{3,1},... | collective-permute-start | bytes 1572872 | tf_op jit(solution)/shard_map/ppermute | solution.py:24
  68.9 19.5 %collective-permute-start.26 = (bf16[2048,1024]{1,0:T(8,128)(2,1)}, bf16[2048,1024]{1,0:T(8,128)(2,1)}, u32[]{:S(2)}, u32[]{:S(2)}) collective-permute-start(bf16[2048,1024]{1,0:T(8,128)(2,1)} %get-tuple-element.114.refs_11_), channel_id=1, source_target_pairs={{0,1},{1,0},{2,3},{3,2},{4,5},{5,4},{6,7},{7,6},{8,9},{9,8},{10,11... | collective-permute-start | bytes 12582920 | tf_op jit(solution)/shard_map/ppermute | solution.py:42
  70.4 5.2 %collective-permute-start.21 = (f32[8,2,128]{2,1,0:T(2,128)S(1)}, f32[8,2,128]{2,1,0:T(2,128)S(1)}, u32[]{:S(2)}, u32[]{:S(2)}) collective-permute-start(f32[8,2,128]{2,1,0:T(2,128)S(1)} %bitcast.60), channel_id=1, source_target_pairs={{0,16},{16,0},{32,48},{48,32},{64,80},{80,64},{96,112},{112,96},{1... | collective-permute-start | bytes 24584 | tf_op jit(solution)/shard_map/ppermute | solution.py:28
  70.8 8.1 %collective-permute-start.17 = (f32[8,2,128]{2,1,0:T(2,128)S(1)}, f32[8,2,128]{2,1,0:T(2,128)S(1)}, u32[]{:S(2)}, u32[]{:S(2)}) collective-permute-start(f32[8,2,128]{2,1,0:T(2,128)S(1)} %bitcast.62), channel_id=1, source_target_pairs={{0,2},{2,0},{4,6},{6,4},{8,10},{10,8},{12,14},{14,12},{1,3},{3,1},... | collective-permute-start | bytes 24584 | tf_op jit(solution)/shard_map/ppermute | solution.py:24
  75.7 7.7 %collective-permute-start.23 = (f32[16,128]{1,0:T(8,128)S(1)}, f32[16,128]{1,0:T(8,128)S(1)}, u32[]{:S(2)}, u32[]{:S(2)}) collective-permute-start(f32[16,128]{1,0:T(8,128)S(1)} %bitcast.53), channel_id=1, source_target_pairs={{0,64},{16,80},{32,96},{48,112},{64,0},{80,16},{96,32},{112,48},{1... | collective-permute-start | bytes 24584 | tf_op jit(solution)/shard_map/ppermute | solution.py:28
  78.5 6.0 %collective-permute-start.24 = (f32[16,128]{1,0:T(8,128)S(1)}, f32[16,128]{1,0:T(8,128)S(1)}, u32[]{:S(2)}, u32[]{:S(2)}) collective-permute-start(f32[16,128]{1,0:T(8,128)S(1)} %bitcast.54), channel_id=1, source_target_pairs={{0,96},{16,112},{32,0},{48,16},{64,32},{80,48},{96,64},{112,80},{1... | collective-permute-start | bytes 24584 | tf_op jit(solution)/shard_map/ppermute | solution.py:28
  79.0 5.5 %collective-permute-start.18 = (f32[16,128]{1,0:T(8,128)S(1)}, f32[16,128]{1,0:T(8,128)S(1)}, u32[]{:S(2)}, u32[]{:S(2)}) collective-permute-start(f32[16,128]{1,0:T(8,128)S(1)} %bitcast.56), channel_id=1, source_target_pairs={{0,4},{2,6},{4,8},{6,10},{8,12},{10,14},{12,0},{14,2},{1,5},{3,7},... | collective-permute-start | bytes 24584 | tf_op jit(solution)/shard_map/ppermute | solution.py:24
  87.1 22.7 %collective-permute-start.25 = (bf16[1024,256]{1,0:T(8,128)(2,1)S(1)}, bf16[1024,256]{1,0:T(8,128)(2,1)S(1)}, u32[]{:S(2)}, u32[]{:S(2)}) collective-permute-start(bf16[1024,256]{1,0:T(8,128)(2,1)S(1)} %get-tuple-element.112), channel_id=1, source_target_pairs={{0,2},{2,0},{4,6},{6,4},{8,10},{10,8},{12,14},{14,12},{1,3},{3,1},... | collective-permute-start | bytes 1572872 | tf_op jit(solution)/shard_map/ppermute | solution.py:24
  104.0 16.0 %collective-permute-start.27 = (bf16[256,1024]{1,0:T(8,128)(2,1)}, bf16[256,1024]{1,0:T(8,128)(2,1)S(1)}, u32[]{:S(2)}, u32[]{:S(2)}) collective-permute-start(bf16[256,1024]{1,0:T(8,128)(2,1)} %get-tuple-element.124), channel_id=1, source_target_pairs={{0,4},{2,6},{4,8},{6,10},{8,12},{10,14},{12,0},{14,2},{1,5},{3,7},... | collective-permute-start | bytes 1572872 | tf_op jit(solution)/shard_map/ppermute | solution.py:24
  104.9 22.8 %collective-permute-start.28 = (bf16[256,1024]{1,0:T(8,128)(2,1)}, bf16[256,1024]{1,0:T(8,128)(2,1)S(1)}, u32[]{:S(2)}, u32[]{:S(2)}) collective-permute-start(bf16[256,1024]{1,0:T(8,128)(2,1)} %get-tuple-element.125), channel_id=1, source_target_pairs={{0,8},{2,10},{4,12},{6,14},{8,0},{10,2},{12,4},{14,6},{1,9},{3,11}... | collective-permute-start | bytes 1572872 | tf_op jit(solution)/shard_map/ppermute | solution.py:24
  107.8 20.0 %collective-permute-start.29 = (bf16[256,1024]{1,0:T(8,128)(2,1)}, bf16[256,1024]{1,0:T(8,128)(2,1)S(1)}, u32[]{:S(2)}, u32[]{:S(2)}) collective-permute-start(bf16[256,1024]{1,0:T(8,128)(2,1)} %get-tuple-element.126), channel_id=1, source_target_pairs={{0,12},{2,14},{4,0},{6,2},{8,4},{10,6},{12,8},{14,10},{1,13},{3,15... | collective-permute-start | bytes 1572872 | tf_op jit(solution)/shard_map/ppermute | solution.py:24
  108.5 22.5 %collective-permute-start.30 = (bf16[256,1024]{1,0:T(8,128)(2,1)}, bf16[256,1024]{1,0:T(8,128)(2,1)S(1)}, u32[]{:S(2)}, u32[]{:S(2)}) collective-permute-start(bf16[256,1024]{1,0:T(8,128)(2,1)} %get-tuple-element.132), channel_id=1, source_target_pairs={{0,32},{16,48},{32,64},{48,80},{64,96},{80,112},{96,0},{112,16},{1... | collective-permute-start | bytes 1572872 | tf_op jit(solution)/shard_map/ppermute | solution.py:28
  110.5 20.5 %collective-permute-start.31 = (bf16[256,1024]{1,0:T(8,128)(2,1)}, bf16[256,1024]{1,0:T(8,128)(2,1)S(1)}, u32[]{:S(2)}, u32[]{:S(2)}) collective-permute-start(bf16[256,1024]{1,0:T(8,128)(2,1)} %get-tuple-element.133), channel_id=1, source_target_pairs={{0,64},{16,80},{32,96},{48,112},{64,0},{80,16},{96,32},{112,48},{1... | collective-permute-start | bytes 1572872 | tf_op jit(solution)/shard_map/ppermute | solution.py:28
  120.0 12.4 %collective-permute-start.32 = (bf16[256,1024]{1,0:T(8,128)(2,1)}, bf16[256,1024]{1,0:T(8,128)(2,1)S(1)}, u32[]{:S(2)}, u32[]{:S(2)}) collective-permute-start(bf16[256,1024]{1,0:T(8,128)(2,1)} %get-tuple-element.134), channel_id=1, source_target_pairs={{0,96},{16,112},{32,0},{48,16},{64,32},{80,48},{96,64},{112,80},{1... | collective-permute-start | bytes 1572872 | tf_op jit(solution)/shard_map/ppermute | solution.py:28
  135.7 6.7 %collective-permute-start.33 = (bf16[128,1024]{1,0:T(8,128)(2,1)}, bf16[128,1024]{1,0:T(8,128)(2,1)S(1)}, u32[]{:S(2)}, u32[]{:S(2)}) collective-permute-start(bf16[128,1024]{1,0:T(8,128)(2,1)} %get-tuple-element.140), channel_id=1, source_target_pairs={{0,2},{2,0},{4,6},{6,4},{8,10},{10,8},{12,14},{14,12},{1,3},{3,1},... | collective-permute-start | bytes 786440 | tf_op jit(solution)/shard_map/ppermute | solution.py:24
  136.3 8.9 %collective-permute-start.34 = (bf16[128,1024]{1,0:T(8,128)(2,1)}, bf16[128,1024]{1,0:T(8,128)(2,1)S(1)}, u32[]{:S(2)}, u32[]{:S(2)}) collective-permute-start(bf16[128,1024]{1,0:T(8,128)(2,1)} %get-tuple-element.142), channel_id=1, source_target_pairs={{0,16},{16,0},{32,48},{48,32},{64,80},{80,64},{96,112},{112,96},{1... | collective-permute-start | bytes 786440 | tf_op jit(solution)/shard_map/ppermute | solution.py:28
  148.6 9.4 %collective-permute-start.36 = (bf16[256,1024]{1,0:T(8,128)(2,1)}, bf16[256,1024]{1,0:T(8,128)(2,1)S(1)}, u32[]{:S(2)}, u32[]{:S(2)}) collective-permute-start(bf16[256,1024]{1,0:T(8,128)(2,1)} %shard_map.79.refs_0_), channel_id=1, source_target_pairs={{0,2},{2,0},{4,6},{6,4},{8,10},{10,8},{12,14},{14,12},{1,3},{3,1},... | collective-permute-start | bytes 1572872 | tf_op jit(solution)/shard_map/ppermute | solution.py:24
  149.2 8.9 %collective-permute-start.38 = (bf16[1024,256]{1,0:T(8,128)(2,1)S(1)}, bf16[1024,256]{1,0:T(8,128)(2,1)S(1)}, u32[]{:S(2)}, u32[]{:S(2)}) collective-permute-start(bf16[1024,256]{1,0:T(8,128)(2,1)S(1)} %copy-done.24), channel_id=1, source_target_pairs={{0,1},{1,0},{2,3},{3,2},{4,5},{5,4},{6,7},{7,6},{8,9},{9,8},{10,11... | collective-permute-start | bytes 1572872 | tf_op jit(solution)/shard_map/ppermute | solution.py:42
  149.2 8.9 %collective-permute-start.39 = (bf16[1024,256]{1,0:T(8,128)(2,1)S(1)}, bf16[1024,256]{1,0:T(8,128)(2,1)S(1)}, u32[]{:S(2)}, u32[]{:S(2)}) collective-permute-start(bf16[1024,256]{1,0:T(8,128)(2,1)S(1)} %copy-done.46), channel_id=1, source_target_pairs={{0,1},{1,0},{2,3},{3,2},{4,5},{5,4},{6,7},{7,6},{8,9},{9,8},{10,11... | collective-permute-start | bytes 1572872 | tf_op jit(solution)/shard_map/ppermute | solution.py:42
  149.7 8.4 %collective-permute-start.35 = (bf16[256,1024]{1,0:T(8,128)(2,1)}, bf16[256,1024]{1,0:T(8,128)(2,1)S(1)}, u32[]{:S(2)}, u32[]{:S(2)}) collective-permute-start(bf16[256,1024]{1,0:T(8,128)(2,1)} %shard_map.79.refs_0_), channel_id=1, source_target_pairs={{0,1},{1,0},{2,3},{3,2},{4,5},{5,4},{6,7},{7,6},{8,9},{9,8},{10,11... | collective-permute-start | bytes 1572872 | tf_op jit(solution)/shard_map/ppermute | solution.py:42
  (56 other events, 377.2 us)

commit v4 on v2

--- a/solution.py
+++ b/solution.py
@@ -540,10 +540,10 @@
     h_both, h_core, *got = lax.optimization_barrier((h_both, h_core, *row_got, *col_got))
     h_both = move_query(h_both, 0, 1)
     parts = grads(k_own, k_oth, e_own, mix, mix_far, got[:4], got[4:])
-    h_both, *parts = lax.optimization_barrier((h_both, *parts))
     inv = parts[8]
     query_in = to_owners(parts[:4], move_query)
     key_in = to_owners(parts[4:8], move_key)
+    h_both, *query_in = lax.optimization_barrier((h_both, *query_in))
     q_send, k_send = pass_on(query_in, key_in)
     q_got = move_query(q_send, 0, 1)
     k_got = move_key(k_send, 0, 1)

time: 211 us -> 208 us (0.986)
    all_to_all x1, blocking collectives: 42.5 us -> 40.4 us  [local(): lax.all_to_all(out, ('row', 'col'), 0, 0, tiled=True, axis_index_groups=P...]
where the time goes in v4:
time: 208 us
  waiting for transfers between devices  61.7 us (30%)
  Pallas kernels  48.2 us (23%)
  starting transfers between devices  42.9 us (21%)
  blocking collectives  40.4 us (19%)
  local copies, waits for them, and re-layouts  9.13 us (4%)
  other arithmetic  3.88 us (2%)
    all_to_all x1, blocking collectives, local(): lax.all_to_all(out, ('row', 'col'), 0, 0, tiled=True, axis_index_groups=P...  40.4 us
    ppermute x16, waiting for transfers between devices, move_query(): return lax.ppermute(value, 'col', ring_pair(step, flip))  32.3 us
    ppermute x13, waiting for transfers between devices, move_key(): return lax.ppermute(value, 'row', ring_pair(step, flip))  26.1 us
    ppermute x16, starting transfers between devices, move_query(): return lax.ppermute(value, 'col', ring_pair(step, flip))  22.4 us
    ppermute x13, starting transfers between devices, move_key(): return lax.ppermute(value, 'row', ring_pair(step, flip))  19.2 us
    pallas_call x1, Pallas kernels, grads(): pl.pallas_call(grads_body, in_specs=[ANY] * 13 + [VMEM] * 8, out_specs=[A...  15.5 us
    pallas_call x1, Pallas kernels, scores(): pl.pallas_call(scores_body, in_specs=[ANY] * 15 + [SMEM, VMEM], out_specs...  11.3 us
    pallas_call x1, Pallas kernels, project(): pl.pallas_call(project_body, in_specs=[ANY] * 3, out_specs=[VMEM] * 4, ou...  5.78 us
  transfers between devices with their start and end apart: 40, of which 22 were waited for; matrix products, arithmetic and copies ran while one was open for 3% of the time, Pallas kernels for 15%

profile of v4, /device:TPU:0, one launch (start us, length us, event | category | flops | bytes accessed | tf_op | source)
XLA Modules:
  0.0 207.5 jit_solution(14226755205157772111)
XLA Ops:
  0.0 5.8 %shard_map.73 = (bf16[128,1024]{1,0:T(8,128)(2,1)}, bf16[128,1024]{1,0:T(8,128)(2,1)}, bf16[128,1024]{1,0:T(8,128)(2,1)}, bf16[128,1024]{1,0:T(8,128)(2,1)}) custom-call(bf16[128,4096]{1,0:T(8,128)(2,1)} %hq.1, bf16[128,4096]{1,0:T(8,128)(2,1)} %hk.1, bf16[4096,1024]{1,0:T(8,128)(2,1)} %proj.1), custom_call_target="tpu_custom_call" | custom-call | tf_op jit(solution)/shard_map/pallas_call | solution.py:104
  5.8 2.1 %collective-permute-start.1 = (bf16[128,1024]{1,0:T(8,128)(2,1)}, bf16[128,1024]{1,0:T(8,128)(2,1)S(1)}, u32[]{:S(2)}, u32[]{:S(2)}) collective-permute-start(bf16[128,1024]{1,0:T(8,128)(2,1)} %get-tuple-element.78.q_unit.refs_8_), channel_id=1, source_target_pairs={{0,2},{2,0},{4,6},{6,4},{8,10},{10,8},{12,14},{14,12},{1,3},{3,1},... | collective-permute-start | bytes 786440 | tf_op jit(solution)/shard_map/ppermute | solution.py:24
  7.9 3.6 %collective-permute-start = (bf16[128,1024]{1,0:T(8,128)(2,1)}, bf16[128,1024]{1,0:T(8,128)(2,1)}, u32[]{:S(2)}, u32[]{:S(2)}) collective-permute-start(bf16[128,1024]{1,0:T(8,128)(2,1)} %get-tuple-element.77.k_unit), channel_id=1, source_target_pairs={{0,16},{16,0},{32,48},{48,32},{64,80},{80,64},{96,112},{112,96},{1... | collective-permute-start | bytes 786440 | tf_op jit(solution)/shard_map/ppermute | solution.py:28
  16.1 2.1 %shard_map.74 = (bf16[128,1024]{1,0:T(8,128)(2,1)}, bf16[128,1024]{1,0:T(8,128)(2,1)}, f32[8,128]{1,0:T(8,128)}) custom-call(bf16[128,1024]{1,0:T(8,128)(2,1)} %get-tuple-element.78.q_unit.refs_8_, bf16[128,1024]{1,0:T(8,128)(2,1)} %get-tuple-element.77.k_unit, s32[128,1]{1,0:T(8,128)} %copy.16.pos), custom_call_target="tpu_custom_call" | custom-call | tf_op jit(solution)/shard_map/pallas_call | solution.py:144
  19.3 4.1 %collective-permute-done = bf16[128,1024]{1,0:T(8,128)(2,1)} collective-permute-done((bf16[128,1024]{1,0:T(8,128)(2,1)}, bf16[128,1024]{1,0:T(8,128)(2,1)}, u32[]{:S(2)}, u32[]{:S(2)}) %collective-permute-start) | collective-permute-done | bytes 262176 | tf_op jit(solution)/shard_map/ppermute | solution.py:28
  26.0 1.6 collective-permute-start.3
  27.6 1.7 collective-permute-start.4
  29.4 1.7 collective-permute-start.5
  31.0 7.5 %collective-permute-done.2.refs_6_.refs_1_ = bf16[256,1024]{1,0:T(8,128)(2,1)S(1)} collective-permute-done((bf16[256,1024]{1,0:T(8,128)(2,1)S(1)}, bf16[256,1024]{1,0:T(8,128)(2,1)S(1)}, u32[]{:S(2)}, u32[]{:S(2)}) %collective-permute-start.2) | collective-permute-done | bytes 524320 | tf_op jit(solution)/shard_map/ppermute | solution.py:28
  41.8 3.0 %collective-permute-start.12 = (bf16[128,1024]{1,0:T(8,128)(2,1)S(1)}, bf16[128,1024]{1,0:T(8,128)(2,1)S(1)}, u32[]{:S(2)}, u32[]{:S(2)}) collective-permute-start(bf16[128,1024]{1,0:T(8,128)(2,1)S(1)} %slice.30), channel_id=1, source_target_pairs={{0,96},{16,112},{32,0},{48,16},{64,32},{80,48},{96,64},{112,80},{1... | collective-permute-start | bytes 786440 | tf_op jit(solution)/shard_map/ppermute | solution.py:28
  44.9 1.7 collective-permute-start.7
  46.5 1.7 collective-permute-start.8
  48.3 3.2 %collective-permute-done.10.refs_7_.refs_2_ = bf16[128,1024]{1,0:T(8,128)(2,1)S(1)} collective-permute-done((bf16[128,1024]{1,0:T(8,128)(2,1)S(1)}, bf16[128,1024]{1,0:T(8,128)(2,1)S(1)}, u32[]{:S(2)}, u32[]{:S(2)}) %collective-permute-start.10) | collective-permute-done | bytes 262176 | tf_op jit(solution)/shard_map/ppermute | solution.py:28
  51.9 2.9 %collective-permute-done.7.refs_2_ = bf16[128,1024]{1,0:T(8,128)(2,1)S(1)} collective-permute-done((bf16[128,1024]{1,0:T(8,128)(2,1)S(1)}, bf16[128,1024]{1,0:T(8,128)(2,1)S(1)}, u32[]{:S(2)}, u32[]{:S(2)}) %collective-permute-start.7) | collective-permute-done | bytes 262176 | tf_op jit(solution)/shard_map/ppermute | solution.py:24
  56.1 11.3 %shard_map.75 = (bf16[1024,1024]{1,0:T(8,128)(2,1)}, bf16[2048,1024]{1,0:T(8,128)(2,1)}, f32[24,128]{1,0:T(8,128)}) custom-call(bf16[256,1024]{1,0:T(8,128)(2,1)} %copy-done.10, bf16[256,1024]{1,0:T(8,128)(2,1)} %copy-done.17, bf16[128,1024]{1,0:T(8,128)(2,1)} %copy-done.31, bf16[128,1024]{1,0:T(8,128)(2,1)} %copy-done.32, bf16[256,1024]{1,0:T(8,128)(2,1)} %copy-done.18, ...), custom_call_target="tpu_custom_call" | custom-call | tf_op jit(solution)/shard_map/pallas_call | solution.py:229
  71.9 3.7 %collective-permute-done.21 = f32[8,2,128]{2,1,0:T(2,128)S(1)} collective-permute-done((f32[8,2,128]{2,1,0:T(2,128)S(1)}, f32[8,2,128]{2,1,0:T(2,128)S(1)}, u32[]{:S(2)}, u32[]{:S(2)}) %collective-permute-start.21) | collective-permute-done | bytes 8224 | tf_op jit(solution)/shard_map/ppermute | solution.py:28
  75.7 2.8 %collective-permute-start.23 = (f32[16,128]{1,0:T(8,128)S(1)}, f32[16,128]{1,0:T(8,128)S(1)}, u32[]{:S(2)}, u32[]{:S(2)}) collective-permute-start(f32[16,128]{1,0:T(8,128)S(1)} %bitcast.53), channel_id=1, source_target_pairs={{0,64},{16,80},{32,96},{48,112},{64,0},{80,16},{96,32},{112,48},{1... | collective-permute-start | bytes 24584 | tf_op jit(solution)/shard_map/ppermute | solution.py:28
  80.6 2.8 %collective-permute-start.19 = (f32[16,128]{1,0:T(8,128)S(1)}, f32[16,128]{1,0:T(8,128)S(1)}, u32[]{:S(2)}, u32[]{:S(2)}) collective-permute-start(f32[16,128]{1,0:T(8,128)S(1)} %bitcast.57), channel_id=1, source_target_pairs={{0,8},{2,10},{4,12},{6,14},{8,0},{10,2},{12,4},{14,6},{1,9},{3,11}... | collective-permute-start | bytes 24584 | tf_op jit(solution)/shard_map/ppermute | solution.py:24
  88.5 15.5 %shard_map.76 = (bf16[256,1024]{1,0:T(8,128)(2,1)}, bf16[256,1024]{1,0:T(8,128)(2,1)}, bf16[256,1024]{1,0:T(8,128)(2,1)}, bf16[256,1024]{1,0:T(8,128)(2,1)}, bf1...) custom-call(bf16[256,1024]{1,0:T(8,128)(2,1)} %copy-done.1, ...), custom_call_target="tpu_custom_call" | custom-call | tf_op jit(solution)/shard_map/pallas_call | solution.py:322
  104.9 2.9 %collective-permute-start.28 = (bf16[256,1024]{1,0:T(8,128)(2,1)}, bf16[256,1024]{1,0:T(8,128)(2,1)S(1)}, u32[]{:S(2)}, u32[]{:S(2)}) collective-permute-start(bf16[256,1024]{1,0:T(8,128)(2,1)} %get-tuple-element.125), channel_id=1, source_target_pairs={{0,8},{2,10},{4,12},{6,14},{8,0},{10,2},{12,4},{14,6},{1,9},{3,11}... | collective-permute-start | bytes 1572872 | tf_op jit(solution)/shard_map/ppermute | solution.py:24
  110.5 2.0 collective-permute-start.31
  112.5 7.4 %collective-permute-done.27.refs_1_ = bf16[256,1024]{1,0:T(8,128)(2,1)S(1)} collective-permute-done((bf16[256,1024]{1,0:T(8,128)(2,1)}, bf16[256,1024]{1,0:T(8,128)(2,1)S(1)}, u32[]{:S(2)}, u32[]{:S(2)}) %collective-permute-start.27) | collective-permute-done | bytes 524320 | tf_op jit(solution)/shard_map/ppermute | solution.py:24
  121.0 6.7 %collective-permute-done.28.refs_2_ = bf16[256,1024]{1,0:T(8,128)(2,1)S(1)} collective-permute-done((bf16[256,1024]{1,0:T(8,128)(2,1)}, bf16[256,1024]{1,0:T(8,128)(2,1)S(1)}, u32[]{:S(2)}, u32[]{:S(2)}) %collective-permute-start.28) | collective-permute-done | bytes 524320 | tf_op jit(solution)/shard_map/ppermute | solution.py:24
  127.9 3.1 %collective-permute-done.30.refs_5_ = bf16[256,1024]{1,0:T(8,128)(2,1)S(1)} collective-permute-done((bf16[256,1024]{1,0:T(8,128)(2,1)}, bf16[256,1024]{1,0:T(8,128)(2,1)S(1)}, u32[]{:S(2)}, u32[]{:S(2)}) %collective-permute-start.30) | collective-permute-done | bytes 524320 | tf_op jit(solution)/shard_map/ppermute | solution.py:28
  133.2 2.5 %shard_map.78 = (bf16[128,1024]{1,0:T(8,128)(2,1)}, bf16[128,1024]{1,0:T(8,128)(2,1)}) custom-call(bf16[256,1024]{1,0:T(8,128)(2,1)} %get-tuple-element.127.refs_0_, bf16[256,1024]{1,0:T(8,128)(2,1)} %copy-done.11, bf16[256,1024]{1,0:T(8,128)(2,1)} %copy-done.12, bf16[256,1024]{1,0:T(8,128)(2,1)} %copy-done.13, ...), custom_call_target="tpu_custom_call" | custom-call | tf_op jit(solution)/shard_map/pallas_call | solution.py:352
  138.0 3.1 %shard_map.77 = (f32[128,1024]{1,0:T(8,128)}, f32[128,1024]{1,0:T(8,128)}) custom-call(bf16[256,1024]{1,0:T(8,128)(2,1)} %get-tuple-element.127.refs_0_, bf16[256,1024]{1,0:T(8,128)(2,1)} %copy-done.11, bf16[256,1024]{1,0:T(8,128)(2,1)} %copy-done.12, bf16[256,1024]{1,0:T(8,128)(2,1)} %copy-done.13, bf16[256,1024]{1,0:T(8,128)(2,1)} %get-tuple-element.131.refs_4_, ...), custom_call_target="tpu_custom_call" | custom-call | tf_op jit(solution)/shard_map/pallas_call | solution.py:382
  142.3 2.9 %collective-permute-done.34.k_got = bf16[128,1024]{1,0:T(8,128)(2,1)S(1)} collective-permute-done((bf16[128,1024]{1,0:T(8,128)(2,1)}, bf16[128,1024]{1,0:T(8,128)(2,1)S(1)}, u32[]{:S(2)}, u32[]{:S(2)}) %collective-permute-start.34) | collective-permute-done | bytes 262176 | tf_op jit(solution)/shard_map/ppermute | solution.py:28
  145.9 2.7 %shard_map.79.refs_0_ = bf16[256,1024]{1,0:T(8,128)(2,1)} custom-call(f32[128,1024]{1,0:T(8,128)} %get-tuple-element.139.q_keep, bf16[128,1024]{1,0:T(8,128)(2,1)} %copy-done.33, f32[128,1024]{1,0:T(8,128)} %get-tuple-element.141.k_keep, bf16[128,1024]{1,0:T(8,128)(2,1)} %copy-done.34, bf16[128,1024]{1,0:T(8,128)(2,1)} %get-tuple-element.143.q_raw, ...), custom_call_target="tpu_custom_call" | custom-call | tf_op jit(solution)/shard_map/pallas_call | solution.py:401
  149.8 8.3 %collective-permute-done.36.refs_2_ = bf16[256,1024]{1,0:T(8,128)(2,1)S(1)} collective-permute-done((bf16[256,1024]{1,0:T(8,128)(2,1)}, bf16[256,1024]{1,0:T(8,128)(2,1)S(1)}, u32[]{:S(2)}, u32[]{:S(2)}) %collective-permute-start.36) | collective-permute-done | bytes 524320 | tf_op jit(solution)/shard_map/ppermute | solution.py:24
  158.1 1.9 collective-permute-done.37.refs_3_
  160.7 5.4 %shard_map.80 = bf16[1024,1024]{1,0:T(8,128)(2,1)} custom-call(bf16[256,1024]{1,0:T(8,128)(2,1)} %shard_map.79.refs_0_, bf16[256,1024]{1,0:T(8,128)(2,1)} %copy-done.29, bf16[256,1024]{1,0:T(8,128)(2,1)} %copy-done.26, bf16[256,1024]{1,0:T(8,128)(2,1)} %copy-done.30, bf16[4,1024,256]{2,1,0:T(8,128)(2,1)} %bitcast.49, bf16[1024,256]{1,0:T(8,128)(2,1)} %copy-done.27, ...), custom_call_target="tpu_custom_call" | custom-call | tf_op jit(solution)/shard_map/pallas_call | solution.py:434
  166.1 40.4 %all_to_all.9 = bf16[32,32,1024]{2,1,0:T(8,128)(2,1)S(1)} all-to-all(bf16[32,32,1024]{2,1,0:T(8,128)(2,1)} %bitcast.51), channel_id=1, replica_groups={{0,4,8,12,16,20,24,28,32,36,40,44,48,52,56,60,64,68,72,76,80,84,88,92,9..., dimensions={0} | all-to-all | bytes 4194304 | tf_op jit(solution)/shard_map/all_to_all | solution.py:559
  (182 shorter events, 38.3 us)
Async XLA Ops:
  5.8 13.5 %collective-permute-start.1 = (bf16[128,1024]{1,0:T(8,128)(2,1)}, bf16[128,1024]{1,0:T(8,128)(2,1)S(1)}, u32[]{:S(2)}, u32[]{:S(2)}) collective-permute-start(bf16[128,1024]{1,0:T(8,128)(2,1)} %get-tuple-element.78.q_unit.refs_8_), channel_id=1, source_target_pairs={{0,2},{2,0},{4,6},{6,4},{8,10},{10,8},{12,14},{14,12},{1,3},{3,1},... | collective-permute-start | bytes 786440 | tf_op jit(solution)/shard_map/ppermute | solution.py:24
  7.9 15.5 %collective-permute-start = (bf16[128,1024]{1,0:T(8,128)(2,1)}, bf16[128,1024]{1,0:T(8,128)(2,1)}, u32[]{:S(2)}, u32[]{:S(2)}) collective-permute-start(bf16[128,1024]{1,0:T(8,128)(2,1)} %get-tuple-element.77.k_unit), channel_id=1, source_target_pairs={{0,16},{16,0},{32,48},{48,32},{64,80},{80,64},{96,112},{112,96},{1... | collective-permute-start | bytes 786440 | tf_op jit(solution)/shard_map/ppermute | solution.py:28
  24.5 14.1 %collective-permute-start.2 = (bf16[256,1024]{1,0:T(8,128)(2,1)S(1)}, bf16[256,1024]{1,0:T(8,128)(2,1)S(1)}, u32[]{:S(2)}, u32[]{:S(2)}) collective-permute-start(bf16[256,1024]{1,0:T(8,128)(2,1)S(1)} %get-tuple-element.88.refs_5_.refs_0_), channel_id=1, source_target_pairs={{0,32},{16,48},{32,64},{48,80},{64,96},{80,112},{96,0},{112,16},{1... | collective-permute-start | bytes 1572872 | tf_op jit(solution)/shard_map/ppermute | solution.py:28
  26.0 13.8 %collective-permute-start.3 = (bf16[256,1024]{1,0:T(8,128)(2,1)S(1)}, bf16[256,1024]{1,0:T(8,128)(2,1)S(1)}, u32[]{:S(2)}, u32[]{:S(2)}) collective-permute-start(bf16[256,1024]{1,0:T(8,128)(2,1)S(1)} %get-tuple-element.96.refs_0_), channel_id=1, source_target_pairs={{0,4},{2,6},{4,8},{6,10},{8,12},{10,14},{12,0},{14,2},{1,5},{3,7},... | collective-permute-start | bytes 1572872 | tf_op jit(solution)/shard_map/ppermute | solution.py:24
  27.6 12.2 %collective-permute-start.4 = (bf16[256,1024]{1,0:T(8,128)(2,1)S(1)}, bf16[256,1024]{1,0:T(8,128)(2,1)S(1)}, u32[]{:S(2)}, u32[]{:S(2)}) collective-permute-start(bf16[256,1024]{1,0:T(8,128)(2,1)S(1)} %get-tuple-element.88.refs_5_.refs_0_), channel_id=1, source_target_pairs={{0,96},{16,112},{32,0},{48,16},{64,32},{80,48},{96,64},{112,80},{1... | collective-permute-start | bytes 1572872 | tf_op jit(solution)/shard_map/ppermute | solution.py:28
  29.4 11.9 %collective-permute-start.5 = (bf16[256,1024]{1,0:T(8,128)(2,1)S(1)}, bf16[256,1024]{1,0:T(8,128)(2,1)S(1)}, u32[]{:S(2)}, u32[]{:S(2)}) collective-permute-start(bf16[256,1024]{1,0:T(8,128)(2,1)S(1)} %get-tuple-element.96.refs_0_), channel_id=1, source_target_pairs={{0,12},{2,14},{4,0},{6,2},{8,4},{10,6},{12,8},{14,10},{1,13},{3,15... | collective-permute-start | bytes 1572872 | tf_op jit(solution)/shard_map/ppermute | solution.py:24
  31.0 10.3 %collective-permute-start.6 = (bf16[256,1024]{1,0:T(8,128)(2,1)S(1)}, bf16[256,1024]{1,0:T(8,128)(2,1)S(1)}, u32[]{:S(2)}, u32[]{:S(2)}) collective-permute-start(bf16[256,1024]{1,0:T(8,128)(2,1)S(1)} %get-tuple-element.88.refs_5_.refs_0_), channel_id=1, source_target_pairs={{0,1},{1,0},{2,3},{3,2},{4,5},{5,4},{6,7},{7,6},{8,9},{9,8},{10,11... | collective-permute-start | bytes 1572872 | tf_op jit(solution)/shard_map/ppermute | solution.py:42
  41.4 10.0 %collective-permute-start.10 = (bf16[128,1024]{1,0:T(8,128)(2,1)S(1)}, bf16[128,1024]{1,0:T(8,128)(2,1)S(1)}, u32[]{:S(2)}, u32[]{:S(2)}) collective-permute-start(bf16[128,1024]{1,0:T(8,128)(2,1)S(1)} %slice.29), channel_id=1, source_target_pairs={{0,32},{16,48},{32,64},{48,80},{64,96},{80,112},{96,0},{112,16},{1... | collective-permute-start | bytes 786440 | tf_op jit(solution)/shard_map/ppermute | solution.py:28
  41.8 9.6 %collective-permute-start.12 = (bf16[128,1024]{1,0:T(8,128)(2,1)S(1)}, bf16[128,1024]{1,0:T(8,128)(2,1)S(1)}, u32[]{:S(2)}, u32[]{:S(2)}) collective-permute-start(bf16[128,1024]{1,0:T(8,128)(2,1)S(1)} %slice.30), channel_id=1, source_target_pairs={{0,96},{16,112},{32,0},{48,16},{64,32},{80,48},{96,64},{112,80},{1... | collective-permute-start | bytes 786440 | tf_op jit(solution)/shard_map/ppermute | solution.py:28
  44.8 10.2 %collective-permute-start.14 = (bf16[256,1024]{1,0:T(8,128)(2,1)S(1)}, bf16[256,1024]{1,0:T(8,128)(2,1)S(1)}, u32[]{:S(2)}, u32[]{:S(2)}) collective-permute-start(bf16[256,1024]{1,0:T(8,128)(2,1)S(1)} %collective-permute-done.4.refs_9_.refs_4_), channel_id=1, source_target_pairs={{0,1},{1,0},{2,3},{3,2},{4,5},{5,4},{6,7},{7,6},{8,9},{9,8},{10,11... | collective-permute-start | bytes 1572872 | tf_op jit(solution)/shard_map/ppermute | solution.py:42
  44.9 10.0 %collective-permute-start.7 = (bf16[128,1024]{1,0:T(8,128)(2,1)S(1)}, bf16[128,1024]{1,0:T(8,128)(2,1)S(1)}, u32[]{:S(2)}, u32[]{:S(2)}) collective-permute-start(bf16[128,1024]{1,0:T(8,128)(2,1)S(1)} %slice.27), channel_id=1, source_target_pairs={{0,4},{2,6},{4,8},{6,10},{8,12},{10,14},{12,0},{14,2},{1,5},{3,7},... | collective-permute-start | bytes 786440 | tf_op jit(solution)/shard_map/ppermute | solution.py:24
  46.5 8.5 %collective-permute-start.8 = (bf16[128,1024]{1,0:T(8,128)(2,1)S(1)}, bf16[128,1024]{1,0:T(8,128)(2,1)S(1)}, u32[]{:S(2)}, u32[]{:S(2)}) collective-permute-start(bf16[128,1024]{1,0:T(8,128)(2,1)S(1)} %slice.28), channel_id=1, source_target_pairs={{0,12},{2,14},{4,0},{6,2},{8,4},{10,6},{12,8},{14,10},{1,13},{3,15... | collective-permute-start | bytes 786440 | tf_op jit(solution)/shard_map/ppermute | solution.py:24
  55.1 13.9 %collective-permute-start.16 = (bf16[1024,256]{1,0:T(8,128)(2,1)}, bf16[1024,256]{1,0:T(8,128)(2,1)S(1)}, u32[]{:S(2)}, u32[]{:S(2)}) collective-permute-start(bf16[1024,256]{1,0:T(8,128)(2,1)} %get-tuple-element.110), channel_id=1, source_target_pairs={{0,2},{2,0},{4,6},{6,4},{8,10},{10,8},{12,14},{14,12},{1,3},{3,1},... | collective-permute-start | bytes 1572872 | tf_op jit(solution)/shard_map/ppermute | solution.py:24
  68.9 19.5 %collective-permute-start.26 = (bf16[2048,1024]{1,0:T(8,128)(2,1)}, bf16[2048,1024]{1,0:T(8,128)(2,1)}, u32[]{:S(2)}, u32[]{:S(2)}) collective-permute-start(bf16[2048,1024]{1,0:T(8,128)(2,1)} %get-tuple-element.114.refs_11_), channel_id=1, source_target_pairs={{0,1},{1,0},{2,3},{3,2},{4,5},{5,4},{6,7},{7,6},{8,9},{9,8},{10,11... | collective-permute-start | bytes 12582920 | tf_op jit(solution)/shard_map/ppermute | solution.py:42
  70.4 5.2 %collective-permute-start.21 = (f32[8,2,128]{2,1,0:T(2,128)S(1)}, f32[8,2,128]{2,1,0:T(2,128)S(1)}, u32[]{:S(2)}, u32[]{:S(2)}) collective-permute-start(f32[8,2,128]{2,1,0:T(2,128)S(1)} %bitcast.60), channel_id=1, source_target_pairs={{0,16},{16,0},{32,48},{48,32},{64,80},{80,64},{96,112},{112,96},{1... | collective-permute-start | bytes 24584 | tf_op jit(solution)/shard_map/ppermute | solution.py:28
  70.8 8.1 %collective-permute-start.17 = (f32[8,2,128]{2,1,0:T(2,128)S(1)}, f32[8,2,128]{2,1,0:T(2,128)S(1)}, u32[]{:S(2)}, u32[]{:S(2)}) collective-permute-start(f32[8,2,128]{2,1,0:T(2,128)S(1)} %bitcast.62), channel_id=1, source_target_pairs={{0,2},{2,0},{4,6},{6,4},{8,10},{10,8},{12,14},{14,12},{1,3},{3,1},... | collective-permute-start | bytes 24584 | tf_op jit(solution)/shard_map/ppermute | solution.py:24
  75.7 7.7 %collective-permute-start.23 = (f32[16,128]{1,0:T(8,128)S(1)}, f32[16,128]{1,0:T(8,128)S(1)}, u32[]{:S(2)}, u32[]{:S(2)}) collective-permute-start(f32[16,128]{1,0:T(8,128)S(1)} %bitcast.53), channel_id=1, source_target_pairs={{0,64},{16,80},{32,96},{48,112},{64,0},{80,16},{96,32},{112,48},{1... | collective-permute-start | bytes 24584 | tf_op jit(solution)/shard_map/ppermute | solution.py:28
  78.5 6.0 %collective-permute-start.24 = (f32[16,128]{1,0:T(8,128)S(1)}, f32[16,128]{1,0:T(8,128)S(1)}, u32[]{:S(2)}, u32[]{:S(2)}) collective-permute-start(f32[16,128]{1,0:T(8,128)S(1)} %bitcast.54), channel_id=1, source_target_pairs={{0,96},{16,112},{32,0},{48,16},{64,32},{80,48},{96,64},{112,80},{1... | collective-permute-start | bytes 24584 | tf_op jit(solution)/shard_map/ppermute | solution.py:28
  79.0 5.5 %collective-permute-start.18 = (f32[16,128]{1,0:T(8,128)S(1)}, f32[16,128]{1,0:T(8,128)S(1)}, u32[]{:S(2)}, u32[]{:S(2)}) collective-permute-start(f32[16,128]{1,0:T(8,128)S(1)} %bitcast.56), channel_id=1, source_target_pairs={{0,4},{2,6},{4,8},{6,10},{8,12},{10,14},{12,0},{14,2},{1,5},{3,7},... | collective-permute-start | bytes 24584 | tf_op jit(solution)/shard_map/ppermute | solution.py:24
  87.1 22.7 %collective-permute-start.25 = (bf16[1024,256]{1,0:T(8,128)(2,1)S(1)}, bf16[1024,256]{1,0:T(8,128)(2,1)S(1)}, u32[]{:S(2)}, u32[]{:S(2)}) collective-permute-start(bf16[1024,256]{1,0:T(8,128)(2,1)S(1)} %get-tuple-element.112), channel_id=1, source_target_pairs={{0,2},{2,0},{4,6},{6,4},{8,10},{10,8},{12,14},{14,12},{1,3},{3,1},... | collective-permute-start | bytes 1572872 | tf_op jit(solution)/shard_map/ppermute | solution.py:24
  104.0 16.0 %collective-permute-start.27 = (bf16[256,1024]{1,0:T(8,128)(2,1)}, bf16[256,1024]{1,0:T(8,128)(2,1)S(1)}, u32[]{:S(2)}, u32[]{:S(2)}) collective-permute-start(bf16[256,1024]{1,0:T(8,128)(2,1)} %get-tuple-element.124), channel_id=1, source_target_pairs={{0,4},{2,6},{4,8},{6,10},{8,12},{10,14},{12,0},{14,2},{1,5},{3,7},... | collective-permute-start | bytes 1572872 | tf_op jit(solution)/shard_map/ppermute | solution.py:24
  104.9 22.8 %collective-permute-start.28 = (bf16[256,1024]{1,0:T(8,128)(2,1)}, bf16[256,1024]{1,0:T(8,128)(2,1)S(1)}, u32[]{:S(2)}, u32[]{:S(2)}) collective-permute-start(bf16[256,1024]{1,0:T(8,128)(2,1)} %get-tuple-element.125), channel_id=1, source_target_pairs={{0,8},{2,10},{4,12},{6,14},{8,0},{10,2},{12,4},{14,6},{1,9},{3,11}... | collective-permute-start | bytes 1572872 | tf_op jit(solution)/shard_map/ppermute | solution.py:24
  107.8 20.0 %collective-permute-start.29 = (bf16[256,1024]{1,0:T(8,128)(2,1)}, bf16[256,1024]{1,0:T(8,128)(2,1)S(1)}, u32[]{:S(2)}, u32[]{:S(2)}) collective-permute-start(bf16[256,1024]{1,0:T(8,128)(2,1)} %get-tuple-element.126), channel_id=1, source_target_pairs={{0,12},{2,14},{4,0},{6,2},{8,4},{10,6},{12,8},{14,10},{1,13},{3,15... | collective-permute-start | bytes 1572872 | tf_op jit(solution)/shard_map/ppermute | solution.py:24
  108.5 22.5 %collective-permute-start.30 = (bf16[256,1024]{1,0:T(8,128)(2,1)}, bf16[256,1024]{1,0:T(8,128)(2,1)S(1)}, u32[]{:S(2)}, u32[]{:S(2)}) collective-permute-start(bf16[256,1024]{1,0:T(8,128)(2,1)} %get-tuple-element.132), channel_id=1, source_target_pairs={{0,32},{16,48},{32,64},{48,80},{64,96},{80,112},{96,0},{112,16},{1... | collective-permute-start | bytes 1572872 | tf_op jit(solution)/shard_map/ppermute | solution.py:28
  110.5 20.5 %collective-permute-start.31 = (bf16[256,1024]{1,0:T(8,128)(2,1)}, bf16[256,1024]{1,0:T(8,128)(2,1)S(1)}, u32[]{:S(2)}, u32[]{:S(2)}) collective-permute-start(bf16[256,1024]{1,0:T(8,128)(2,1)} %get-tuple-element.133), channel_id=1, source_target_pairs={{0,64},{16,80},{32,96},{48,112},{64,0},{80,16},{96,32},{112,48},{1... | collective-permute-start | bytes 1572872 | tf_op jit(solution)/shard_map/ppermute | solution.py:28
  120.0 12.4 %collective-permute-start.32 = (bf16[256,1024]{1,0:T(8,128)(2,1)}, bf16[256,1024]{1,0:T(8,128)(2,1)S(1)}, u32[]{:S(2)}, u32[]{:S(2)}) collective-permute-start(bf16[256,1024]{1,0:T(8,128)(2,1)} %get-tuple-element.134), channel_id=1, source_target_pairs={{0,96},{16,112},{32,0},{48,16},{64,32},{80,48},{96,64},{112,80},{1... | collective-permute-start | bytes 1572872 | tf_op jit(solution)/shard_map/ppermute | solution.py:28
  135.7 6.7 %collective-permute-start.33 = (bf16[128,1024]{1,0:T(8,128)(2,1)}, bf16[128,1024]{1,0:T(8,128)(2,1)S(1)}, u32[]{:S(2)}, u32[]{:S(2)}) collective-permute-start(bf16[128,1024]{1,0:T(8,128)(2,1)} %get-tuple-element.140), channel_id=1, source_target_pairs={{0,2},{2,0},{4,6},{6,4},{8,10},{10,8},{12,14},{14,12},{1,3},{3,1},... | collective-permute-start | bytes 786440 | tf_op jit(solution)/shard_map/ppermute | solution.py:24
  136.3 8.9 %collective-permute-start.34 = (bf16[128,1024]{1,0:T(8,128)(2,1)}, bf16[128,1024]{1,0:T(8,128)(2,1)S(1)}, u32[]{:S(2)}, u32[]{:S(2)}) collective-permute-start(bf16[128,1024]{1,0:T(8,128)(2,1)} %get-tuple-element.142), channel_id=1, source_target_pairs={{0,16},{16,0},{32,48},{48,32},{64,80},{80,64},{96,112},{112,96},{1... | collective-permute-start | bytes 786440 | tf_op jit(solution)/shard_map/ppermute | solution.py:28
  148.6 9.4 %collective-permute-start.36 = (bf16[256,1024]{1,0:T(8,128)(2,1)}, bf16[256,1024]{1,0:T(8,128)(2,1)S(1)}, u32[]{:S(2)}, u32[]{:S(2)}) collective-permute-start(bf16[256,1024]{1,0:T(8,128)(2,1)} %shard_map.79.refs_0_), channel_id=1, source_target_pairs={{0,2},{2,0},{4,6},{6,4},{8,10},{10,8},{12,14},{14,12},{1,3},{3,1},... | collective-permute-start | bytes 1572872 | tf_op jit(solution)/shard_map/ppermute | solution.py:24
  149.2 8.9 %collective-permute-start.38 = (bf16[1024,256]{1,0:T(8,128)(2,1)S(1)}, bf16[1024,256]{1,0:T(8,128)(2,1)S(1)}, u32[]{:S(2)}, u32[]{:S(2)}) collective-permute-start(bf16[1024,256]{1,0:T(8,128)(2,1)S(1)} %copy-done.24), channel_id=1, source_target_pairs={{0,1},{1,0},{2,3},{3,2},{4,5},{5,4},{6,7},{7,6},{8,9},{9,8},{10,11... | collective-permute-start | bytes 1572872 | tf_op jit(solution)/shard_map/ppermute | solution.py:42
  149.2 8.9 %collective-permute-start.39 = (bf16[1024,256]{1,0:T(8,128)(2,1)S(1)}, bf16[1024,256]{1,0:T(8,128)(2,1)S(1)}, u32[]{:S(2)}, u32[]{:S(2)}) collective-permute-start(bf16[1024,256]{1,0:T(8,128)(2,1)S(1)} %copy-done.46), channel_id=1, source_target_pairs={{0,1},{1,0},{2,3},{3,2},{4,5},{5,4},{6,7},{7,6},{8,9},{9,8},{10,11... | collective-permute-start | bytes 1572872 | tf_op jit(solution)/shard_map/ppermute | solution.py:42
  149.7 8.4 %collective-permute-start.35 = (bf16[256,1024]{1,0:T(8,128)(2,1)}, bf16[256,1024]{1,0:T(8,128)(2,1)S(1)}, u32[]{:S(2)}, u32[]{:S(2)}) collective-permute-start(bf16[256,1024]{1,0:T(8,128)(2,1)} %shard_map.79.refs_0_), channel_id=1, source_target_pairs={{0,1},{1,0},{2,3},{3,2},{4,5},{5,4},{6,7},{7,6},{8,9},{9,8},{10,11... | collective-permute-start | bytes 1572872 | tf_op jit(solution)/shard_map/ppermute | solution.py:42
  (56 other events, 377.2 us)
